TPU v7x, 32 devices: a whole 2x2x4 slice. The times are simulated.
32 devices in a mesh: section: 2 (over core), row: 4 (over y, x), seq: 4 (over z).
Axes of the slice: x: 2, y: 2, z: 4, core: 2. Of those that a mesh axis runs over, the one named last changes fastest.
Arguments:
- inputs: bfloat16 [16, 1024, 576], P('row', 'seq'), may hold values from -6 to 6
- cotangent: bfloat16 [16, 1024, 576], P('row', 'seq'), may hold values from -6 to 6
- group_ids: int32 [16, 1024], P('row', 'seq'), may hold values from 0 to 2, as said below
- w_query: bfloat16 [2, 576, 576], P('section'), may hold values from -0.25 to 0.25
- w_key: bfloat16 [2, 576, 192], P('section'), may hold values from -0.25 to 0.25
- w_value: bfloat16 [2, 576, 192], P('section'), may hold values from -0.25 to 0.25
- w_out: bfloat16 [2, 576, 576], P('section'), may hold values from -1 to 1
- w_gate: bfloat16 [2, 576, 1536], P('section'), may hold values from -0.25 to 0.25
- w_up: bfloat16 [2, 576, 1536], P('section'), may hold values from -0.25 to 0.25
- w_down: bfloat16 [2, 1536, 576], P('section'), may hold values from -0.15625 to 0.15625
- gain_attn: float32 [2, 576], P('section'), may hold values from 0.5 to 1.5
- gain_mlp: float32 [2, 576], P('section'), may hold values from 0.5 to 1.5
Outputs:
- activations: bfloat16 [2, 16, 1024, 576], P('section', 'row', 'seq')
- input_grads: bfloat16 [2, 16, 1024, 576], P('section', 'row', 'seq')
- grad_query: float32 [2, 576, 576], P('section', 'seq')
- grad_key: float32 [2, 576, 192], P('section', 'seq')
- grad_value: float32 [2, 576, 192], P('section', 'seq')
- grad_out: float32 [2, 576, 576], P('section', 'seq')
- grad_gate: float32 [2, 576, 1536], P('section', 'seq')
- grad_up: float32 [2, 576, 1536], P('section', 'seq')
- grad_down: float32 [2, 1536, 576], P('section', 'seq')
- grad_gain_attn: float32 [2, 576], P('section', 'seq')
- grad_gain_mlp: float32 [2, 576], P('section', 'seq')
Inputs may be any that keep to these rules, and one draw needn't show every extreme that they name: `group_ids`: along each row the ids never fall; id 1 begins within the first 256 places and ends within the last 256 places, id 0 comes before it and id 2 after it.
All inputs are finite; a program needn't handle non-finite values.
Results may differ from a plain program's by a relative error of at most 0.04.
Values may be sent and summed in bfloat16 or wider, within the bound.
No kernel may reach another device: no remote copies, remote signals or barrier semaphores. Data moves between devices by JAX's collectives and lax.ppermute only.
A program may use at most 192 MiB of HBM per device.

v0:
```python
import functools

import jax
import jax.numpy as jnp
from jax import lax
from jax.experimental import pallas as pl
from jax.experimental.pallas import tpu as pltpu
from jax.sharding import PartitionSpec as P

D = 576
HQ = 9
KVH = 3
HD = 64
GROUPS = HQ // KVH
KVW = KVH * HD
LANES = 128
QKV = 1024
FF = 1536
CHUNKS = 4
SUB = D // CHUNKS // 2
TILE = FF // 4
PACK = 16
ROW_STEP = 256
KEY_STEP = 256
SCALE = HD**-0.5
SPARE = 8 * 1024 * 1024
EPSILON = 1e-05
MASKED = -1e30
F32 = jnp.float32
BF16 = jnp.bfloat16
VMEM = pl.BlockSpec(memory_space=pltpu.VMEM)
SMEM = pl.BlockSpec(memory_space=pltpu.SMEM)
ANY = pl.BlockSpec(memory_space=pl.ANY)
SWAP = [(0, 1), (1, 0)]


def mm(a, b):
    return jnp.dot(a, b, preferred_element_type=F32)


def mm_nt(a, b):
    return lax.dot_general(a, b, (((1,), (1,)), ((), ())), preferred_element_type=F32)


def mm_tn(a, b):
    return lax.dot_general(a, b, (((0,), (0,)), ((), ())), preferred_element_type=F32)


def shape(dims, kind=BF16):
    return jax.ShapeDtypeStruct(tuple(dims), kind)


def size_of(array):
    if not jnp.issubdtype(array.dtype, jnp.number):
        return 0
    *lead, rows, columns = (1, 1, *array.shape)
    size = -(-rows // 16) * 16 * -(-columns // LANES) * LANES * array.dtype.itemsize
    for dim in lead:
        size *= dim
    return size


def call(body, ins, specs, outs, scratch, flops, stack=(), room=None):
    moved = sum(a.size * a.dtype.itemsize for a in list(ins) + list(outs))
    inner, piled = len(ins), len(stack)
    held = [a for a, spec in zip(ins, specs) if spec is VMEM] + list(outs) + list(scratch)
    if room is None:
        room = sum(size_of(a) for a in held) + SPARE
        room += sum(size_of(a) for a in stack)
    piles = [shape((piled, *stack[0].shape), stack[0].dtype)] if piled else []

    def strip(*refs):
        mid = piled + inner
        if not piled:
            return body(*refs)
        pile, sems = refs[mid], refs[-1]
        copies = [
            pltpu.make_async_copy(source, pile.at[i], sems.at[i])
            for i, source in enumerate(refs[:piled])
        ]
        for copy in copies:
            copy.start()
        body(*refs[piled:mid], *refs[mid + 1 : -1])
        for copy in copies:
            copy.wait()

    return pl.pallas_call(
        strip,
        out_shape=tuple(piles) + tuple(outs),
        in_specs=[ANY] * piled + list(specs),
        out_specs=tuple([VMEM] * (len(piles) + len(outs))),
        scratch_shapes=list(scratch) + [pltpu.SemaphoreType.DMA((piled,))] * len(piles),
        compiler_params=pltpu.CompilerParams(vmem_limit_bytes=min(room, 56 * 1024 * 1024)),
        cost_estimate=pl.CostEstimate(
            flops=int(flops), bytes_accessed=int(moved), transcendentals=0
        ),
    )(*stack, *ins)


def hold(value, *others):
    return lax.optimization_barrier((value, others))[0]


def lane_of(dims):
    return lax.broadcasted_iota(jnp.int32, dims, len(dims) - 1)


def roll(value, by):
    return pltpu.roll(value, by, value.ndim - 1)


def low_half(dims):
    return lane_of(dims) < HD


def halves(value):
    first = (lane_of(value.shape) & (HD - 1)) < HD // 2
    return jnp.where(first, roll(value, LANES - HD // 2), roll(value, HD // 2))


def tiles_of(count, step):
    step = min(count, step)
    return [(start, step) for start in range(0, count, step)]


def norm_inverse(stream):
    return lax.rsqrt(jnp.mean(stream * stream, -1, keepdims=True) + EPSILON)


def norm_back(incoming, stream, inverse, gain):
    weighted = incoming * gain
    slope = jnp.mean(weighted * stream, -1, keepdims=True)
    grad_gain = jnp.sum(incoming * (stream * inverse), 0, keepdims=True)
    return inverse * (weighted - stream * (inverse * inverse * slope)), grad_gain


def start_copy(layer, core, mine, theirs, target, sem):
    @pl.when(core == layer)
    def _():
        pltpu.make_async_copy(mine, target, sem).start()

    @pl.when(core != layer)
    def _():
        pltpu.make_async_copy(theirs, target, sem).start()


class Weights:
    def __init__(self, layer, core, mine, theirs, targets, sems):
        self.pending = {}
        for number, (name, target) in enumerate(targets.items()):
            if name in ("qkv", "gains"):
                lines = pl.ds(0, D) if name == "qkv" else pl.ds(D, PACK)
                pair = mine["qkv"].at[lines], theirs["qkv"].at[lines]
            else:
                pair = mine[name], theirs[name]
            start_copy(layer, core, *pair, target, sems.at[number])
            self.pending[name] = (pair[0], target, sems.at[number])

    def wait(self, *names):
        for name in names:
            pltpu.make_async_copy(*self.pending.pop(name)).wait()


def gain_row(lines, kind):
    parts = lines[...].astype(F32)
    parts = [parts[3 * kind + i : 3 * kind + i + 1, :D] for i in range(3)]
    return parts[0] + parts[1] + parts[2]


def project_rows(stream, gain, w_ref, cos, sin, q_ref, kv_ref, start, count):
    normed = (stream * norm_inverse(stream) * gain).astype(BF16)
    raw = mm(normed, w_ref[...])
    low = low_half((count, LANES))
    tiles = []
    for t in range(6):
        tile = raw[:, t * LANES : (t + 1) * LANES]
        tiles.append(tile * cos + halves(tile) * sin)
    rows = pl.ds(start, count)
    for head in range(HQ):
        tile = tiles[head // 2]
        tile = roll(tile, HD) if head % 2 else tile
        q_ref[head, rows, :] = jnp.where(low, tile * SCALE, 0.0).astype(BF16)
    kv_ref[rows, 0:LANES] = jnp.where(low, roll(tiles[4], HD), roll(tiles[5], HD)).astype(BF16)
    kv_ref[rows, LANES : 2 * LANES] = jnp.where(
        low, roll(tiles[5], HD), raw[:, 6 * LANES : 7 * LANES]
    ).astype(BF16)
    kv_ref[rows, 2 * LANES :] = raw[:, 7 * LANES :].astype(BF16)


def place_keys(core, own, other, kz, vz):
    for part, index in ((own, core), (other, 1 - core)):
        blocks, half, _ = part.shape
        low = low_half((blocks, half, LANES))
        tiles = [part[:, :, t * LANES : (t + 1) * LANES].astype(F32) for t in range(3)]
        turned = [roll(tile, HD) for tile in tiles]
        for target, heads in (
            (kz, (tiles[0], turned[0], tiles[1])),
            (vz, (turned[1], tiles[2], turned[2])),
        ):
            for group in range(KVH):
                value = jnp.where(low, heads[group], 1.0).astype(BF16)
                target[group, :, pl.ds(index, 1)] = value[:, None]


def key_rows(ref, group, start, count):
    _, _, _, half, _ = ref.shape
    span = 2 * half
    part = ref[group, start // span : (start + count) // span]
    return part.reshape(count, LANES)


def places(core, wagon, rows, tokens, start, dims, axis):
    half = tokens // 2
    local = lax.broadcasted_iota(jnp.int32, dims, axis) + start
    block, inside = local // half, local % half
    return (wagon * rows + block) * tokens + core * half + inside


def opening(place, docs):
    first, second = docs[0], docs[1]
    return jnp.where(place < first, 0, jnp.where(place < second, first, second))


def query_blocks(geometry):
    rows, tokens, chips = geometry
    half = tokens // 2
    if chips == 1:
        return [(b * half, half, (b + 1) * tokens) for b in range(rows)]
    return [(0, rows * half, chips * rows * tokens)]


def attend(geometry, core, wagon, docs, q_ref, kz, vz, heads_out, q_out):
    rows, tokens, _ = geometry
    for start, count, keys in query_blocks(geometry):
        place = places(core, wagon, rows, tokens, start, (count, 1), 0)
        key_place = lane_of((1, keys))
        allowed = (key_place <= place) & (key_place >= opening(place, docs))
        bias = jnp.where(allowed, 0.0, MASKED)
        low = low_half((GROUPS * count, LANES))
        lane = lane_of((GROUPS * count, LANES))
        for group in range(KVH):
            heads = slice(group * GROUPS, (group + 1) * GROUPS)
            q = q_ref[heads, start : start + count, :].reshape(GROUPS * count, LANES)
            scores = mm_nt(q, key_rows(kz, group, 0, keys))
            scores = scores.reshape(GROUPS, count, keys) + bias[None]
            scores = scores.reshape(GROUPS * count, keys)
            top = jnp.max(scores, -1, keepdims=True)
            weights = jnp.exp(scores - top).astype(BF16)
            out = mm(weights, key_rows(vz, group, 0, keys))
            total = jnp.where(low, 1.0, out)
            lse = -(top + jnp.log(total))
            high = lse.astype(BF16).astype(F32)
            rest = lse - high
            middle = rest.astype(BF16).astype(F32)
            tail = jnp.where(
                lane == HD,
                high,
                jnp.where(lane == HD + 1, middle, jnp.where(lane == HD + 2, rest - middle, 0.0)),
            )
            q_aug = jnp.where(low, q.astype(F32), tail).astype(BF16)
            q_out[heads, start : start + count, :] = q_aug.reshape(GROUPS, count, LANES)
            out = jnp.where(low, out / jnp.where(low, roll(out, HD), 1.0), 0.0)
            heads_out[heads, start : start + count, :] = out.reshape(GROUPS, count, LANES)


def attend_back(geometry, core, wagon, docs, q_ref, do_ref, kz, vz, dq, dk, dv):
    rows, tokens, _ = geometry
    span = tokens
    dk[...] = jnp.zeros_like(dk)
    dv[...] = jnp.zeros_like(dv)
    for start, count, keys in query_blocks(geometry):
        width = GROUPS * count
        lane = lane_of((1, width)) % count
        half = tokens // 2
        local = lane + start
        place = (wagon * rows + local // half) * tokens + core * half + local % half
        first = opening(place, docs)
        for key_start, key_count in tiles_of(keys, KEY_STEP):
            key_place = key_start + lax.broadcasted_iota(jnp.int32, (key_count, 1), 0)
            allowed = (key_place <= place) & (key_place >= first)
            blocks = slice(key_start // span, (key_start + key_count) // span)
            for group in range(KVH):
                heads = slice(group * GROUPS, (group + 1) * GROUPS)
                q = q_ref[heads, start : start + count, :].reshape(width, LANES)
                do = do_ref[heads, start : start + count, :].reshape(width, LANES)
                k = key_rows(kz, group, key_start, key_count)
                v = key_rows(vz, group, key_start, key_count)
                probs = jnp.where(allowed, jnp.exp(mm_nt(k, q)), 0.0)
                slopes = (probs * mm_nt(v, do)).astype(BF16)
                part = (key_count // span, 2, half, LANES)
                dv[group, blocks] += mm(probs.astype(BF16), do).reshape(part)
                dk[group, blocks] += mm(slopes, q).reshape(part)
                back = mm_tn(slopes, k).reshape(GROUPS, count, LANES)
                if key_start == 0:
                    dq[heads, start : start + count, :] = back
                else:
                    dq[heads, start : start + count, :] += back


def pack_heads(ref, rows, tile):
    count = rows.size
    low = low_half((count, LANES))
    first = ref[2 * tile, rows, :]
    if 2 * tile + 1 == HQ:
        return jnp.where(low, first, 0.0)
    return jnp.where(low, first, roll(ref[2 * tile + 1, rows, :], HD))


def piece_bits(h, row):
    x_bit, y_bit = row & 1, row >> 1
    return (x_bit, y_bit) if h == 0 else (y_bit, x_bit)


def store_piece(place, turned, core, row, h, f, g, chunk, value, kept, sent):
    f_bit, g_bit = piece_bits(h, row)
    spot = chunk ^ place if turned else chunk
    spot = (spot & 1) * 2 + spot // 2 if turned else spot
    value = value.astype(BF16)

    @pl.when(core == h)
    def _():
        kept[f ^ f_bit, g ^ g_bit, spot] = value

    @pl.when(core != h)
    def _():
        sent[f ^ f_bit, g ^ g_bit, spot] = value


def pack_kernel(geometry, where, inputs, cotangent, ids, wq, wk, wv, gain1, gain2, *refs):
    rows, tokens, _ = geometry
    half = tokens // 2
    core, member = where[0], where[3]
    outs, w_ref, (counts, sems) = refs[: 2 * rows], refs[2 * rows], refs[2 * rows + 1 :]
    mine = pl.ds(pl.multiple_of(core * half, half), half)
    copies = []
    for step in range(rows):
        target = member ^ step
        docs = ids[pl.ds(target, 1), :]
        first = jnp.sum((docs < 1).astype(F32), -1, keepdims=True)
        second = jnp.sum((docs < 2).astype(F32), -1, keepdims=True)
        lane = lane_of((PACK, half))
        value = jnp.where(lane == 0, first, jnp.where(lane == 1, second, 0.0))
        counts[step] = value.astype(BF16)
        copies += [
            (inputs.at[target, :, mine], outs[step].at[pl.ds(0, D)]),
            (counts.at[step], outs[step].at[pl.ds(D, PACK)]),
            (cotangent.at[target, :, mine], outs[rows + step]),
        ]
    copies = [pltpu.make_async_copy(a, b, sems.at[i]) for i, (a, b) in enumerate(copies)]
    for copy in copies:
        copy.start()
    one = lax.broadcasted_iota(jnp.int32, (KVW, KVW), 0) == lane_of((KVW, KVW))
    one = jnp.where(one, 1.0, 0.0).astype(BF16)
    keys, values = mm_tn(wk[...], one), mm_tn(wv[...], one)
    queries = wq[...].astype(F32)
    zeros = jnp.zeros((D, HD), F32)
    w_ref[:D] = jnp.concatenate([queries, keys, zeros, values], 1).astype(BF16)
    lines = []
    for gain in (gain1, gain2):
        rest = gain[...]
        for _ in range(3):
            part = rest.astype(BF16).astype(F32)
            lines.append(part)
            rest = rest - part
    lines = jnp.concatenate(lines + [jnp.zeros((PACK - 6, D), F32)], 0)
    lines = jnp.concatenate([lines, jnp.zeros((PACK, QKV - D), F32)], 1)
    w_ref[D:] = lines.astype(BF16)
    for copy in copies:
        copy.wait()


def unpack(block, half):
    return block[:D].T if half % LANES == 0 else block[:half]


def project_kernel(geometry, where, *refs):
    rows, tokens, _ = geometry
    half = tokens // 2
    packets, refs = refs[:rows], refs[rows:]
    mine, theirs, cos, sin, x_ref, q_ref, kv_ref, w_ref, lines, sems = refs
    core, member = where[0], where[3]
    weights = Weights(
        0, core, {"qkv": mine}, {"qkv": theirs}, {"qkv": w_ref, "gains": lines}, sems
    )
    for step in range(rows):
        x_ref[member ^ step] = unpack(packets[step][...], half)
    weights.wait("qkv", "gains")
    gain = gain_row(lines, 0)
    for start, count in tiles_of(rows * half, max(ROW_STEP, half)):
        stream = x_ref[start // half : (start + count) // half].reshape(count, D).astype(F32)
        rows_of = slice(start, start + count)
        project_rows(
            stream, gain, w_ref, cos[rows_of], sin[rows_of], q_ref, kv_ref, start, count
        )


def store_blocks(geometry, where, target, start, value):
    rows, tokens, _ = geometry
    half = tokens // 2
    for block in range(start // half, (start + value.shape[0]) // half):
        part = value[block * half - start : (block + 1) * half - start]
        part = part.T if half % LANES == 0 else part
        target[block ^ where[3]] = part


def forward_kernel(layer, geometry, where, docs, *refs):
    x_ref, q_ref, own, other, cos, sin = refs[:6]
    wg, wg2, wu, wu2, wd, wd2, wo, wo2, wq, wq2 = refs[6:16]
    refs = refs[16:]
    if layer == 1:
        earlier, refs = refs[0], refs[1:]
    q_aug, att, middle_ref, gate_ref, up_ref, y_ref = refs[:6]
    outs = refs[6:]
    if layer == 0:
        blocks_ref, q_next, kv_next = outs[:3]
        outs = outs[3:]
    else:
        pair_refs, blocks_ref = outs[: geometry[0]], outs[geometry[0]]
        outs = outs[geometry[0] + 1 :]
    kz, vz, heads, wo_v, wg_v, wu_v, wd_v, lines, sems = outs[:9]
    core, wagon = where[0], where[4]
    mine = {"gate": wg, "up": wu, "down": wd, "out": wo, "qkv": wq}
    theirs = {"gate": wg2, "up": wu2, "down": wd2, "out": wo2, "qkv": wq2}
    names = {"out": wo_v, "gains": lines, "gate": wg_v, "up": wu_v, "down": wd_v}
    weights = Weights(layer, core, mine, theirs, names, sems)
    if layer == 0:
        wq_v, lines_next, sems_next = outs[9:]
        following = Weights(1, core, mine, theirs, {"qkv": wq_v, "gains": lines_next}, sems_next)
    place_keys(core, own, other, kz, vz)
    attend(geometry, core, wagon, docs, q_ref, kz, vz, heads, q_aug)
    weights.wait("out", "gains", "gate", "up", "down")
    gain_mlp = gain_row(lines, 1)
    if layer == 0:
        following.wait("qkv", "gains")
        gain_next = gain_row(lines_next, 0)
    tokens = x_ref.shape[0]
    half = geometry[1] // 2
    for start, count in tiles_of(tokens, max(ROW_STEP, half)):
        rows = pl.ds(start, count)
        for tile in range(4):
            att[rows, tile * LANES : (tile + 1) * LANES] = pack_heads(heads, rows, tile).astype(
                BF16
            )
        att[rows, 4 * LANES :] = heads[HQ - 1, rows, :HD].astype(BF16)
        middle = x_ref[rows, :].astype(F32) + mm(att[rows, :], wo_v[...])
        normed = (middle * norm_inverse(middle) * gain_mlp).astype(BF16)
        gate, up = mm(normed, wg_v[...]), mm(normed, wu_v[...])
        middle_ref[rows, :] = middle
        gate_ref[rows, :] = gate.astype(BF16)
        up_ref[rows, :] = up.astype(BF16)
        hidden = (gate * jax.nn.sigmoid(gate) * up).astype(BF16)
        result = (middle + mm_nt(hidden, wd_v[...])).astype(BF16)
        y_ref[rows, :] = result
        store_blocks(geometry, where, blocks_ref, start, result)
        if layer == 0:
            project_rows(
                result.astype(F32),
                gain_next,
                wq_v,
                cos[rows, :],
                sin[rows, :],
                q_next,
                kv_next,
                start,
                count,
            )
    if layer == 1:
        for step, pair in enumerate(pair_refs):
            pair[pl.ds(core, 1)] = earlier[pl.ds(step, 1)]
            pair[pl.ds(1 - core, 1)] = blocks_ref[pl.ds(step, 1)]


def feed_kernel(layer, geometry, where, *refs):
    rows_in, tokens_in, chips = geometry
    half = tokens_in // 2
    core, row, place, member = where[0], where[1], where[2], where[3]
    if layer == 1:
        packets, refs = refs[:rows_in], refs[rows_in:]
    else:
        grad_ref, refs = refs[0], refs[1:]
    middle_ref, gate_ref, up_ref, wd, wd2, wq, wq2 = refs[:7]
    refs = refs[7:]
    if layer == 1:
        grad_ref, refs = refs[0], refs[1:]
    dgate, dup, kept, sent, normed, turned, hidden, downs, wd_v, lines, sems = refs
    weights = Weights(
        layer,
        core,
        {"down": wd, "qkv": wq},
        {"down": wd2, "qkv": wq2},
        {"down": wd_v, "gains": lines},
        sems,
    )
    if layer == 1:
        for step in range(rows_in):
            grad_ref[member ^ step] = unpack(packets[step][...], half)
    weights.wait("down", "gains")
    gain_mlp = gain_row(lines, 1)
    tokens = middle_ref.shape[0]
    for start, count in tiles_of(tokens, max(ROW_STEP, half)):
        rows = pl.ds(start, count)
        if layer == 1:
            branch = grad_ref[start // half : (start + count) // half].reshape(count, D)
        else:
            branch = grad_ref[rows, :]
        middle = middle_ref[rows, :]
        normed[rows, :] = (middle * norm_inverse(middle) * gain_mlp).astype(BF16)
        gate, up = gate_ref[rows, :].astype(F32), up_ref[rows, :].astype(F32)
        sig = jax.nn.sigmoid(gate)
        lifted = gate * sig
        grad_hidden = mm(branch, wd_v[...])
        hidden[rows, :] = (lifted * up).astype(BF16)
        dgate[rows, :] = (grad_hidden * up * (sig + lifted * (1.0 - sig))).astype(BF16)
        dup[rows, :] = (grad_hidden * lifted).astype(BF16)
    turned[...] = grad_ref[...].reshape(tokens, D).T
    for chunk in range(CHUNKS):
        downs[chunk] = mm(turned[...], hidden[:, chunk * TILE : (chunk + 1) * TILE])
    turned[...] = normed[...].T
    for h in range(2):
        for f in range(2):
            columns = slice((2 * h + f) * TILE, (2 * h + f + 1) * TILE)
            gates = mm(turned[...], dgate[:, columns])
            ups = mm(turned[...], dup[:, columns])
            for g in range(2):
                for chunk in range(CHUNKS):
                    lines_of = slice((2 * chunk + g) * SUB, (2 * chunk + g + 1) * SUB)
                    spots = pl.ds(((2 * h + f) * 2 + g) * SUB, SUB)
                    value = jnp.concatenate(
                        [gates[lines_of], ups[lines_of], downs[chunk, spots, :]], 0
                    )
                    store_piece(place, chips == 1, core, row, h, f, g, chunk, value, kept, sent)


def middle_kernel(layer, geometry, where, *refs):
    grad_ref, middle_ref, dgate, dup, att, wg, wg2, wu, wu2, wo, wo2, wq, wq2 = refs[:13]
    dm_ref, gain_out, do_heads, wg_v, wu_v, wo_v, lines, sems = refs[13:]
    weights = Weights(
        layer,
        where[0],
        {"gate": wg, "up": wu, "out": wo, "qkv": wq},
        {"gate": wg2, "up": wu2, "out": wo2, "qkv": wq2},
        {"gate": wg_v, "up": wu_v, "out": wo_v, "gains": lines},
        sems,
    )
    weights.wait("gate", "up", "out", "gains")
    gain_mlp = gain_row(lines, 1)
    tokens = middle_ref.shape[0]
    grad_gain = jnp.zeros((1, D), F32)
    for start, count in tiles_of(tokens, ROW_STEP):
        rows = pl.ds(start, count)
        middle = middle_ref[rows, :]
        grad_normed = mm_nt(dgate[rows, :], wg_v[...]) + mm_nt(dup[rows, :], wu_v[...])
        back, more = norm_back(grad_normed, middle, norm_inverse(middle), gain_mlp)
        grad_gain = grad_gain + more
        dm = grad_ref[rows, :].astype(F32) + back
        dm_ref[rows, :] = dm
        grad_att = mm_nt(dm.astype(BF16), wo_v[...]).astype(BF16).astype(F32)
        low = low_half((count, LANES))
        lane = lane_of((count, LANES))
        for head in range(HQ):
            if head < HQ - 1:
                tile = slice(head // 2 * LANES, (head // 2 + 1) * LANES)
                do = grad_att[:, tile]
                out = att[rows, tile].astype(F32)
            else:
                pad = jnp.zeros((count, HD), F32)
                do = jnp.concatenate([grad_att[:, 4 * LANES :], pad], 1)
                out = jnp.concatenate([att[rows, 4 * LANES :].astype(F32), pad], 1)
            if head % 2:
                do, out = roll(do, HD), roll(out, HD)
            do = jnp.where(low, do, 0.0)
            delta = -jnp.sum(do * out, -1, keepdims=True)
            high = delta.astype(BF16).astype(F32)
            do = jnp.where(lane == HD, high, jnp.where(lane == HD + 1, delta - high, do))
            do_heads[head, rows, :] = do.astype(BF16)
    gain_out[...] = grad_gain


def attend_back_kernel(geometry, where, docs, *refs):
    q_aug, do_heads, own, other, cos, sin = refs[:6]
    dq_out, kept, sent = refs[6:9]
    kz, vz, dq, dk, dv = refs[9:]
    core, wagon = where[0], where[4]
    place_keys(core, own, other, kz, vz)
    attend_back(geometry, core, wagon, docs, q_aug, do_heads, kz, vz, dq, dk, dv)
    for start, count in tiles_of(q_aug.shape[1], ROW_STEP):
        rows = pl.ds(start, count)
        for tile in range(5):
            value = pack_heads(dq, rows, tile) * SCALE
            value = value * cos[rows, :] - halves(value) * sin[rows, :]
            dq_out[rows, tile * LANES : (tile + 1) * LANES] = value.astype(BF16)
    _, blocks, _, half, _ = dk.shape
    low = low_half((blocks, half, LANES))
    for target, index in ((kept, core), (sent, 1 - core)):

        def pick(ref, group):
            return ref[group, :, pl.ds(index, 1)].reshape(blocks, half, LANES)

        def join(first, second):
            return jnp.where(low, first, roll(second, HD)).astype(target.dtype)

        target[:, :, 0:LANES] = join(pick(dk, 0), pick(dk, 1))
        target[:, :, LANES : 2 * LANES] = join(pick(dk, 2), pick(dv, 0))
        target[:, :, 2 * LANES :] = join(pick(dv, 1), pick(dv, 2))


def input_back_kernel(layer, geometry, where, *refs):
    rows_in, tokens_in, chips = geometry
    dm_ref, att, x_ref, dq, dkv, dkv2, gain_mlp, wq, wq2, cos, sin = refs[:11]
    dx_ref, blocks_refs, refs = refs[11], refs[12 : 12 + rows_in], refs[12 + rows_in :]
    kept, sent, blocks_ref, dqkv, normed, da, wq_v, lines, sems = refs
    core, row, place = where[0], where[1], where[2]
    weights = Weights(
        layer, core, {"qkv": wq}, {"qkv": wq2}, {"qkv": wq_v, "gains": lines}, sems
    )
    weights.wait("qkv", "gains")
    gain = gain_row(lines, 0)
    tokens = x_ref.shape[0]
    half = tokens_in // 2
    grad_gain = jnp.zeros((1, D), F32)
    for start, count in tiles_of(tokens, max(ROW_STEP, half)):
        rows = pl.ds(start, count)
        low = low_half((count, LANES))
        grads = [
            dkv[rows, t * LANES : (t + 1) * LANES]
            + dkv2[rows, t * LANES : (t + 1) * LANES].astype(F32)
            for t in range(3)
        ]
        for tile in range(4):
            lanes = slice(tile * LANES, (tile + 1) * LANES)
            dqkv[rows, lanes] = dq[rows, lanes]
        turned = roll(grads[0], HD)

        def unrotate(value):
            return value * cos[rows, :] - halves(value) * sin[rows, :]

        last = dq[rows, 4 * LANES :].astype(F32)
        dqkv[rows, 4 * LANES : 5 * LANES] = jnp.where(low, last, unrotate(turned)).astype(BF16)
        keys = unrotate(jnp.where(low, turned, roll(grads[1], HD)))
        dqkv[rows, 5 * LANES : 6 * LANES] = keys.astype(BF16)
        dqkv[rows, 6 * LANES : 7 * LANES] = jnp.where(low, 0.0, grads[1]).astype(BF16)
        dqkv[rows, 7 * LANES :] = grads[2].astype(BF16)
        stream = x_ref[rows, :].astype(F32)
        inverse = norm_inverse(stream)
        normed[rows, :] = (stream * inverse * gain).astype(BF16)
        grad_normed = mm_nt(dqkv[rows, :], wq_v[...])
        back, more = norm_back(grad_normed, stream, inverse, gain)
        grad_gain = grad_gain + more
        dm = dm_ref[rows, :]
        dx = (dm + back).astype(BF16)
        dx_ref[rows, :] = dx
        store_blocks(geometry, where, blocks_ref, start, dx)
        da[rows, 0:D] = dm.astype(BF16)
        da[rows, D:] = jnp.zeros((count, 2 * TILE - D), BF16)
    for step, block in enumerate(blocks_refs):
        block[...] = blocks_ref[step]
    pad = jnp.zeros((1, 2 * TILE - D), F32)
    lines = []
    for vector in (grad_gain, gain_mlp[...]):
        wide = jnp.concatenate([vector, pad], 1)
        lines += [wide[:, :TILE], wide[:, TILE:]]
    lines = jnp.concatenate(lines + [jnp.zeros((4, TILE), F32)], 0)
    for h in range(2):
        for f in range(2):
            if h == 0:
                value = mm_tn(normed[...], dqkv[:, f * TILE : (f + 1) * TILE])
            else:
                value = mm_tn(att[...], da[:, f * TILE : (f + 1) * TILE])
            if h == 1 and f == 1:
                more = mm_tn(normed[...], dqkv[:, 6 * LANES :])
                value = jnp.concatenate(
                    [
                        value[:, :LANES],
                        value[:, LANES : 2 * LANES] + more[:, :LANES],
                        more[:, LANES:],
                    ],
                    1,
                )
            for g in range(2):
                for chunk in range(CHUNKS):
                    part = value[(2 * chunk + g) * SUB : (2 * chunk + g + 1) * SUB]
                    part = jnp.concatenate([part, lines], 0)
                    store_piece(place, chips == 1, core, row, h, f, g, chunk, part, kept, sent)


def owners_kernel(geometry, where, *refs):
    rows, tokens, _ = geometry
    half = tokens // 2
    core, member = where[0], where[3]
    sets = [refs[i : i + rows + 1] for i in range(0, len(refs) - 2, rows + 1)]
    out, sems = refs[-2:]

    def move(blocks):
        copies = []
        for step in range(rows):
            target = member ^ step
            for side, index in ((0, core), (1, 1 - core)):
                lanes = pl.ds(pl.multiple_of(index * half, half), half)
                source = blocks[rows].at[step] if side else blocks[step]
                if len(sets) == 1:
                    source = source.at[side]
                sem = sems.at[2 * step + side]
                copies.append(pltpu.make_async_copy(source, out.at[target, :, lanes], sem))
        for copy in copies:
            copy.start()
        for copy in copies:
            copy.wait()

    if len(sets) == 1:
        move(sets[0])
    else:
        for number in range(2):

            @pl.when(core == number)
            def _():
                move(sets[number])


def gather_kernel(where, *refs):
    mlp0, mlp1, attn = refs[:2], refs[2:4], refs[4:6]
    wq, wk, wv, wo, wg, wu, wd, g1, g2 = refs[6:15]
    wide, share = refs[15:]
    core, row, place = where[0], where[1], where[2]
    for step in range(4):
        peer = row ^ step
        x_bit, y_bit = peer & 1, peer >> 1
        for kind in range(2):
            h = core if kind == 0 else 1 - core
            f = jnp.where(h == 0, x_bit, y_bit)
            g = jnp.where(h == 0, y_bit, x_bit)

            @pl.when(core == 0)
            def _():
                share[...] = mlp0[kind][step]

            @pl.when(core == 1)
            def _():
                share[...] = mlp1[1 - kind][step]

            part = share[...].astype(F32)
            rows = pl.ds(pl.multiple_of(g * SUB, 8), SUB)
            tile = 2 * h + f
            columns = pl.ds(pl.multiple_of(tile * TILE, LANES), TILE)
            wg[0, rows, columns] = part[:SUB]
            wu[0, rows, columns] = part[SUB : 2 * SUB]
            wd[0, pl.ds(pl.multiple_of((2 * tile + g) * SUB, 8), SUB), :] = part[2 * SUB :]
            part = attn[kind][step, core].astype(F32)
            wide[rows, columns] = part[:SUB]
    wq[0] = wide[:, :D]
    wk[0] = wide[:, D : D + KVW]
    wo[0] = wide[:, 2 * TILE : 2 * TILE + D]
    wv[0] = wide[:, 2 * TILE + D :]
    lines = attn[0][0, core].astype(F32)[SUB:]
    for kind, out in ((0, g1), (1, g2)):
        whole = jnp.concatenate(
            [lines[2 * kind : 2 * kind + 1], lines[2 * kind + 1 : 2 * kind + 2]], 1
        )
        for chunk in range(CHUNKS):

            @pl.when(place == chunk)
            def _():
                out[...] = whole[:, chunk * 2 * SUB : (chunk + 1) * 2 * SUB]


def rotary(place):
    frequency = 10000.0 ** (-jnp.arange(HD // 2, dtype=F32) * 2.0 / HD)
    angles = place.astype(F32)[:, None] * frequency[None, :]
    cosine, sine = jnp.cos(angles), jnp.sin(angles)
    return jnp.concatenate([cosine] * 4, 1), jnp.concatenate([-sine, sine] * 2, 1)


def on_device(
    inputs,
    cotangent,
    group_ids,
    w_query,
    w_key,
    w_value,
    w_out,
    w_gate,
    w_up,
    w_down,
    gain_attn,
    gain_mlp,
):
    core = lax.axis_index("section")
    row = lax.axis_index("row")
    place = lax.axis_index("seq")
    spans = lax.axis_size("seq")
    rows, tokens, _ = inputs.shape
    half = tokens // 2
    chips = spans // rows
    member, wagon = place % rows, place // rows
    own = rows * half
    blocks = chips * rows
    length = blocks * tokens
    geometry = (rows, tokens, chips)
    flipped = half % LANES == 0
    where = jnp.stack([core, row, place, member, wagon]).astype(jnp.int32)
    clans = [[b + rows * j for j in range(chips)] for b in range(rows)]

    def turn(step):
        return [(s, s ^ step) for s in range(spans)]

    def sems(count):
        return pltpu.SemaphoreType.DMA((count,))

    def vmem(*dims, kind=BF16):
        return pltpu.VMEM(dims, kind)

    def flip(array):
        return jnp.swapaxes(array, -1, -2)

    pack_ins = [
        where,
        flip(inputs),
        flip(cotangent),
        group_ids,
        w_query[0],
        flip(w_key[0]),
        flip(w_value[0]),
        gain_attn,
        gain_mlp,
    ]
    if flipped:
        packed = call(
            functools.partial(pack_kernel, geometry),
            pack_ins,
            [SMEM] + [ANY] * 2 + [VMEM] * 6,
            [shape((D + PACK, half))] * rows + [shape((D, half))] * rows + [shape((D + PACK, QKV))],
            [vmem(rows, PACK, half), sems(3 * rows)],
            0,
            room=56 * 1024 * 1024,
        )
        packets, shares, w_qkv = packed[:rows], packed[rows : 2 * rows], packed[-1]
    else:
        packets, shares = [], []
        below = [jnp.sum((group_ids < i).astype(F32), 1) for i in (1, 2)]
        counts = jnp.pad(jnp.stack(below, 1), ((0, 0), (0, D - 2))).astype(BF16)
        counts = jnp.pad(counts[:, None], ((0, 0), (0, PACK - 1), (0, 0)))
        for step in range(rows):
            target = member ^ step
            for array, outs in ((inputs, packets), (cotangent, shares)):
                part = lax.dynamic_index_in_dim(array, target, 0, False)
                part = lax.dynamic_slice_in_dim(part, core * half, half, 0)
                outs.append(part)
            line = lax.dynamic_index_in_dim(counts, target, 0, False)
            packets[-1] = jnp.concatenate([packets[-1], line], 0)
        w_qkv = jnp.concatenate(
            [w_query[0], w_key[0], jnp.zeros((D, HD), BF16), w_value[0]], 1
        )
        parts, rest = [], jnp.concatenate([gain_attn, gain_mlp], 0)
        for _ in range(3):
            parts.append(rest.astype(BF16))
            rest = rest - parts[-1].astype(F32)
        lines = jnp.stack(parts, 1).reshape(6, D)
        w_qkv = jnp.concatenate([w_qkv, jnp.pad(lines, ((0, PACK - 6), (0, QKV - D)))], 0)
    packets = [packets[0]] + [
        lax.ppermute(packets[step], "seq", turn(step)) for step in range(1, rows)
    ]
    w_qkv = [w_qkv, lax.ppermute(w_qkv, "section", SWAP)]
    mine = {"gate": w_gate[0], "up": w_up[0], "down": flip(w_down[0]), "out": w_out[0]}
    gates = dict(zip(mine, [w_qkv[1], *packets[1:4]]))
    pairs = {
        name: (value, lax.ppermute(hold(value, gates[name]), "section", SWAP))
        for name, value in mine.items()
    }
    pairs["qkv"] = w_qkv

    def weights_of(*names):
        return [side for name in names for side in pairs[name]]

    if flipped:
        docs = sum(packet[D, :2].astype(F32) for packet in packets)
    else:
        docs = sum(packet[half, :2].astype(F32) for packet in packets)
    if chips > 1:
        docs = lax.psum(docs, "seq", axis_index_groups=clans)
    docs = docs.astype(jnp.int32)
    local = jnp.arange(own, dtype=jnp.int32)
    tables = rotary((wagon * rows + local // half) * tokens + core * half + local % half)

    x_in, query, kv = call(
        functools.partial(project_kernel, geometry),
        [where, *packets, *w_qkv, *tables],
        [SMEM] + [VMEM] * rows + [ANY] * 2 + [VMEM] * 2,
        [shape((rows, half, D)), shape((HQ, own, LANES)), shape((own, 2 * KVW))],
        [vmem(D, QKV), vmem(PACK, QKV), sems(2)],
        2 * own * D * QKV,
    )
    x_in = x_in.reshape(own, D)

    def exchange(kv):
        kv = kv.reshape(rows, half, 2 * KVW)
        if chips > 1:
            kv = lax.all_gather(kv, "seq", axis=0, tiled=True, axis_index_groups=clans)
        return kv, lax.ppermute(kv, "section", SWAP)

    key_scratch = [vmem(KVH, blocks, 2, half, LANES)] * 2
    head_scratch = [vmem(HQ, own, LANES, kind=F32)]
    weight = {"gate": vmem(D, FF), "up": vmem(D, FF), "down": vmem(D, FF), "out": vmem(D, D)}
    lines_scratch = vmem(PACK, QKV)
    attn_flops = 4 * HQ * own * length * LANES
    feed_flops = 2 * own * D * (D + 3 * FF)
    flat = shape((own, D))
    wide = shape((own, FF))
    heads = shape((HQ, own, LANES))
    sent_blocks = shape((rows, D, half) if flipped else (rows, half, D))

    def forward(layer, x, query, kv, *earlier):
        outs = [heads, flat, shape((own, D), F32), wide, wide, flat, sent_blocks]
        scratch = key_scratch + head_scratch
        scratch += [weight["out"], weight["gate"], weight["up"], weight["down"]]
        scratch += [lines_scratch, sems(5)]
        if layer == 0:
            outs += [heads, shape((own, 2 * KVW))]
            scratch += [vmem(D, QKV), lines_scratch, sems(2)]
        else:
            scratch = [vmem(*sent_blocks.shape)] + scratch
            outs = outs[:-1] + [shape((2,) + sent_blocks.shape[1:])] * rows
        return call(
            functools.partial(forward_kernel, layer, geometry),
            [where, docs, x, query, *kv, *tables]
            + weights_of("gate", "up", "down", "out", "qkv")
            + list(earlier),
            [SMEM] * 2 + [VMEM] * 6 + [ANY] * 10 + [VMEM] * len(earlier),
            outs,
            scratch,
            attn_flops + feed_flops,
        )

    kv0 = exchange(kv)
    q0, att0, middle0, gate0, up0, y0, blocks0, query, kv = forward(0, x_in, query, kv0)
    shares = [shares[0]] + [
        lax.ppermute(shares[step], "seq", turn(step)) for step in range(1, rows)
    ]
    kv1 = exchange(kv)
    outs = forward(1, y0, query, kv1, blocks0)
    q1, att1, middle1, gate1, up1, y1, *pair_blocks = hold(outs, shares)
    mlp_pieces = shape((2, 2, CHUNKS, 3 * SUB, TILE))
    attn_pieces = shape((2, 2, CHUNKS, SUB + 8, TILE))

    def feed(layer, where, grads, middle, gate, up, **order):
        outs = [shape((rows, half, D))] if layer == 1 else []
        return call(
            functools.partial(feed_kernel, layer, geometry),
            [where, *grads, middle, gate, up] + weights_of("down", "qkv"),
            [SMEM] + [VMEM] * (len(grads) + 3) + [ANY] * 4,
            outs + [wide, wide, mlp_pieces, mlp_pieces],
            [vmem(own, D), vmem(D, own), vmem(own, FF), vmem(CHUNKS, D, TILE, kind=F32)]
            + [weight["down"], lines_scratch, sems(2)],
            8 * own * D * FF,
            **order,
        )

    def spread(layer, where, grad, middle, dgate, dup, att, **order):
        return call(
            functools.partial(middle_kernel, layer, geometry),
            [where, grad, middle, dgate, dup, att] + weights_of("gate", "up", "out", "qkv"),
            [SMEM] + [VMEM] * 5 + [ANY] * 8,
            [shape((own, D), F32), shape((1, D), F32), heads],
            [weight["gate"], weight["up"], weight["out"], lines_scratch, sems(4)],
            2 * own * D * (D + 2 * FF),
            **order,
        )

    def attention_back(where, q_aug, do_heads, kv, **order):
        return call(
            functools.partial(attend_back_kernel, geometry),
            [where, docs, q_aug, do_heads, *kv, *tables],
            [SMEM] * 2 + [VMEM] * 6,
            [
                shape((own, 5 * LANES)),
                shape((blocks, half, 2 * KVW), F32),
                shape((blocks, half, 2 * KVW)),
            ],
            key_scratch
            + head_scratch
            + [vmem(KVH, blocks, 2, half, LANES, kind=F32)] * 2,
            3 * attn_flops,
            **order,
        )

    def trade_keys(dq, dkv, dkv_sent):
        dkv_got = lax.ppermute(dkv_sent, "section", SWAP)
        if chips > 1:
            dkv = lax.psum_scatter(
                (dkv + dkv_got).astype(BF16),
                "seq",
                scatter_dimension=0,
                tiled=True,
                axis_index_groups=clans,
            ).astype(F32)
            dkv_got = jnp.zeros(dkv.shape, BF16)
        return dq, dkv.reshape(own, 2 * KVW), dkv_got.reshape(own, 2 * KVW)

    def input_back(layer, where, dm, att, x, dq, dkv, dkv_got, gain_grad, **order):
        return call(
            functools.partial(input_back_kernel, layer, geometry),
            [where, dm, att, x, dq, dkv, dkv_got, gain_grad, *w_qkv, *tables],
            [SMEM] + [VMEM] * 7 + [ANY] * 2 + [VMEM] * 2,
            [flat]
            + [shape(sent_blocks.shape[1:])] * rows
            + [attn_pieces, attn_pieces],
            [vmem(*sent_blocks.shape), vmem(own, QKV), vmem(own, D), vmem(own, 2 * TILE), vmem(D, QKV)]
            + [lines_scratch, sems(2)],
            4 * own * D * QKV + 2 * own * D * D,
            **order,
        )

    def line(section, r):
        return section * 4 + r

    first_pairs = [(line(0, r), line(0, r ^ 1)) for r in range(4)]
    first_pairs += [(line(1, r), line(1, r ^ 2)) for r in range(4)]
    second_pairs = [(line(0, r), line(0, r ^ 2)) for r in range(4)]
    second_pairs += [(line(1, r), line(1, r ^ 1)) for r in range(4)]

    def to_core(sent):
        return lax.ppermute(sent, "section", SWAP)

    def sum_cores(kept, got):
        return (kept[1].astype(F32) + got[1]).astype(BF16)

    def to_first(out):
        return lax.ppermute(out, ("section", "row"), first_pairs)

    def sum_first(kept, got, near):
        return (kept[0, 1].astype(F32) + got[0, 1] + near[1]).astype(BF16)

    def to_second(out):
        return lax.ppermute(out, ("section", "row"), second_pairs)

    def sum_second(kept, got, near, far):
        return (kept[0, 0].astype(F32) + got[0, 0] + near[0] + far).astype(BF16)

    def to_seq(total):
        if chips > 1:
            return [lax.psum(total, "seq")]
        return [total[0]] + [
            lax.ppermute(total[spot], "seq", turn(step)) for spot, step in ((2, 1), (1, 2), (3, 3))
        ]

    def halve(total, step):
        count = total.shape[0] // 2
        got = lax.ppermute(total[count:], "seq", turn(step))
        return got, (total[:count].astype(F32) + got).astype(BF16)

    def sum_seq(first, others):
        return sum((part.astype(F32) for part in others), first.astype(F32)).astype(BF16)

    def to_rows(blocks):
        return list(blocks[:1]) + [
            lax.ppermute(blocks[step], "seq", turn(step)) for step in range(1, rows)
        ]

    def to_owners(sets):
        if flipped:
            return call(
                functools.partial(owners_kernel, geometry),
                [where, *sum(sets, [])],
                [SMEM] + [ANY] * ((rows + 1) * len(sets)),
                [shape((rows, D, tokens))],
                [sems(2 * rows)],
                0,
            )[0]
        out = jnp.zeros((rows, 2, half, D), BF16)
        for step in range(rows):
            if len(sets) == 1:
                pair = [sets[0][step][0], sets[0][rows][step][1]]
            else:
                pair = [
                    jnp.where(core == 0, sets[0][step], sets[1][step]),
                    jnp.where(core == 0, sets[0][rows][step], sets[1][rows][step]),
                ]
            pair = jnp.where(core == 0, jnp.stack(pair), jnp.stack(pair[::-1]))
            out = lax.dynamic_update_index_in_dim(out, pair, member ^ step, 0)
        return flip(out.reshape(rows, tokens, D))

    def to_all(piece):
        return [piece] + [
            lax.ppermute(piece, "row", [(r, r ^ step) for r in range(4)]) for step in range(1, 4)
        ]

    ys = to_rows(pair_blocks)
    grad1, dgate, dup, kept_m1, sent = hold(feed(1, where, shares, middle1, gate1, up1), ys[2])
    grad1 = grad1.reshape(own, D)
    got_m1 = to_core(sent)

    dm, gain_grad, do_heads = hold(
        spread(1, where, grad1, middle1, dgate, dup, att1), ys[1], got_m1
    )

    out = sum_cores(hold(kept_m1, dm), got_m1)
    near_m1 = to_first(out)
    kept_m1, *outs = hold(
        (kept_m1, *attention_back(where, q1, do_heads, kv1)), ys[3], near_m1
    )
    dq, dkv, dkv_got = trade_keys(*outs)

    out = sum_first(kept_m1, got_m1, near_m1)
    far_m1 = to_second(out)
    outs = input_back(
        1, hold(where, out), dm, att1, y0, dq, dkv, dkv_got, gain_grad, stack=ys
    )
    kept_m1, pile, dx1, *blocks1, kept_a1, sent = hold((kept_m1, *outs), far_m1)
    got_a1 = to_core(sent)
    ys.append(to_core(pile))

    total = sum_second(kept_m1, got_m1, near_m1, far_m1)
    parts_m1 = to_seq(total)
    outs = feed(0, hold(where, total), [dx1], middle0, gate0, up0)
    dgate, dup, kept_m0, sent = hold(outs, ys[rows], got_a1, parts_m1)
    got_m0 = to_core(sent)

    mlp1 = to_all(sum_seq(hold(parts_m1[0], dgate), parts_m1[1:]))
    out = sum_cores(hold(kept_a1, dgate), got_a1)
    near_a1 = to_first(out)
    activations = to_owners([ys])
    outs = spread(0, hold(where, out, mlp1[0]), dx1, middle0, dgate, dup, att0)
    dm, gain_grad, do_heads = hold(outs, activations, mlp1, near_a1, got_m0)

    out_a1 = sum_first(hold(kept_a1, dm), got_a1, near_a1)
    far_a1 = to_second(out_a1)
    out_m0 = sum_cores(hold(kept_m0, dm), got_m0)
    near_m0 = to_first(out_m0)
    dxs1 = to_rows(hold(blocks1, dm))
    pile, *outs = attention_back(hold(where, out_a1, out_m0), q0, do_heads, kv0, stack=mlp1)
    kept_a1, kept_m0, pile, *outs = hold(
        (kept_a1, kept_m0, pile, *outs), far_a1, near_m0, dxs1
    )
    mlp1 = lax.ppermute(pile, "section", [(0, 1)]), pile
    dq, dkv, dkv_got = trade_keys(*outs)

    total_a1 = sum_second(kept_a1, got_a1, near_a1, far_a1)
    parts_a1 = to_seq(total_a1)
    out = sum_first(kept_m0, got_m0, near_m0)
    far_m0 = to_second(out)
    outs = input_back(
        0, hold(where, out, total_a1), dm, att0, x_in, dq, dkv, dkv_got, gain_grad, stack=dxs1
    )
    kept_m0, pile, dx0, *blocks0, kept_a0, sent = hold(
        (kept_m0, *outs), far_m0, parts_a1, mlp1[0]
    )

    got_a0 = to_core(sent)
    total = sum_second(kept_m0, got_m0, near_m0, far_m0)
    out = sum_cores(hold(kept_a0, total), got_a0)
    near_a0 = to_first(out)
    if chips == 1:
        got, total = halve(total, 1)
        kept_a0 = hold(kept_a0, got, near_a0)
        got, total = halve(total, 2)
        piece = total[0]
    else:
        piece = lax.psum(total, "seq")
    out = sum_first(kept_a0, got_a0, near_a0)
    far_a0 = to_second(out)
    mlp0 = to_all(piece)
    total = sum_second(hold(kept_a0, piece), got_a0, near_a0, far_a0)
    parts_a0 = to_seq(total)
    blocks0, pile = hold((blocks0, pile), total)
    dxs1.append(lax.ppermute(pile, "section", [(0, 1)]))
    dxs0 = to_rows(blocks0)
    attn = jnp.stack([sum_seq(p[0], p[1:]) for p in (parts_a0, parts_a1)])
    mlp0 = hold(mlp0, attn)
    attn = to_all(attn)
    mlp0 = jnp.stack(mlp0)
    mlp0 = mlp0, lax.ppermute(mlp0, "section", [(1, 0)])
    dxs0 = hold(dxs0, attn)
    attn = jnp.stack(attn)
    attn = attn, to_core(attn)
    dxs0.append(lax.ppermute(hold(jnp.stack(dxs0), attn[0]), "section", [(1, 0)]))
    input_grads = to_owners([dxs0, dxs1])
    input_grads = flip(input_grads)[None]
    activations = flip(activations)[None]
    share = D // spans
    if chips == 1:
        grads = call(
            gather_kernel,
            [where, *mlp0, *mlp1, *attn],
            [SMEM] + [VMEM] * 6,
            [shape((1, share, width), F32) for width in (D, KVW, KVW, D, FF, FF)]
            + [shape((1, D, TILE), F32)]
            + [shape((1, share), F32)] * 2,
            [vmem(2 * SUB, FF, kind=F32), vmem(3 * SUB, TILE)],
            0,
        )
        grads = list(grads)
        grads[6] = flip(grads[6])
        return (activations, input_grads) + tuple(grads)

    def ordered(parts):
        parts = parts.reshape(2, 4, *parts.shape[1:]).swapaxes(0, 1).astype(F32)
        parts = jnp.take(parts, jnp.arange(4) ^ row, axis=0)
        parts = jnp.take(parts, jnp.arange(2) ^ core, axis=1)
        parts = parts.reshape((2, 2) + parts.shape[1:])
        return jnp.stack([parts[:, :, 0].swapaxes(0, 1), parts[:, :, 1]])

    def rows_of(part):
        full = part.transpose(3, 2, 4, 0, 1, 5).reshape(D, FF)
        return lax.dynamic_slice_in_dim(full, place * share, share, 0)[None]

    mlp1 = jnp.concatenate([mlp1[1], mlp1[0]], 0)
    mlp = ordered(jnp.where(core == 0, jnp.concatenate(mlp0, 0), mlp1))
    attn = ordered(lax.dynamic_index_in_dim(jnp.concatenate(attn, 0), core, 1, False))
    downs = mlp[..., 2 * SUB :, :].transpose(0, 1, 2, 4, 3, 5).reshape(D, FF)
    downs = lax.dynamic_slice_in_dim(downs, place * (FF // spans), FF // spans, 1).T[None]
    full = rows_of(attn[..., :SUB, :])
    lines = attn[0, 0, 0, 0, SUB : SUB + 4].reshape(2, 2 * TILE)[:, :D]
    lines = lax.dynamic_slice_in_dim(lines, place * share, share, 1)
    return (
        activations,
        input_grads,
        full[..., :D],
        full[..., D : D + KVW],
        full[..., 2 * TILE + D :],
        full[..., 2 * TILE : 2 * TILE + D],
        rows_of(mlp[..., :SUB, :]),
        rows_of(mlp[..., SUB : 2 * SUB, :]),
        downs,
        lines[:1],
        lines[1:],
    )


def solution(mesh):
    weights = P("section", None, None)
    shares = P("section", "seq", None)
    return jax.shard_map(
        on_device,
        mesh=mesh,
        in_specs=(P("row", "seq", None), P("row", "seq", None), P("row", "seq"))
        + (weights,) * 7
        + (P("section", None),) * 2,
        out_specs=(P("section", "row", "seq", None),) * 2
        + (shares,) * 7
        + (P("section", "seq"),) * 2,
        check_vma=False,
    )
```

profile of v0, /device:TPU:0, one launch (start us, length us, event | category | flops | bytes accessed | tf_op | source)
XLA Modules:
  0.0 252.9 jit_solution(14948965396962232572)
XLA Ops:
  1.3 4.3 %shard_map.203 = (bf16[592,128]{1,0:T(8,128)(2,1)}, bf16[592,128]{1,0:T(8,128)(2,1)}, bf16[592,128]{1,0:T(8,128)(2,1)}, bf16[592,128]{1,0:T(8,128)(2,1)}, bf16[5...) custom-call(s32[5]{0:T(128)} %stack.77.refs_0_.refs_4_, ...), custom_call_target="tpu_custom_call" | custom-call | bytes 5882388 | tf_op jit(solution)/shard_map/pallas_call | solution.py:87
  6.1 2.6 %collective-permute-start = (bf16[592,128]{1,0:T(8,128)(2,1)}, bf16[592,128]{1,0:T(8,128)(2,1)S(1)}, u32[]{:S(2)}, u32[]{:S(2)}) collective-permute-start(bf16[592,128]{1,0:T(8,128)(2,1)} %get-tuple-element.174), channel_id=1, source_target_pairs={{0,1},{1,0},{2,3},{3,2},{4,5},{5,4},{6,7},{7,6},{8,9},{9,8},{10,11... | collective-permute-start | bytes 454664 | tf_op jit(solution)/shard_map/ppermute | solution.py:859
  8.8 2.6 %collective-permute-start.1 = (bf16[592,128]{1,0:T(8,128)(2,1)}, bf16[592,128]{1,0:T(8,128)(2,1)S(1)}, u32[]{:S(2)}, u32[]{:S(2)}) collective-permute-start(bf16[592,128]{1,0:T(8,128)(2,1)} %get-tuple-element.175), channel_id=1, source_target_pairs={{0,2},{1,3},{2,0},{3,1},{4,6},{5,7},{6,4},{7,5},{8,10},{9,11},{10,... | collective-permute-start | bytes 454664 | tf_op jit(solution)/shard_map/ppermute | solution.py:859
  11.4 5.3 %collective-permute-done.refs_2_ = bf16[592,128]{1,0:T(8,128)(2,1)S(1)} collective-permute-done((bf16[592,128]{1,0:T(8,128)(2,1)}, bf16[592,128]{1,0:T(8,128)(2,1)S(1)}, u32[]{:S(2)}, u32[]{:S(2)}) %collective-permute-start) | collective-permute-done | bytes 151584 | tf_op jit(solution)/shard_map/ppermute | solution.py:859
  16.7 2.5 %collective-permute-done.1.refs_3_ = bf16[592,128]{1,0:T(8,128)(2,1)S(1)} collective-permute-done((bf16[592,128]{1,0:T(8,128)(2,1)}, bf16[592,128]{1,0:T(8,128)(2,1)S(1)}, u32[]{:S(2)}, u32[]{:S(2)}) %collective-permute-start.1) | collective-permute-done | bytes 151584 | tf_op jit(solution)/shard_map/ppermute | solution.py:859
  20.4 2.5 collective-permute-start.2
  22.9 6.1 %collective-permute-done.2.refs_4_ = bf16[592,128]{1,0:T(8,128)(2,1)} collective-permute-done((bf16[592,128]{1,0:T(8,128)(2,1)}, bf16[592,128]{1,0:T(8,128)(2,1)}, u32[]{:S(2)}, u32[]{:S(2)}) %collective-permute-start.2) | collective-permute-done | bytes 151584 | tf_op jit(solution)/shard_map/ppermute | solution.py:859
  30.5 3.5 %shard_map.204 = (bf16[4,128,576]{2,1,0:T(8,128)(2,1)S(1)}, bf16[9,512,128]{2,1,0:T(8,128)(2,1)S(1)}, bf16[512,384]{1,0:T(8,128)(2,1)S(1)}) custom-call(s32[5]{0:T(128)S(1)} %copy-done.5, bf16[592,128]{1,0:T(8,128)(2,1)S(1)} %copy-done.2, bf16[592,128]{1,0:T(8,128)(2,1)S(1)} %collective-permute-done.refs_2_, bf16[592,128]{1,0:T(8,128)(2,1)S(1)} %copy-done.4, ...), custom_call_target="tpu_custom_call" | custom-call | flops 603979776 | bytes 5718036 | tf_op jit(solution)/shard_map/pallas_call | solution.py:87
  36.0 13.8 %shard_map.205 = (bf16[9,512,128]{2,1,0:T(8,128)(2,1)S(1)}, bf16[512,576]{1,0:T(8,128)(2,1)S(1)}, f32[512,576]{1,0:T(8,128)S(1)}, bf16[512,1536]{1,0:T(8,128)(2,...) custom-call(s32[5]{0:T(128)S(1)} %copy-done.5, ...), custom_call_target="tpu_custom_call" | custom-call | flops 5473566720 | bytes 26296348 | tf_op jit(solution)/shard_map/pallas_call | solution.py:87
  51.0 1.2 copy-done.15
  52.5 1.8 collective-permute-start.10
  54.3 1.2 collective-permute-start.11
  55.6 1.3 collective-permute-start.12
  56.9 12.8 %shard_map.206 = (bf16[9,512,128]{2,1,0:T(8,128)(2,1)S(1)}, bf16[512,576]{1,0:T(8,128)(2,1)S(1)}, f32[512,576]{1,0:T(8,128)S(1)}, bf16[512,1536]{1,0:T(8,128)(2,...) custom-call(s32[5]{0:T(128)S(1)} %copy-done.5, ...), custom_call_target="tpu_custom_call" | custom-call | flops 5473566720 | bytes 25903132 | tf_op jit(solution)/shard_map/pallas_call | solution.py:87
  71.7 9.3 %shard_map.207 = (bf16[4,128,576]{2,1,0:T(8,128)(2,1)S(1)}, bf16[512,1536]{1,0:T(8,128)(2,1)S(1)}, bf16[512,1536]{1,0:T(8,128)(2,1)S(1)}, bf16[2,2,4,216,384]{4,...) custom-call(s32[5]{0:T(128)S(1)} %copy-done.5, bf16[576,128]{1,0:T(8,128)(2,1)S(1)} %copy-done.10, ...), custom_call_target="tpu_custom_call" | custom-call | flops 3623878656 | bytes 19922964 | tf_op jit(solution)/shard_map/pallas_call | solution.py:87
  80.9 5.5 %collective-permute-done.14.refs_2_.refs_3_ = bf16[2,576,128]{2,1,0:T(8,128)(2,1)S(1)} collective-permute-done((bf16[2,576,128]{2,1,0:T(8,128)(2,1)S(1)}, bf16[2,576,128]{2,1,0:T(8,128)(2,1)S(1)}, u32[]{:S(2)}, u32[]{:S(2)}) %collective-permute-start.14) | collective-permute-done | bytes 294944 | tf_op jit(solution)/shard_map/ppermute | solution.py:1054
  86.4 8.3 %shard_map.208 = (f32[512,576]{1,0:T(8,128)S(1)}, f32[1,576]{1,0:T(1,128)S(1)}, bf16[9,512,128]{2,1,0:T(8,128)(2,1)S(1)}) custom-call(s32[5]{0:T(128)S(1)} %copy-done.5, bf16[512,576]{1,0:T(8,128)(2,1)S(1)} %bitcast.158, f32[512,576]{1,0:T(8,128)S(1)} %get-tuple-element.206.refs_5_.refs_2_, bf16[512,1536]{1,0:T(8,128)(2,1)S(1)} %get-tuple-element.217.refs_3_, ...), custom_call_target="tpu_custom_call" | custom-call | flops 2151677952 | bytes 18696468 | tf_op jit(solution)/shard_map/pallas_call | solution.py:87
  96.2 1.6 collective-permute-start.17
  97.8 1.5 collective-permute-start.15
  99.3 11.5 %shard_map.209 = (bf16[512,640]{1,0:T(8,128)(2,1)S(1)}, f32[4,128,384]{2,1,0:T(8,128)S(1)}, bf16[4,128,384]{2,1,0:T(8,128)(2,1)S(1)}) custom-call(s32[5]{0:T(128)S(1)} %copy-done.5, s32[2]{0:T(128)S(1)} %fusion.37.refs_1_.refs_5_, bf16[9,512,128]{2,1,0:T(8,128)(2,1)S(1)} %copy-done.12, bf16[9,512,128]{2,1,0:T(8,128)(2,1)S(1)} %get-tuple-element.224.refs_3_, ...), custom_call_target="tpu_custom_call" | custom-call | flops 7247757312 | bytes 5505052 | tf_op jit(solution)/shard_map/pallas_call | solution.py:87
  110.8 3.3 %collective-permute-done.17 = bf16[2,4,216,384]{3,2,1,0:T(8,128)(2,1)S(1)} collective-permute-done((bf16[2,4,216,384]{3,2,1,0:T(8,128)(2,1)S(1)}, bf16[2,4,216,384]{3,2,1,0:T(8,128)(2,1)S(1)}, u32[]{:S(2)}, u32[]{:S(2)}) %collective-permute-start.17) | collective-permute-done | bytes 1327136 | tf_op jit(solution)/shard_map/ppermute | solution.py:1026
  114.3 1.6 collective-permute-start.19
  115.9 1.7 collective-permute-done.18
  117.6 5.0 %shard_map.210 = (bf16[4,2,576,128]{3,2,1,0:T(8,128)(2,1)S(1)}, bf16[512,576]{1,0:T(8,128)(2,1)S(1)}, bf16[576,128]{1,0:T(8,128)(2,1)S(1)}, bf16[576,128]{1,0:T(...) custom-call(bf16[2,576,128]{2,1,0:T(8,128)(2,1)S(1)} %get-tuple-elem, ...), custom_call_target="tpu_custom_call" | custom-call | flops 1547698176 | bytes 10291476 | tf_op jit(solution)/shard_map/pallas_call | solution.py:87
  122.7 2.4 collective-permute-done.19
  126.0 1.6 collective-permute-start.24
  128.5 2.0 collective-permute-start.22
  130.5 9.6 %shard_map.212 = (bf16[512,1536]{1,0:T(8,128)(2,1)S(1)}, bf16[512,1536]{1,0:T(8,128)(2,1)S(1)}, bf16[2,2,4,216,384]{4,3,2,1,0:T(8,128)(2,1)S(1)}, bf16[2,2,4,216,384]{4,3,2,1,0:T(8,128)(2,1)S(1)}) custom-call(s32[5]{0:T(128)S(1)} %copy-done.5, bf16[512,576]{1,0:T(8,128)(2,1)S(1)} %get-tuple-element.248.refs_1_, f32[512,576]{1,0:T(8,128)S(1)} %get-tuple-element.249.refs_2_, ...), custom_call_target="tpu_custom_call" | custom-call | flops 3623878656 | bytes 19333140 | tf_op jit(solution)/shard_map/pallas_call | solution.py:87
  140.1 3.2 %collective-permute-done.23 = bf16[216,384]{1,0:T(8,128)(2,1)S(1)} collective-permute-done((bf16[216,384]{1,0:T(8,128)(2,1)S(1)}, bf16[216,384]{1,0:T(8,128)(2,1)S(1)}, u32[]{:S(2)}, u32[]{:S(2)}) %collective-permute-start.23) | collective-permute-done | bytes 165920 | tf_op jit(solution)/shard_map/ppermute | solution.py:1041
  144.6 1.6 collective-permute-start.28
  146.2 1.5 collective-permute-start.27
  148.3 1.5 collective-permute-start.25
  149.8 1.8 shard_map.211
  151.6 8.3 %shard_map.213 = (f32[512,576]{1,0:T(8,128)S(1)}, f32[1,576]{1,0:T(1,128)S(1)}, bf16[9,512,128]{2,1,0:T(8,128)(2,1)S(1)}) custom-call(s32[5]{0:T(128)S(1)} %copy-done.5, bf16[512,576]{1,0:T(8,128)(2,1)S(1)} %get-tuple-element.248.refs_1_, f32[512,576]{1,0:T(8,128)S(1)} %get-tuple-element.249.refs_2_, bf16[512,1536]{1,0:T(8,128)(2,1)S(1)} %get-tuple-element.258.refs_3_, ...), custom_call_target="tpu_custom_call" | custom-call | flops 2151677952 | bytes 18696468 | tf_op jit(solution)/shard_map/pallas_call | solution.py:87
  161.0 1.6 collective-permute-start.31
  163.6 1.6 collective-permute-start.30
  165.2 2.1 collective-permute-start.33
  167.3 2.2 collective-permute-start.34
  169.6 12.4 %shard_map.214 = (bf16[4,216,384]{2,1,0:T(8,128)(2,1)S(1)}, bf16[512,640]{1,0:T(8,128)(2,1)S(1)}, f32[4,128,384]{2,1,0:T(8,128)S(1)}, bf16[4,128,384]{2,1,0:T(8,128)(2,1)S(1)}) custom-call(bf16[216,384]{1,0:T(8,128)(2,1)S(1)} %add_convert_fusion.6.refs_0_, bf16[216,384]{1,0:T(8,128)(2,1)S(1)} %collective-permute-done.25.refs_1_, ...), custom_call_target="tpu_custom_call" | custom-call | flops 7247757312 | bytes 5505052 | tf_op jit(solution)/shard_map/pallas_call | solution.py:87
  183.3 1.3 collective-permute-start.40
  185.8 1.6 collective-permute-start.39
  187.5 2.8 %collective-permute-start.37 = (bf16[80,384]{1,0:T(8,128)(2,1)S(1)}, bf16[80,384]{1,0:T(8,128)(2,1)S(1)}, u32[]{:S(2)}, u32[]{:S(2)}) collective-permute-start(bf16[80,384]{1,0:T(8,128)(2,1)S(1)} %get-tuple-element.344), channel_id=1, source_target_pairs={{0,1},{1,0},{2,3},{3,2},{4,5},{5,4},{6,7},{7,6},{8,9},{9,8},{10,11... | collective-permute-start | bytes 184328 | tf_op jit(solution)/shard_map/ppermute | solution.py:1041
  190.3 6.8 %shard_map.215 = (bf16[4,576,128]{2,1,0:T(8,128)(2,1)S(1)}, bf16[512,576]{1,0:T(8,128)(2,1)}, bf16[576,128]{1,0:T(8,128)(2,1)S(1)}, bf16[576,128]{1,0:T(8,128)(2...) custom-call(bf16[576,128]{1,0:T(8,128)(2,1)S(1)} %get-tuple-element., ...), custom_call_target="tpu_custom_call" | custom-call | flops 1547698176 | bytes 10291476 | tf_op jit(solution)/shard_map/pallas_call | solution.py:87
  197.7 2.1 collective-permute-done.42
  199.9 1.6 collective-permute-start.43
  201.5 6.4 %collective-permute-done.41 = bf16[2,216,384]{2,1,0:T(8,128)(2,1)S(1)} collective-permute-done((bf16[2,216,384]{2,1,0:T(8,128)(2,1)S(1)}, bf16[2,216,384]{2,1,0:T(8,128)(2,1)S(1)}, u32[]{:S(2)}, u32[]{:S(2)}) %collective-permute-start.41) | collective-permute-done | bytes 331808 | tf_op jit(solution)/shard_map/ppermute | solution.py:1046
  210.0 8.3 %collective-permute-done.44 = bf16[1,216,384]{2,1,0:T(8,128)(2,1)S(1)} collective-permute-done((bf16[1,216,384]{2,1,0:T(8,128)(2,1)S(1)}, bf16[1,216,384]{2,1,0:T(8,128)(2,1)S(1)}, u32[]{:S(2)}, u32[]{:S(2)}) %collective-permute-start.44) | collective-permute-done | bytes 165920 | tf_op jit(solution)/shard_map/ppermute | solution.py:1046
  218.6 1.6 collective-permute-start.51
  220.2 1.8 collective-permute-start.50
  222.1 1.5 collective-permute-start.59
  223.6 1.5 collective-permute-start.58
  225.7 1.9 collective-permute-start.46
  227.9 2.3 collective-permute-done.59
  230.2 1.6 collective-permute-start.48
  232.0 1.5 collective-permute-start.54
  233.4 1.4 collective-permute-start.53
  235.6 4.8 %collective-permute-done.47.refs_3_ = bf16[576,128]{1,0:T(8,128)(2,1)S(1)} collective-permute-done((bf16[576,128]{1,0:T(8,128)(2,1)S(1)}, bf16[576,128]{1,0:T(8,128)(2,1)S(1)}, u32[]{:S(2)}, u32[]{:S(2)}) %collective-permute-start.47) | collective-permute-done | bytes 147488 | tf_op jit(solution)/shard_map/ppermute | solution.py:1054
  240.4 1.3 collective-permute-start.56
  241.7 1.3 collective-permute-start.60
  243.2 1.3 collective-permute-start.55
  244.5 1.3 collective-permute-start.61
  245.8 2.1 collective-permute-done.61.refs_6_
  247.8 3.0 %shard_map.217 = (f32[1,144,576]{2,1,0:T(8,128)}, f32[1,144,192]{2,1,0:T(8,128)}, f32[1,144,192]{2,1,0:T(8,128)}, f32[1,144,576]{2,1,0:T(8,128)}, f32[1,144,1536...) custom-call(s32[5]{0:T(128)S(1)} %copy-done.5, ...), custom_call_target="tpu_custom_call" | custom-call | bytes 7177364 | tf_op jit(solution)/shard_map/pallas_call | solution.py:87
  250.8 1.9 shard_map.216
  (151 shorter events, 24.1 us)
Async XLA Ops:
  1.3 27.6 %copy-start.1 = (bf16[1,576,576]{2,1,0:T(8,128)(2,1)S(1)}, bf16[1,576,576]{2,1,0:T(8,128)(2,1)}, u32[]{:S(2)}) copy-start(bf16[1,576,576]{2,1,0:T(8,128)(2,1)} %param.18) | copy-start | bytes 1990660
  5.6 24.8 %copy-start = (bf16[592,1024]{1,0:T(8,128)(2,1)S(1)}, bf16[592,1024]{1,0:T(8,128)(2,1)}, u32[]{:S(2)}) copy-start(bf16[592,1024]{1,0:T(8,128)(2,1)} %get-tuple-element.177.refs_5_.refs_16_.refs_10_.refs_12_.refs_7_) | copy-start | bytes 3637252
  5.6 14.8 %collective-permute-start.3 = (bf16[592,1024]{1,0:T(8,128)(2,1)}, bf16[592,1024]{1,0:T(8,128)(2,1)S(1)}, u32[]{:S(2)}, u32[]{:S(2)}) collective-permute-start(bf16[592,1024]{1,0:T(8,128)(2,1)} %get-tuple-element.177.refs_5_.refs_16_.refs_10_.refs_12_.refs_7_), channel_id=1, source_target_pairs={{0,16},{16,0},{1,17},{17,1},{2,18},{18,2},{3,19},{19,3},{4,20},{20... | collective-permute-start | bytes 3637256 | tf_op jit(solution)/shard_map/ppermute | solution.py:861
  6.1 10.5 %collective-permute-start = (bf16[592,128]{1,0:T(8,128)(2,1)}, bf16[592,128]{1,0:T(8,128)(2,1)S(1)}, u32[]{:S(2)}, u32[]{:S(2)}) collective-permute-start(bf16[592,128]{1,0:T(8,128)(2,1)} %get-tuple-element.174), channel_id=1, source_target_pairs={{0,1},{1,0},{2,3},{3,2},{4,5},{5,4},{6,7},{7,6},{8,9},{9,8},{10,11... | collective-permute-start | bytes 454664 | tf_op jit(solution)/shard_map/ppermute | solution.py:859
  8.8 10.4 %collective-permute-start.1 = (bf16[592,128]{1,0:T(8,128)(2,1)}, bf16[592,128]{1,0:T(8,128)(2,1)S(1)}, u32[]{:S(2)}, u32[]{:S(2)}) collective-permute-start(bf16[592,128]{1,0:T(8,128)(2,1)} %get-tuple-element.175), channel_id=1, source_target_pairs={{0,2},{1,3},{2,0},{3,1},{4,6},{5,7},{6,4},{7,5},{8,10},{9,11},{10,... | collective-permute-start | bytes 454664 | tf_op jit(solution)/shard_map/ppermute | solution.py:859
  19.9 16.1 %collective-permute-start.7 = (bf16[576,1536]{1,0:T(8,128)(2,1)}, bf16[576,1536]{1,0:T(8,128)(2,1)}, u32[]{:S(2)}, u32[]{:S(2)}) collective-permute-start(bf16[576,1536]{1,0:T(8,128)(2,1)} %bitcast.18.refs_12_.refs_8_.refs_5_), channel_id=1, source_target_pairs={{0,16},{16,0},{1,17},{17,1},{2,18},{18,2},{3,19},{19,3},{4,20},{20... | collective-permute-start | bytes 5308424 | tf_op jit(solution)/shard_map/ppermute | solution.py:865
  19.9 16.1 %collective-permute-start.6 = (bf16[576,1536]{1,0:T(8,128)(2,1)}, bf16[576,1536]{1,0:T(8,128)(2,1)}, u32[]{:S(2)}, u32[]{:S(2)}) collective-permute-start(bf16[576,1536]{1,0:T(8,128)(2,1)} %bitcast.16.refs_10_.refs_8_), channel_id=1, source_target_pairs={{0,16},{16,0},{1,17},{17,1},{2,18},{18,2},{3,19},{19,3},{4,20},{20... | collective-permute-start | bytes 5308424 | tf_op jit(solution)/shard_map/ppermute | solution.py:865
  20.4 15.6 %collective-permute-start.5 = (bf16[576,1536]{1,0:T(8,128)(2,1)}, bf16[576,1536]{1,0:T(8,128)(2,1)}, u32[]{:S(2)}, u32[]{:S(2)}) collective-permute-start(bf16[576,1536]{1,0:T(8,128)(2,1)} %bitcast.15.refs_8_.refs_6_), channel_id=1, source_target_pairs={{0,16},{16,0},{1,17},{17,1},{2,18},{18,2},{3,19},{19,3},{4,20},{20... | collective-permute-start | bytes 5308424 | tf_op jit(solution)/shard_map/ppermute | solution.py:865
  20.4 8.6 %collective-permute-start.2 = (bf16[592,128]{1,0:T(8,128)(2,1)}, bf16[592,128]{1,0:T(8,128)(2,1)}, u32[]{:S(2)}, u32[]{:S(2)}) collective-permute-start(bf16[592,128]{1,0:T(8,128)(2,1)} %get-tuple-element.176), channel_id=1, source_target_pairs={{0,3},{1,2},{2,1},{3,0},{4,7},{5,6},{6,5},{7,4},{8,11},{9,10},{10,... | collective-permute-start | bytes 454664 | tf_op jit(solution)/shard_map/ppermute | solution.py:859
  29.0 6.3 %collective-permute-start.8 = (bf16[576,576]{1,0:T(8,128)(2,1)S(1)}, bf16[576,576]{1,0:T(8,128)(2,1)S(1)}, u32[]{:S(2)}, u32[]{:S(2)}) collective-permute-start(bf16[576,576]{1,0:T(8,128)(2,1)S(1)} %bitcast.149), channel_id=1, source_target_pairs={{0,16},{16,0},{1,17},{17,1},{2,18},{18,2},{3,19},{19,3},{4,20},{20... | collective-permute-start | bytes 1990664 | tf_op jit(solution)/shard_map/ppermute | solution.py:865
  34.0 1.9 collective-permute-start.4
  52.1 4.8 %collective-permute-start.9 = (bf16[4,128,384]{2,1,0:T(8,128)(2,1)S(1)}, bf16[4,128,384]{2,1,0:T(8,128)(2,1)S(1)}, u32[]{:S(2)}, u32[]{:S(2)}) collective-permute-start(bf16[4,128,384]{2,1,0:T(8,128)(2,1)S(1)} %bitcast.168), channel_id=1, source_target_pairs={{0,16},{16,0},{1,17},{17,1},{2,18},{18,2},{3,19},{19,3},{4,20},{20... | collective-permute-start | bytes 1179656 | tf_op jit(solution)/shard_map/ppermute | solution.py:897
  52.5 18.3 %collective-permute-start.10 = (bf16[576,128]{1,0:T(8,128)(2,1)S(1)}, bf16[576,128]{1,0:T(8,128)(2,1)S(1)}, u32[]{:S(2)}, u32[]{:S(2)}) collective-permute-start(bf16[576,128]{1,0:T(8,128)(2,1)S(1)} %copy-done.21), channel_id=1, source_target_pairs={{0,1},{1,0},{2,3},{3,2},{4,5},{5,4},{6,7},{7,6},{8,9},{9,8},{10,11... | collective-permute-start | bytes 442376 | tf_op jit(solution)/shard_map/ppermute | solution.py:935
  54.3 16.5 %collective-permute-start.11 = (bf16[576,128]{1,0:T(8,128)(2,1)S(1)}, bf16[576,128]{1,0:T(8,128)(2,1)S(1)}, u32[]{:S(2)}, u32[]{:S(2)}) collective-permute-start(bf16[576,128]{1,0:T(8,128)(2,1)S(1)} %copy-done.20), channel_id=1, source_target_pairs={{0,2},{1,3},{2,0},{3,1},{4,6},{5,7},{6,4},{7,5},{8,10},{9,11},{10,... | collective-permute-start | bytes 442376 | tf_op jit(solution)/shard_map/ppermute | solution.py:935
  55.6 15.2 %collective-permute-start.12 = (bf16[576,128]{1,0:T(8,128)(2,1)S(1)}, bf16[576,128]{1,0:T(8,128)(2,1)S(1)}, u32[]{:S(2)}, u32[]{:S(2)}) collective-permute-start(bf16[576,128]{1,0:T(8,128)(2,1)S(1)} %copy-done.19), channel_id=1, source_target_pairs={{0,3},{1,2},{2,1},{3,0},{4,7},{5,6},{6,5},{7,4},{8,11},{9,10},{10,... | collective-permute-start | bytes 442376 | tf_op jit(solution)/shard_map/ppermute | solution.py:935
  70.8 15.6 %collective-permute-start.14 = (bf16[2,576,128]{2,1,0:T(8,128)(2,1)S(1)}, bf16[2,576,128]{2,1,0:T(8,128)(2,1)S(1)}, u32[]{:S(2)}, u32[]{:S(2)}) collective-permute-start(bf16[2,576,128]{2,1,0:T(8,128)(2,1)S(1)} %get-tuple-element.204), channel_id=1, source_target_pairs={{0,2},{1,3},{2,0},{3,1},{4,6},{5,7},{6,4},{7,5},{8,10},{9,11},{10,... | collective-permute-start | bytes 884744 | tf_op jit(solution)/shard_map/ppermute | solution.py:1054
  86.4 9.4 %collective-permute-start.16 = (bf16[2,2,4,216,384]{4,3,2,1,0:T(8,128)(2,1)S(1)}, bf16[2,2,4,216,384]{4,3,2,1,0:T(8,128)(2,1)S(1)}, u32[]{:S(2)}, u32[]{:S(2)}) collective-permute-start(bf16[2,2,4,216,384]{4,3,2,1,0:T(8,128)(2,1)S(1)} %get-tuple-element.223), channel_id=1, source_target_pairs={{0,16},{16,0},{1,17},{17,1},{2,18},{18,2},{3,19},{19,3},{4,20},{20... | collective-permute-start | bytes 7962632 | tf_op jit(solution)/shard_map/ppermute | solution.py:1020
  86.4 9.4 %collective-permute-start.13 = (bf16[2,576,128]{2,1,0:T(8,128)(2,1)S(1)}, bf16[2,576,128]{2,1,0:T(8,128)(2,1)S(1)}, u32[]{:S(2)}, u32[]{:S(2)}) collective-permute-start(bf16[2,576,128]{2,1,0:T(8,128)(2,1)S(1)} %get-tuple-element.203), channel_id=1, source_target_pairs={{0,1},{1,0},{2,3},{3,2},{4,5},{5,4},{6,7},{7,6},{8,9},{9,8},{10,11... | collective-permute-start | bytes 884744 | tf_op jit(solution)/shard_map/ppermute | solution.py:1054
  96.2 17.8 %collective-permute-start.17 = (bf16[2,4,216,384]{3,2,1,0:T(8,128)(2,1)S(1)}, bf16[2,4,216,384]{3,2,1,0:T(8,128)(2,1)S(1)}, u32[]{:S(2)}, u32[]{:S(2)}) collective-permute-start(bf16[2,4,216,384]{3,2,1,0:T(8,128)(2,1)S(1)} %fusion), channel_id=1, source_target_pairs={{0,4},{4,0},{8,12},{12,8},{16,24},{20,28},{24,16},{28,20},{1,5},{5... | collective-permute-start | bytes 3981320 | tf_op jit(solution)/shard_map/ppermute | solution.py:1026
  97.8 13.0 %collective-permute-start.15 = (bf16[2,576,128]{2,1,0:T(8,128)(2,1)S(1)}, bf16[2,576,128]{2,1,0:T(8,128)(2,1)S(1)}, u32[]{:S(2)}, u32[]{:S(2)}) collective-permute-start(bf16[2,576,128]{2,1,0:T(8,128)(2,1)S(1)} %get-tuple-element.205), channel_id=1, source_target_pairs={{0,3},{1,2},{2,1},{3,0},{4,7},{5,6},{6,5},{7,4},{8,11},{9,10},{10,... | collective-permute-start | bytes 884744 | tf_op jit(solution)/shard_map/ppermute | solution.py:1054
  114.3 10.7 %collective-permute-start.19 = (bf16[4,216,384]{2,1,0:T(8,128)(2,1)S(1)}, bf16[4,216,384]{2,1,0:T(8,128)(2,1)S(1)}, u32[]{:S(2)}, u32[]{:S(2)}) collective-permute-start(bf16[4,216,384]{2,1,0:T(8,128)(2,1)S(1)} %fusion.7), channel_id=1, source_target_pairs={{0,8},{4,12},{8,0},{12,4},{16,20},{20,16},{24,28},{28,24},{1,9},{5... | collective-permute-start | bytes 1990664 | tf_op jit(solution)/shard_map/ppermute | solution.py:1032
  115.9 1.7 collective-permute-start.18
  125.1 18.2 %collective-permute-start.20 = (bf16[4,2,576,128]{3,2,1,0:T(8,128)(2,1)S(1)}, bf16[4,2,576,128]{3,2,1,0:T(8,128)(2,1)S(1)}, u32[]{:S(2)}, u32[]{:S(2)}) collective-permute-start(bf16[4,2,576,128]{3,2,1,0:T(8,128)(2,1)S(1)} %get-tuple-element.244), channel_id=1, source_target_pairs={{0,16},{16,0},{1,17},{17,1},{2,18},{18,2},{3,19},{19,3},{4,20},{20... | collective-permute-start | bytes 3538952 | tf_op jit(solution)/shard_map/ppermute | solution.py:1020
  125.1 18.2 %collective-permute-start.21 = (bf16[2,2,4,80,384]{4,3,2,1,0:T(8,128)(2,1)S(1)}, bf16[2,2,4,80,384]{4,3,2,1,0:T(8,128)(2,1)}, u32[]{:S(2)}, u32[]{:S(2)}) collective-permute-start(bf16[2,2,4,80,384]{4,3,2,1,0:T(8,128)(2,1)S(1)} %get-tuple-element.256), channel_id=1, source_target_pairs={{0,16},{16,0},{1,17},{17,1},{2,18},{18,2},{3,19},{19,3},{4,20},{20... | collective-permute-start | bytes 2949128 | tf_op jit(solution)/shard_map/ppermute | solution.py:1020
  126.0 14.1 %collective-permute-start.24 = (bf16[216,384]{1,0:T(8,128)(2,1)S(1)}, bf16[216,384]{1,0:T(8,128)(2,1)S(1)}, u32[]{:S(2)}, u32[]{:S(2)}) collective-permute-start(bf16[216,384]{1,0:T(8,128)(2,1)S(1)} %get-tuple-element.335), channel_id=1, source_target_pairs={{0,3},{1,2},{2,1},{3,0},{4,7},{5,6},{6,5},{7,4},{8,11},{9,10},{10,... | collective-permute-start | bytes 497672 | tf_op jit(solution)/shard_map/ppermute | solution.py:1041
  127.6 15.7 %collective-permute-start.23 = (bf16[216,384]{1,0:T(8,128)(2,1)S(1)}, bf16[216,384]{1,0:T(8,128)(2,1)S(1)}, u32[]{:S(2)}, u32[]{:S(2)}) collective-permute-start(bf16[216,384]{1,0:T(8,128)(2,1)S(1)} %get-tuple-element.336), channel_id=1, source_target_pairs={{0,2},{1,3},{2,0},{3,1},{4,6},{5,7},{6,4},{7,5},{8,10},{9,11},{10,... | collective-permute-start | bytes 497672 | tf_op jit(solution)/shard_map/ppermute | solution.py:1041
  128.5 14.8 %collective-permute-start.22 = (bf16[216,384]{1,0:T(8,128)(2,1)S(1)}, bf16[216,384]{1,0:T(8,128)(2,1)S(1)}, u32[]{:S(2)}, u32[]{:S(2)}) collective-permute-start(bf16[216,384]{1,0:T(8,128)(2,1)S(1)} %get-tuple-element.337), channel_id=1, source_target_pairs={{0,1},{1,0},{2,3},{3,2},{4,5},{5,4},{6,7},{7,6},{8,9},{9,8},{10,11... | collective-permute-start | bytes 497672 | tf_op jit(solution)/shard_map/ppermute | solution.py:1041
  143.3 17.3 %collective-permute-start.29 = (bf16[2,2,4,216,384]{4,3,2,1,0:T(8,128)(2,1)S(1)}, bf16[2,2,4,216,384]{4,3,2,1,0:T(8,128)(2,1)S(1)}, u32[]{:S(2)}, u32[]{:S(2)}) collective-permute-start(bf16[2,2,4,216,384]{4,3,2,1,0:T(8,128)(2,1)S(1)} %get-tuple-element.267), channel_id=1, source_target_pairs={{0,16},{16,0},{1,17},{17,1},{2,18},{18,2},{3,19},{19,3},{4,20},{20... | collective-permute-start | bytes 7962632 | tf_op jit(solution)/shard_map/ppermute | solution.py:1020
  144.6 16.1 %collective-permute-start.28 = (bf16[2,4,80,384]{3,2,1,0:T(8,128)(2,1)S(1)}, bf16[2,4,80,384]{3,2,1,0:T(8,128)(2,1)S(1)}, u32[]{:S(2)}, u32[]{:S(2)}) collective-permute-start(bf16[2,4,80,384]{3,2,1,0:T(8,128)(2,1)S(1)} %fusion.8), channel_id=1, source_target_pairs={{0,4},{4,0},{8,12},{12,8},{16,24},{20,28},{24,16},{28,20},{1,5},{5... | collective-permute-start | bytes 1474568 | tf_op jit(solution)/shard_map/ppermute | solution.py:1026
  146.2 13.7 %collective-permute-start.27 = (bf16[216,384]{1,0:T(8,128)(2,1)S(1)}, bf16[216,384]{1,0:T(8,128)(2,1)S(1)}, u32[]{:S(2)}, u32[]{:S(2)}) collective-permute-start(bf16[216,384]{1,0:T(8,128)(2,1)S(1)} %add_convert_fusion.6.refs_0_), channel_id=1, source_target_pairs={{0,12},{4,8},{8,4},{12,0},{1,13},{5,9},{9,5},{13,1},{2,14},{6,10},... | collective-permute-start | bytes 497672 | tf_op jit(solution)/shard_map/ppermute | solution.py:1082
  147.8 12.2 %collective-permute-start.26 = (bf16[216,384]{1,0:T(8,128)(2,1)S(1)}, bf16[216,384]{1,0:T(8,128)(2,1)S(1)}, u32[]{:S(2)}, u32[]{:S(2)}) collective-permute-start(bf16[216,384]{1,0:T(8,128)(2,1)S(1)} %add_convert_fusion.6.refs_0_), channel_id=1, source_target_pairs={{0,8},{4,12},{8,0},{12,4},{1,9},{5,13},{9,1},{13,5},{2,10},{6,14},... | collective-permute-start | bytes 497672 | tf_op jit(solution)/shard_map/ppermute | solution.py:1082
  148.3 12.3 %collective-permute-start.25 = (bf16[216,384]{1,0:T(8,128)(2,1)S(1)}, bf16[216,384]{1,0:T(8,128)(2,1)S(1)}, u32[]{:S(2)}, u32[]{:S(2)}) collective-permute-start(bf16[216,384]{1,0:T(8,128)(2,1)S(1)} %add_convert_fusion.6.refs_0_), channel_id=1, source_target_pairs={{0,4},{4,0},{8,12},{12,8},{1,5},{5,1},{9,13},{13,9},{2,6},{6,2},{1... | collective-permute-start | bytes 497672 | tf_op jit(solution)/shard_map/ppermute | solution.py:1082
  161.0 21.0 %collective-permute-start.31 = (bf16[2,4,216,384]{3,2,1,0:T(8,128)(2,1)S(1)}, bf16[2,4,216,384]{3,2,1,0:T(8,128)(2,1)S(1)}, u32[]{:S(2)}, u32[]{:S(2)}) collective-permute-start(bf16[2,4,216,384]{3,2,1,0:T(8,128)(2,1)S(1)} %fusion.1), channel_id=1, source_target_pairs={{0,4},{4,0},{8,12},{12,8},{16,24},{20,28},{24,16},{28,20},{1,5},{5... | collective-permute-start | bytes 3981320 | tf_op jit(solution)/shard_map/ppermute | solution.py:1026
  163.6 18.4 %collective-permute-start.30 = (bf16[4,80,384]{2,1,0:T(8,128)(2,1)S(1)}, bf16[4,80,384]{2,1,0:T(8,128)(2,1)S(1)}, u32[]{:S(2)}, u32[]{:S(2)}) collective-permute-start(bf16[4,80,384]{2,1,0:T(8,128)(2,1)S(1)} %fusion.15), channel_id=1, source_target_pairs={{0,8},{4,12},{8,0},{12,4},{16,20},{20,16},{24,28},{28,24},{1,9},{5... | collective-permute-start | bytes 737288 | tf_op jit(solution)/shard_map/ppermute | solution.py:1032
  165.2 16.8 %collective-permute-start.32 = (bf16[576,128]{1,0:T(8,128)(2,1)S(1)}, bf16[576,128]{1,0:T(8,128)(2,1)S(1)}, u32[]{:S(2)}, u32[]{:S(2)}) collective-permute-start(bf16[576,128]{1,0:T(8,128)(2,1)S(1)} %get-tuple-element.283), channel_id=1, source_target_pairs={{0,1},{1,0},{2,3},{3,2},{4,5},{5,4},{6,7},{7,6},{8,9},{9,8},{10,11... | collective-permute-start | bytes 442376 | tf_op jit(solution)/shard_map/ppermute | solution.py:1054
  165.2 16.8 %collective-permute-start.33 = (bf16[576,128]{1,0:T(8,128)(2,1)S(1)}, bf16[576,128]{1,0:T(8,128)(2,1)S(1)}, u32[]{:S(2)}, u32[]{:S(2)}) collective-permute-start(bf16[576,128]{1,0:T(8,128)(2,1)S(1)} %get-tuple-element.284), channel_id=1, source_target_pairs={{0,2},{1,3},{2,0},{3,1},{4,6},{5,7},{6,4},{7,5},{8,10},{9,11},{10,... | collective-permute-start | bytes 442376 | tf_op jit(solution)/shard_map/ppermute | solution.py:1054
  167.3 14.6 %collective-permute-start.34 = (bf16[576,128]{1,0:T(8,128)(2,1)S(1)}, bf16[576,128]{1,0:T(8,128)(2,1)S(1)}, u32[]{:S(2)}, u32[]{:S(2)}) collective-permute-start(bf16[576,128]{1,0:T(8,128)(2,1)S(1)} %get-tuple-element.285), channel_id=1, source_target_pairs={{0,3},{1,2},{2,1},{3,0},{4,7},{5,6},{6,5},{7,4},{8,11},{9,10},{10,... | collective-permute-start | bytes 442376 | tf_op jit(solution)/shard_map/ppermute | solution.py:1054
  182.3 14.9 %collective-permute-start.36 = (bf16[4,216,384]{2,1,0:T(8,128)(2,1)S(1)}, bf16[4,216,384]{2,1,0:T(8,128)(2,1)S(1)}, u32[]{:S(2)}, u32[]{:S(2)}) collective-permute-start(bf16[4,216,384]{2,1,0:T(8,128)(2,1)S(1)} %fusion.4), channel_id=1, source_target_pairs={{0,8},{4,12},{8,0},{12,4},{16,20},{20,16},{24,28},{28,24},{1,9},{5... | collective-permute-start | bytes 1990664 | tf_op jit(solution)/shard_map/ppermute | solution.py:1032
  183.3 13.8 %collective-permute-start.40 = (bf16[4,216,384]{2,1,0:T(8,128)(2,1)S(1)}, bf16[4,216,384]{2,1,0:T(8,128)(2,1)S(1)}, u32[]{:S(2)}, u32[]{:S(2)}) collective-permute-start(bf16[4,216,384]{2,1,0:T(8,128)(2,1)S(1)} %get-tuple-element.300.refs_4_), channel_id=1, source_target_pairs={{0,16},{1,17},{2,18},{3,19},{4,20},{5,21},{6,22},{7,23},{8,24},{9,... | collective-permute-start | bytes 1990664 | tf_op jit(solution)/shard_map/ppermute | solution.py:1132
  184.6 2.8 %collective-permute-start.35 = (bf16[4,128,384]{2,1,0:T(8,128)(2,1)S(1)}, bf16[4,128,384]{2,1,0:T(8,128)(2,1)S(1)}, u32[]{:S(2)}, u32[]{:S(2)}) collective-permute-start(bf16[4,128,384]{2,1,0:T(8,128)(2,1)S(1)} %get-tuple-element.291), channel_id=1, source_target_pairs={{0,16},{16,0},{1,17},{17,1},{2,18},{18,2},{3,19},{19,3},{4,20},{20... | collective-permute-start | bytes 1179656 | tf_op jit(solution)/shard_map/ppermute | solution.py:985
  185.8 11.3 %collective-permute-start.39 = (bf16[80,384]{1,0:T(8,128)(2,1)S(1)}, bf16[80,384]{1,0:T(8,128)(2,1)S(1)}, u32[]{:S(2)}, u32[]{:S(2)}) collective-permute-start(bf16[80,384]{1,0:T(8,128)(2,1)S(1)} %get-tuple-element.342), channel_id=1, source_target_pairs={{0,3},{1,2},{2,1},{3,0},{4,7},{5,6},{6,5},{7,4},{8,11},{9,10},{10,... | collective-permute-start | bytes 184328 | tf_op jit(solution)/shard_map/ppermute | solution.py:1041
  187.5 9.6 %collective-permute-start.38 = (bf16[80,384]{1,0:T(8,128)(2,1)S(1)}, bf16[80,384]{1,0:T(8,128)(2,1)S(1)}, u32[]{:S(2)}, u32[]{:S(2)}) collective-permute-start(bf16[80,384]{1,0:T(8,128)(2,1)S(1)} %get-tuple-element.343), channel_id=1, source_target_pairs={{0,2},{1,3},{2,0},{3,1},{4,6},{5,7},{6,4},{7,5},{8,10},{9,11},{10,... | collective-permute-start | bytes 184328 | tf_op jit(solution)/shard_map/ppermute | solution.py:1041
  187.5 9.6 %collective-permute-start.37 = (bf16[80,384]{1,0:T(8,128)(2,1)S(1)}, bf16[80,384]{1,0:T(8,128)(2,1)S(1)}, u32[]{:S(2)}, u32[]{:S(2)}) collective-permute-start(bf16[80,384]{1,0:T(8,128)(2,1)S(1)} %get-tuple-element.344), channel_id=1, source_target_pairs={{0,1},{1,0},{2,3},{3,2},{4,5},{5,4},{6,7},{7,6},{8,9},{9,8},{10,11... | collective-permute-start | bytes 184328 | tf_op jit(solution)/shard_map/ppermute | solution.py:1041
  197.1 2.6 %collective-permute-start.42 = (bf16[2,2,4,80,384]{4,3,2,1,0:T(8,128)(2,1)S(1)}, bf16[2,2,4,80,384]{4,3,2,1,0:T(8,128)(2,1)S(1)}, u32[]{:S(2)}, u32[]{:S(2)}) collective-permute-start(bf16[2,2,4,80,384]{4,3,2,1,0:T(8,128)(2,1)S(1)} %get-tuple-element.309), channel_id=1, source_target_pairs={{0,16},{16,0},{1,17},{17,1},{2,18},{18,2},{3,19},{19,3},{4,20},{20... | collective-permute-start | bytes 2949128 | tf_op jit(solution)/shard_map/ppermute | solution.py:1020
  197.6 10.3 %collective-permute-start.41 = (bf16[2,216,384]{2,1,0:T(8,128)(2,1)S(1)}, bf16[2,216,384]{2,1,0:T(8,128)(2,1)S(1)}, u32[]{:S(2)}, u32[]{:S(2)}) collective-permute-start(bf16[2,216,384]{2,1,0:T(8,128)(2,1)S(1)} %slice.234), channel_id=1, source_target_pairs={{0,1},{1,0},{2,3},{3,2},{4,5},{5,4},{6,7},{7,6},{8,9},{9,8},{10,11... | collective-permute-start | bytes 995336 | tf_op jit(solution)/shard_map/ppermute | solution.py:1046
  199.9 8.9 %collective-permute-start.43 = (bf16[2,4,80,384]{3,2,1,0:T(8,128)(2,1)S(1)}, bf16[2,4,80,384]{3,2,1,0:T(8,128)(2,1)S(1)}, u32[]{:S(2)}, u32[]{:S(2)}) collective-permute-start(bf16[2,4,80,384]{3,2,1,0:T(8,128)(2,1)S(1)} %fusion.9), channel_id=1, source_target_pairs={{0,4},{4,0},{8,12},{12,8},{16,24},{20,28},{24,16},{28,20},{1,5},{5... | collective-permute-start | bytes 1474568 | tf_op jit(solution)/shard_map/ppermute | solution.py:1026
  208.0 10.3 %collective-permute-start.44 = (bf16[1,216,384]{2,1,0:T(8,128)(2,1)S(1)}, bf16[1,216,384]{2,1,0:T(8,128)(2,1)S(1)}, u32[]{:S(2)}, u32[]{:S(2)}) collective-permute-start(bf16[1,216,384]{2,1,0:T(8,128)(2,1)S(1)} %slice.238), channel_id=1, source_target_pairs={{0,2},{1,3},{2,0},{3,1},{4,6},{5,7},{6,4},{7,5},{8,10},{9,11},{10,... | collective-permute-start | bytes 497672 | tf_op jit(solution)/shard_map/ppermute | solution.py:1046
  208.9 9.4 %collective-permute-start.45 = (bf16[4,80,384]{2,1,0:T(8,128)(2,1)S(1)}, bf16[4,80,384]{2,1,0:T(8,128)(2,1)S(1)}, u32[]{:S(2)}, u32[]{:S(2)}) collective-permute-start(bf16[4,80,384]{2,1,0:T(8,128)(2,1)S(1)} %fusion.10), channel_id=1, source_target_pairs={{0,8},{4,12},{8,0},{12,4},{16,20},{20,16},{24,28},{28,24},{1,9},{5... | collective-permute-start | bytes 737288 | tf_op jit(solution)/shard_map/ppermute | solution.py:1032
  218.5 6.6 %collective-permute-start.49 = (bf16[80,384]{1,0:T(8,128)(2,1)S(1)}, bf16[80,384]{1,0:T(8,128)(2,1)S(1)}, u32[]{:S(2)}, u32[]{:S(2)}) collective-permute-start(bf16[80,384]{1,0:T(8,128)(2,1)S(1)} %get-tuple-element.339), channel_id=1, source_target_pairs={{0,1},{1,0},{2,3},{3,2},{4,5},{5,4},{6,7},{7,6},{8,9},{9,8},{10,11... | collective-permute-start | bytes 184328 | tf_op jit(solution)/shard_map/ppermute | solution.py:1041
  218.6 7.1 %collective-permute-start.51 = (bf16[80,384]{1,0:T(8,128)(2,1)S(1)}, bf16[80,384]{1,0:T(8,128)(2,1)S(1)}, u32[]{:S(2)}, u32[]{:S(2)}) collective-permute-start(bf16[80,384]{1,0:T(8,128)(2,1)S(1)} %get-tuple-element.340), channel_id=1, source_target_pairs={{0,3},{1,2},{2,1},{3,0},{4,7},{5,6},{6,5},{7,4},{8,11},{9,10},{10,... | collective-permute-start | bytes 184328 | tf_op jit(solution)/shard_map/ppermute | solution.py:1041
  220.2 7.5 %collective-permute-start.50 = (bf16[80,384]{1,0:T(8,128)(2,1)S(1)}, bf16[80,384]{1,0:T(8,128)(2,1)S(1)}, u32[]{:S(2)}, u32[]{:S(2)}) collective-permute-start(bf16[80,384]{1,0:T(8,128)(2,1)S(1)} %get-tuple-element.341), channel_id=1, source_target_pairs={{0,2},{1,3},{2,0},{3,1},{4,6},{5,7},{6,4},{7,5},{8,10},{9,11},{10,... | collective-permute-start | bytes 184328 | tf_op jit(solution)/shard_map/ppermute | solution.py:1041
  222.1 8.1 %collective-permute-start.59 = (bf16[216,384]{1,0:T(8,128)(2,1)S(1)}, bf16[216,384]{1,0:T(8,128)(2,1)S(1)}, u32[]{:S(2)}, u32[]{:S(2)}) collective-permute-start(bf16[216,384]{1,0:T(8,128)(2,1)S(1)} %fusion.16), channel_id=1, source_target_pairs={{0,12},{4,8},{8,4},{12,0},{1,13},{5,9},{9,5},{13,1},{2,14},{6,10},... | collective-permute-start | bytes 497672 | tf_op jit(solution)/shard_map/ppermute | solution.py:1082
  223.6 8.3 %collective-permute-start.58 = (bf16[216,384]{1,0:T(8,128)(2,1)S(1)}, bf16[216,384]{1,0:T(8,128)(2,1)S(1)}, u32[]{:S(2)}, u32[]{:S(2)}) collective-permute-start(bf16[216,384]{1,0:T(8,128)(2,1)S(1)} %fusion.16), channel_id=1, source_target_pairs={{0,8},{4,12},{8,0},{12,4},{1,9},{5,13},{9,1},{13,5},{2,10},{6,14},... | collective-permute-start | bytes 497672 | tf_op jit(solution)/shard_map/ppermute | solution.py:1082
  225.1 8.3 %collective-permute-start.57 = (bf16[216,384]{1,0:T(8,128)(2,1)S(1)}, bf16[216,384]{1,0:T(8,128)(2,1)S(1)}, u32[]{:S(2)}, u32[]{:S(2)}) collective-permute-start(bf16[216,384]{1,0:T(8,128)(2,1)S(1)} %fusion.16), channel_id=1, source_target_pairs={{0,4},{4,0},{8,12},{12,8},{1,5},{5,1},{9,13},{13,9},{2,6},{6,2},{1... | collective-permute-start | bytes 497672 | tf_op jit(solution)/shard_map/ppermute | solution.py:1082
  225.7 9.2 %collective-permute-start.46 = (bf16[576,128]{1,0:T(8,128)(2,1)S(1)}, bf16[576,128]{1,0:T(8,128)(2,1)S(1)}, u32[]{:S(2)}, u32[]{:S(2)}) collective-permute-start(bf16[576,128]{1,0:T(8,128)(2,1)S(1)} %get-tuple-element.313), channel_id=1, source_target_pairs={{0,1},{1,0},{2,3},{3,2},{4,5},{5,4},{6,7},{7,6},{8,9},{9,8},{10,11... | collective-permute-start | bytes 442376 | tf_op jit(solution)/shard_map/ppermute | solution.py:1054
  227.8 12.6 %collective-permute-start.47 = (bf16[576,128]{1,0:T(8,128)(2,1)S(1)}, bf16[576,128]{1,0:T(8,128)(2,1)S(1)}, u32[]{:S(2)}, u32[]{:S(2)}) collective-permute-start(bf16[576,128]{1,0:T(8,128)(2,1)S(1)} %get-tuple-element.314), channel_id=1, source_target_pairs={{0,2},{1,3},{2,0},{3,1},{4,6},{5,7},{6,4},{7,5},{8,10},{9,11},{10,... | collective-permute-start | bytes 442376 | tf_op jit(solution)/shard_map/ppermute | solution.py:1054
  230.2 11.5 %collective-permute-start.48 = (bf16[576,128]{1,0:T(8,128)(2,1)S(1)}, bf16[576,128]{1,0:T(8,128)(2,1)S(1)}, u32[]{:S(2)}, u32[]{:S(2)}) collective-permute-start(bf16[576,128]{1,0:T(8,128)(2,1)S(1)} %get-tuple-element.315), channel_id=1, source_target_pairs={{0,3},{1,2},{2,1},{3,0},{4,7},{5,6},{6,5},{7,4},{8,11},{9,10},{10,... | collective-permute-start | bytes 442376 | tf_op jit(solution)/shard_map/ppermute | solution.py:1054
  232.0 11.1 %collective-permute-start.54 = (bf16[2,80,384]{2,1,0:T(8,128)(2,1)S(1)}, bf16[2,80,384]{2,1,0:T(8,128)(2,1)S(1)}, u32[]{:S(2)}, u32[]{:S(2)}) collective-permute-start(bf16[2,80,384]{2,1,0:T(8,128)(2,1)S(1)} %get-tuple-element.346), channel_id=1, source_target_pairs={{0,12},{4,8},{8,4},{12,0},{1,13},{5,9},{9,5},{13,1},{2,14},{6,10},... | collective-permute-start | bytes 368648 | tf_op jit(solution)/shard_map/ppermute | solution.py:1082
  233.4 9.6 %collective-permute-start.53 = (bf16[2,80,384]{2,1,0:T(8,128)(2,1)S(1)}, bf16[2,80,384]{2,1,0:T(8,128)(2,1)S(1)}, u32[]{:S(2)}, u32[]{:S(2)}) collective-permute-start(bf16[2,80,384]{2,1,0:T(8,128)(2,1)S(1)} %get-tuple-element.346), channel_id=1, source_target_pairs={{0,8},{4,12},{8,0},{12,4},{1,9},{5,13},{9,1},{13,5},{2,10},{6,14},... | collective-permute-start | bytes 368648 | tf_op jit(solution)/shard_map/ppermute | solution.py:1082
  234.8 8.2 %collective-permute-start.52 = (bf16[2,80,384]{2,1,0:T(8,128)(2,1)S(1)}, bf16[2,80,384]{2,1,0:T(8,128)(2,1)S(1)}, u32[]{:S(2)}, u32[]{:S(2)}) collective-permute-start(bf16[2,80,384]{2,1,0:T(8,128)(2,1)S(1)} %get-tuple-element.346), channel_id=1, source_target_pairs={{0,4},{4,0},{8,12},{12,8},{1,5},{5,1},{9,13},{13,9},{2,6},{6,2},{1... | collective-permute-start | bytes 368648 | tf_op jit(solution)/shard_map/ppermute | solution.py:1082
  240.4 10.4 %collective-permute-start.56 = (bf16[4,576,128]{2,1,0:T(8,128)(2,1)S(1)}, bf16[4,576,128]{2,1,0:T(8,128)(2,1)S(1)}, u32[]{:S(2)}, u32[]{:S(2)}) collective-permute-start(bf16[4,576,128]{2,1,0:T(8,128)(2,1)S(1)} %get-tuple-element.321), channel_id=1, source_target_pairs={{0,16},{1,17},{2,18},{3,19},{4,20},{5,21},{6,22},{7,23},{8,24},{9,... | collective-permute-start | bytes 1769480 | tf_op jit(solution)/shard_map/ppermute | solution.py:1163
  241.7 6.1 %collective-permute-start.60 = (bf16[4,216,384]{2,1,0:T(8,128)(2,1)S(1)}, bf16[4,216,384]{2,1,0:T(8,128)(2,1)S(1)}, u32[]{:S(2)}, u32[]{:S(2)}) collective-permute-start(bf16[4,216,384]{2,1,0:T(8,128)(2,1)S(1)} %pad_maximum_fusion.refs_1_), channel_id=1, source_target_pairs={{16,0},{17,1},{18,2},{19,3},{20,4},{21,5},{22,6},{23,7},{24,8},{25... | collective-permute-start | bytes 1990664 | tf_op jit(solution)/shard_map/ppermute | solution.py:1169
  243.2 7.6 %collective-permute-start.55 = (bf16[4,576,128]{2,1,0:T(8,128)(2,1)S(1)}, bf16[4,576,128]{2,1,0:T(8,128)(2,1)S(1)}, u32[]{:S(2)}, u32[]{:S(2)}) collective-permute-start(bf16[4,576,128]{2,1,0:T(8,128)(2,1)S(1)} %pad_maximum_fusion.1), channel_id=1, source_target_pairs={{16,0},{17,1},{18,2},{19,3},{20,4},{21,5},{22,6},{23,7},{24,8},{25... | collective-permute-start | bytes 1769480 | tf_op jit(solution)/shard_map/ppermute | solution.py:1173
  244.5 3.3 %collective-permute-start.61 = (bf16[4,2,80,384]{3,2,1,0:T(8,128)(2,1)S(1)}, bf16[4,2,80,384]{3,2,1,0:T(8,128)(2,1)S(1)}, u32[]{:S(2)}, u32[]{:S(2)}) collective-permute-start(bf16[4,2,80,384]{3,2,1,0:T(8,128)(2,1)S(1)} %pad_maximum_fusion.2.refs_5_), channel_id=1, source_target_pairs={{0,16},{16,0},{1,17},{17,1},{2,18},{18,2},{3,19},{19,3},{4,20},{20... | collective-permute-start | bytes 1474568 | tf_op jit(solution)/shard_map/ppermute | solution.py:1020
  (20 other events, 218.0 us)
where the time goes:
time: 258 us; the launch traced here: 253 us
  Pallas kernels  112 us (43%)
  starting transfers between devices  66.7 us (26%)
  waiting for transfers between devices  59.2 us (23%)
  other arithmetic  8.29 us (3%)
  local copies, waits for them, and re-layouts  4.93 us (2%)
    pallas_call x15, Pallas kernels, call(): pl.pallas_call(strip, out_shape=tuple(piles) + tuple(outs), in_specs=[ANY...  112 us
    ppermute x2, waiting for transfers between devices, halve(): got = lax.ppermute(total[count:], 'seq', turn(step))  14.7 us
    ppermute x3, waiting for transfers between devices, on_device(): lax.ppermute(packets[step], 'seq', turn(step))  13.9 us
    ppermute x9, starting transfers between devices, to_seq(): lax.ppermute(total[spot], 'seq', turn(step))  12.5 us
    ppermute x9, waiting for transfers between devices, to_rows(): lax.ppermute(blocks[step], 'seq', turn(step))  11.4 us
    ppermute x9, starting transfers between devices, to_all(): lax.ppermute(piece, 'row', [(r, r ^ step) for r in range(4)])  10.6 us
    ppermute x9, starting transfers between devices, to_rows(): lax.ppermute(blocks[step], 'seq', turn(step))  10.3 us
    ppermute x3, starting transfers between devices, on_device(): lax.ppermute(packets[step], 'seq', turn(step))  7.71 us
  transfers between devices with their start and end apart: 62, of which 20 were waited for; matrix products, arithmetic and copies ran while one was open for 3% of the time, Pallas kernels for 36%

commit v1 on v0

--- a/solution.py
+++ b/solution.py
@@ -23,7 +23,7 @@
 ROW_STEP = 256
 KEY_STEP = 256
 SCALE = HD**-0.5
-SPARE = 8 * 1024 * 1024
+SPARE = 4 * 1024 * 1024
 EPSILON = 1e-05
 MASKED = -1e30
 F32 = jnp.float32
@@ -60,7 +60,7 @@
     return size
 
 
-def call(body, ins, specs, outs, scratch, flops, stack=(), room=None):
+def call(body, ins, specs, outs, scratch, flops, stack=(), room=None, light=False, far=()):
     moved = sum(a.size * a.dtype.itemsize for a in list(ins) + list(outs))
     inner, piled = len(ins), len(stack)
     held = [a for a, spec in zip(ins, specs) if spec is VMEM] + list(outs) + list(scratch)
@@ -86,13 +86,17 @@
 
     return pl.pallas_call(
         strip,
-        out_shape=tuple(piles) + tuple(outs),
+        out_shape=tuple(piles) + tuple(
+            pltpu.HBM(a.shape, a.dtype) if i in far else a for i, a in enumerate(outs)
+        ),
         in_specs=[ANY] * piled + list(specs),
-        out_specs=tuple([VMEM] * (len(piles) + len(outs))),
+        out_specs=tuple([VMEM] * len(piles) + [ANY if i in far else VMEM for i in range(len(outs))]),
         scratch_shapes=list(scratch) + [pltpu.SemaphoreType.DMA((piled,))] * len(piles),
         compiler_params=pltpu.CompilerParams(vmem_limit_bytes=min(room, 56 * 1024 * 1024)),
         cost_estimate=pl.CostEstimate(
-            flops=int(flops), bytes_accessed=int(moved), transcendentals=0
+            flops=0 if light else int(flops),
+            bytes_accessed=0 if light else int(moved),
+            transcendentals=0,
         ),
     )(*stack, *ins)
 
@@ -229,72 +233,108 @@
     return [(0, rows * half, chips * rows * tokens)]
 
 
+def ahead(tasks, first, second):
+    ready = first(*tasks[0])
+    for number, task in enumerate(tasks):
+        following = first(*tasks[number + 1]) if number + 1 < len(tasks) else None
+        second(*task, ready)
+        ready = following
+
+
 def attend(geometry, core, wagon, docs, q_ref, kz, vz, heads_out, q_out):
     rows, tokens, _ = geometry
-    for start, count, keys in query_blocks(geometry):
-        place = places(core, wagon, rows, tokens, start, (count, 1), 0)
-        key_place = lane_of((1, keys))
-        allowed = (key_place <= place) & (key_place >= opening(place, docs))
-        bias = jnp.where(allowed, 0.0, MASKED)
+    biases = {}
+
+    def rows_of(ref, start, count, group):
+        heads = slice(group * GROUPS, (group + 1) * GROUPS)
+        return ref[heads, start : start + count, :].reshape(GROUPS * count, LANES)
+
+    def scores_of(start, count, keys, group):
+        if start not in biases:
+            place = places(core, wagon, rows, tokens, start, (count, 1), 0)
+            key_place = lane_of((1, keys))
+            allowed = (key_place <= place) & (key_place >= opening(place, docs))
+            biases[start] = jnp.where(allowed, 0.0, MASKED)
+        scores = mm_nt(rows_of(q_ref, start, count, group), key_rows(kz, group, 0, keys))
+        scores = scores.reshape(GROUPS, count, keys) + biases[start][None]
+        return scores.reshape(GROUPS * count, keys)
+
+    def finish(start, count, keys, group, scores):
+        heads = slice(group * GROUPS, (group + 1) * GROUPS)
         low = low_half((GROUPS * count, LANES))
         lane = lane_of((GROUPS * count, LANES))
-        for group in range(KVH):
-            heads = slice(group * GROUPS, (group + 1) * GROUPS)
-            q = q_ref[heads, start : start + count, :].reshape(GROUPS * count, LANES)
-            scores = mm_nt(q, key_rows(kz, group, 0, keys))
-            scores = scores.reshape(GROUPS, count, keys) + bias[None]
-            scores = scores.reshape(GROUPS * count, keys)
-            top = jnp.max(scores, -1, keepdims=True)
-            weights = jnp.exp(scores - top).astype(BF16)
-            out = mm(weights, key_rows(vz, group, 0, keys))
-            total = jnp.where(low, 1.0, out)
-            lse = -(top + jnp.log(total))
-            high = lse.astype(BF16).astype(F32)
-            rest = lse - high
-            middle = rest.astype(BF16).astype(F32)
-            tail = jnp.where(
-                lane == HD,
-                high,
-                jnp.where(lane == HD + 1, middle, jnp.where(lane == HD + 2, rest - middle, 0.0)),
-            )
-            q_aug = jnp.where(low, q.astype(F32), tail).astype(BF16)
-            q_out[heads, start : start + count, :] = q_aug.reshape(GROUPS, count, LANES)
-            out = jnp.where(low, out / jnp.where(low, roll(out, HD), 1.0), 0.0)
-            heads_out[heads, start : start + count, :] = out.reshape(GROUPS, count, LANES)
+        top = jnp.max(scores, -1, keepdims=True)
+        weights = jnp.exp(scores - top).astype(BF16)
+        out = mm(weights, key_rows(vz, group, 0, keys))
+        total = jnp.where(low, 1.0, out)
+        lse = -(top + jnp.log(total))
+        high = lse.astype(BF16).astype(F32)
+        rest = lse - high
+        middle = rest.astype(BF16).astype(F32)
+        tail = jnp.where(
+            lane == HD,
+            high,
+            jnp.where(lane == HD + 1, middle, jnp.where(lane == HD + 2, rest - middle, 0.0)),
+        )
+        q = rows_of(q_ref, start, count, group).astype(F32)
+        q_aug = jnp.where(low, q, tail).astype(BF16)
+        q_out[heads, start : start + count, :] = q_aug.reshape(GROUPS, count, LANES)
+        out = jnp.where(low, out / jnp.where(low, roll(out, HD), 1.0), 0.0)
+        heads_out[heads, start : start + count, :] = out.reshape(GROUPS, count, LANES)
+
+    blocks = query_blocks(geometry)
+    ahead([(*block, group) for block in blocks for group in range(KVH)], scores_of, finish)
 
 
 def attend_back(geometry, core, wagon, docs, q_ref, do_ref, kz, vz, dq, dk, dv):
     rows, tokens, _ = geometry
-    span = tokens
+    span, half = tokens, tokens // 2
     dk[...] = jnp.zeros_like(dk)
     dv[...] = jnp.zeros_like(dv)
-    for start, count, keys in query_blocks(geometry):
-        width = GROUPS * count
-        lane = lane_of((1, width)) % count
-        half = tokens // 2
-        local = lane + start
-        place = (wagon * rows + local // half) * tokens + core * half + local % half
-        first = opening(place, docs)
-        for key_start, key_count in tiles_of(keys, KEY_STEP):
+    masks = {}
+
+    def rows_of(ref, start, count, group):
+        heads = slice(group * GROUPS, (group + 1) * GROUPS)
+        return ref[heads, start : start + count, :].reshape(GROUPS * count, LANES)
+
+    def products(start, count, key_start, key_count, group):
+        if (start, key_start) not in masks:
+            local = lane_of((1, GROUPS * count)) % count + start
+            place = (wagon * rows + local // half) * tokens + core * half + local % half
             key_place = key_start + lax.broadcasted_iota(jnp.int32, (key_count, 1), 0)
-            allowed = (key_place <= place) & (key_place >= first)
-            blocks = slice(key_start // span, (key_start + key_count) // span)
-            for group in range(KVH):
-                heads = slice(group * GROUPS, (group + 1) * GROUPS)
-                q = q_ref[heads, start : start + count, :].reshape(width, LANES)
-                do = do_ref[heads, start : start + count, :].reshape(width, LANES)
-                k = key_rows(kz, group, key_start, key_count)
-                v = key_rows(vz, group, key_start, key_count)
-                probs = jnp.where(allowed, jnp.exp(mm_nt(k, q)), 0.0)
-                slopes = (probs * mm_nt(v, do)).astype(BF16)
-                part = (key_count // span, 2, half, LANES)
-                dv[group, blocks] += mm(probs.astype(BF16), do).reshape(part)
-                dk[group, blocks] += mm(slopes, q).reshape(part)
-                back = mm_tn(slopes, k).reshape(GROUPS, count, LANES)
-                if key_start == 0:
-                    dq[heads, start : start + count, :] = back
-                else:
-                    dq[heads, start : start + count, :] += back
+            masks[start, key_start] = (key_place <= place) & (key_place >= opening(place, docs))
+        scores = mm_nt(
+            key_rows(kz, group, key_start, key_count), rows_of(q_ref, start, count, group)
+        )
+        grads = mm_nt(
+            key_rows(vz, group, key_start, key_count), rows_of(do_ref, start, count, group)
+        )
+        return scores, grads
+
+    def finish(start, count, key_start, key_count, group, ready):
+        heads = slice(group * GROUPS, (group + 1) * GROUPS)
+        blocks = slice(key_start // span, (key_start + key_count) // span)
+        scores, grads = ready
+        probs = jnp.where(masks[start, key_start], jnp.exp(scores), 0.0)
+        slopes = (probs * grads).astype(BF16)
+        part = (key_count // span, 2, half, LANES)
+        do = rows_of(do_ref, start, count, group)
+        dv[group, blocks] += mm(probs.astype(BF16), do).reshape(part)
+        dk[group, blocks] += mm(slopes, rows_of(q_ref, start, count, group)).reshape(part)
+        back = mm_tn(slopes, key_rows(kz, group, key_start, key_count))
+        back = back.reshape(GROUPS, count, LANES)
+        if key_start == 0:
+            dq[heads, start : start + count, :] = back
+        else:
+            dq[heads, start : start + count, :] += back
+
+    tasks = [
+        (start, count, key_start, key_count, group)
+        for start, count, keys in query_blocks(geometry)
+        for key_start, key_count in tiles_of(keys, KEY_STEP)
+        for group in range(KVH)
+    ]
+    ahead(tasks, products, finish)
 
 
 def pack_heads(ref, rows, tile):
@@ -326,10 +366,10 @@
         sent[f ^ f_bit, g ^ g_bit, spot] = value
 
 
-def pack_kernel(geometry, where, inputs, cotangent, ids, wq, wk, wv, gain1, gain2, *refs):
+def pack_kernel(geometry, inputs, cotangent, ids, wq, wk, wv, gain1, gain2, *refs):
     rows, tokens, _ = geometry
     half = tokens // 2
-    core, member = where[0], where[3]
+    core, member = lax.axis_index("section"), lax.rem(lax.axis_index("seq"), rows)
     outs, w_ref, (counts, sems) = refs[: 2 * rows], refs[2 * rows], refs[2 * rows + 1 :]
     mine = pl.ds(pl.multiple_of(core * half, half), half)
     copies = []
@@ -413,7 +453,9 @@
     outs = refs[6:]
     if layer == 0:
         blocks_ref, q_next, kv_next = outs[:3]
-        outs = outs[3:]
+        outs, parts, away = outs[3:-5], outs[-5:-1], outs[-1]
+        saved = list(zip((q_aug, middle_ref, gate_ref, up_ref), parts))
+        q_aug, middle_ref, gate_ref, up_ref = parts
     else:
         pair_refs, blocks_ref = outs[: geometry[0]], outs[geometry[0]]
         outs = outs[geometry[0] + 1 :]
@@ -428,6 +470,16 @@
         following = Weights(1, core, mine, theirs, {"qkv": wq_v, "gains": lines_next}, sems_next)
     place_keys(core, own, other, kz, vz)
     attend(geometry, core, wagon, docs, q_ref, kz, vz, heads, q_aug)
+    leaving = []
+
+    def leave(target, part, rows=None):
+        if rows is not None:
+            target, part = target.at[rows], part.at[rows]
+        leaving.append(pltpu.make_async_copy(part, target, away.at[len(leaving)]))
+        leaving[-1].start()
+
+    if layer == 0:
+        leave(*saved[0])
     weights.wait("out", "gains", "gate", "up", "down")
     gain_mlp = gain_row(lines, 1)
     if layer == 0:
@@ -448,6 +500,9 @@
         middle_ref[rows, :] = middle
         gate_ref[rows, :] = gate.astype(BF16)
         up_ref[rows, :] = up.astype(BF16)
+        if layer == 0:
+            for target, part in saved[1:]:
+                leave(target, part, rows)
         hidden = (gate * jax.nn.sigmoid(gate) * up).astype(BF16)
         result = (middle + mm_nt(hidden, wd_v[...])).astype(BF16)
         y_ref[rows, :] = result
@@ -464,6 +519,8 @@
                 start,
                 count,
             )
+    for copy in leaving:
+        copy.wait()
     if layer == 1:
         for step, pair in enumerate(pair_refs):
             pair[pl.ds(core, 1)] = earlier[pl.ds(step, 1)]
@@ -797,6 +854,7 @@
     geometry = (rows, tokens, chips)
     flipped = half % LANES == 0
     where = jnp.stack([core, row, place, member, wagon]).astype(jnp.int32)
+    whole = 0 if chips == 1 else slice(None)
     clans = [[b + rows * j for j in range(chips)] for b in range(rows)]
 
     def turn(step):
@@ -812,7 +870,6 @@
         return jnp.swapaxes(array, -1, -2)
 
     pack_ins = [
-        where,
         flip(inputs),
         flip(cotangent),
         group_ids,
@@ -826,7 +883,7 @@
         packed = call(
             functools.partial(pack_kernel, geometry),
             pack_ins,
-            [SMEM] + [ANY] * 2 + [VMEM] * 6,
+            [ANY] * 2 + [VMEM] * 6,
             [shape((D + PACK, half))] * rows + [shape((D, half))] * rows + [shape((D + PACK, QKV))],
             [vmem(rows, PACK, half), sems(3 * rows)],
             0,
@@ -860,7 +917,7 @@
     ]
     w_qkv = [w_qkv, lax.ppermute(w_qkv, "section", SWAP)]
     mine = {"gate": w_gate[0], "up": w_up[0], "down": flip(w_down[0]), "out": w_out[0]}
-    gates = dict(zip(mine, [w_qkv[1], *packets[1:4]]))
+    gates = dict(zip(mine, [*packets[1:4], w_qkv[1]]))
     pairs = {
         name: (value, lax.ppermute(hold(value, gates[name]), "section", SWAP))
         for name, value in mine.items()
@@ -915,6 +972,8 @@
         if layer == 0:
             outs += [heads, shape((own, 2 * KVW))]
             scratch += [vmem(D, QKV), lines_scratch, sems(2)]
+            scratch += [vmem(HQ, own, LANES), vmem(own, D, kind=F32), vmem(own, FF)]
+            scratch += [vmem(own, FF), sems(16)]
         else:
             scratch = [vmem(*sent_blocks.shape)] + scratch
             outs = outs[:-1] + [shape((2,) + sent_blocks.shape[1:])] * rows
@@ -927,6 +986,7 @@
             outs,
             scratch,
             attn_flops + feed_flops,
+            far=(0, 2, 3, 4) if layer == 0 else (),
         )
 
     kv0 = exchange(kv)
@@ -961,6 +1021,7 @@
             [shape((own, D), F32), shape((1, D), F32), heads],
             [weight["gate"], weight["up"], weight["out"], lines_scratch, sems(4)],
             2 * own * D * (D + 2 * FF),
+            light=layer == 1,
             **order,
         )
 
@@ -1041,10 +1102,14 @@
             lax.ppermute(total[spot], "seq", turn(step)) for spot, step in ((2, 1), (1, 2), (3, 3))
         ]
 
-    def halve(total, step):
+    def part_of(total, step):
+        if chips > 1:
+            return (total, total) if step == 1 else (lax.psum(total, "seq"),) * 2
         count = total.shape[0] // 2
-        got = lax.ppermute(total[count:], "seq", turn(step))
-        return got, (total[:count].astype(F32) + got).astype(BF16)
+        return total[:count], lax.ppermute(total[count:], "seq", turn(step))
+
+    def sum_two(low, got):
+        return low if chips > 1 else (low.astype(F32) + got).astype(BF16)
 
     def sum_seq(first, others):
         return sum((part.astype(F32) for part in others), first.astype(F32)).astype(BF16)
@@ -1083,12 +1148,12 @@
         ]
 
     ys = to_rows(pair_blocks)
-    grad1, dgate, dup, kept_m1, sent = hold(feed(1, where, shares, middle1, gate1, up1), ys[2])
+    grad1, dgate, dup, kept_m1, sent = feed(1, where, shares, middle1, gate1, up1)
     grad1 = grad1.reshape(own, D)
     got_m1 = to_core(sent)
 
     dm, gain_grad, do_heads = hold(
-        spread(1, where, grad1, middle1, dgate, dup, att1), ys[1], got_m1
+        spread(1, where, grad1, middle1, dgate, dup, att1), ys[1], ys[2], got_m1
     )
 
     out = sum_cores(hold(kept_m1, dm), got_m1)
@@ -1108,61 +1173,59 @@
     ys.append(to_core(pile))
 
     total = sum_second(kept_m1, got_m1, near_m1, far_m1)
-    parts_m1 = to_seq(total)
+    low_m1, got = part_of(total, 1)
     outs = feed(0, hold(where, total), [dx1], middle0, gate0, up0)
-    dgate, dup, kept_m0, sent = hold(outs, ys[rows], got_a1, parts_m1)
+    dgate, dup, kept_m0, sent = hold(outs, ys[rows], got_a1, got)
     got_m0 = to_core(sent)
 
-    mlp1 = to_all(sum_seq(hold(parts_m1[0], dgate), parts_m1[1:]))
+    low_m1, got = part_of(sum_two(hold(low_m1, dgate), got), 2)
     out = sum_cores(hold(kept_a1, dgate), got_a1)
     near_a1 = to_first(out)
     activations = to_owners([ys])
-    outs = spread(0, hold(where, out, mlp1[0]), dx1, middle0, dgate, dup, att0)
-    dm, gain_grad, do_heads = hold(outs, activations, mlp1, near_a1, got_m0)
+    outs = spread(0, hold(where, out, low_m1), dx1, middle0, dgate, dup, att0)
+    dm, gain_grad, do_heads, low_m1 = hold((*outs, low_m1), activations, near_a1, got_m0, got)
+    piece_m1 = sum_two(low_m1, got)[whole]
 
     out_a1 = sum_first(hold(kept_a1, dm), got_a1, near_a1)
     far_a1 = to_second(out_a1)
     out_m0 = sum_cores(hold(kept_m0, dm), got_m0)
     near_m0 = to_first(out_m0)
     dxs1 = to_rows(hold(blocks1, dm))
-    pile, *outs = attention_back(hold(where, out_a1, out_m0), q0, do_heads, kv0, stack=mlp1)
-    kept_a1, kept_m0, pile, *outs = hold(
-        (kept_a1, kept_m0, pile, *outs), far_a1, near_m0, dxs1
-    )
-    mlp1 = lax.ppermute(pile, "section", [(0, 1)]), pile
+    outs = attention_back(hold(where, out_a1, out_m0), q0, do_heads, kv0)
+    kept_a1, kept_m0, *outs = hold((kept_a1, kept_m0, *outs), far_a1, near_m0, dxs1)
     dq, dkv, dkv_got = trade_keys(*outs)
 
     total_a1 = sum_second(kept_a1, got_a1, near_a1, far_a1)
-    parts_a1 = to_seq(total_a1)
+    low_a1, got = part_of(total_a1, 1)
     out = sum_first(kept_m0, got_m0, near_m0)
     far_m0 = to_second(out)
     outs = input_back(
         0, hold(where, out, total_a1), dm, att0, x_in, dq, dkv, dkv_got, gain_grad, stack=dxs1
     )
-    kept_m0, pile, dx0, *blocks0, kept_a0, sent = hold(
-        (kept_m0, *outs), far_m0, parts_a1, mlp1[0]
+    mlp1 = to_all(hold(piece_m1, out))
+    kept_m0, low_a1, pile, dx0, *blocks0, kept_a0, sent = hold(
+        (kept_m0, low_a1, *outs), far_m0, got, mlp1
     )
 
     got_a0 = to_core(sent)
     total = sum_second(kept_m0, got_m0, near_m0, far_m0)
+    low_m0, got_low = part_of(total, 1)
     out = sum_cores(hold(kept_a0, total), got_a0)
     near_a0 = to_first(out)
-    if chips == 1:
-        got, total = halve(total, 1)
-        kept_a0 = hold(kept_a0, got, near_a0)
-        got, total = halve(total, 2)
-        piece = total[0]
-    else:
-        piece = lax.psum(total, "seq")
+    kept_a0, low_m0 = hold((kept_a0, low_m0), got_low, near_a0)
+    low_m0, got_low = part_of(sum_two(low_m0, got_low), 2)
+    low_a1, got_a1 = part_of(sum_two(hold(low_a1, kept_a0), got), 2)
     out = sum_first(kept_a0, got_a0, near_a0)
     far_a0 = to_second(out)
-    mlp0 = to_all(piece)
-    total = sum_second(hold(kept_a0, piece), got_a0, near_a0, far_a0)
+    total = sum_second(hold(kept_a0, got_low), got_a0, near_a0, far_a0)
     parts_a0 = to_seq(total)
-    blocks0, pile = hold((blocks0, pile), total)
+    low_m0, low_a1, blocks0, pile, mlp1 = hold((low_m0, low_a1, blocks0, pile, mlp1), total)
+    mlp0 = to_all(sum_two(low_m0, got_low)[whole])
+    mlp1 = jnp.stack(mlp1)
+    mlp1 = lax.ppermute(mlp1, "section", [(0, 1)]), mlp1
     dxs1.append(lax.ppermute(pile, "section", [(0, 1)]))
     dxs0 = to_rows(blocks0)
-    attn = jnp.stack([sum_seq(p[0], p[1:]) for p in (parts_a0, parts_a1)])
+    attn = jnp.stack([sum_seq(parts_a0[0], parts_a0[1:]), sum_two(low_a1, got_a1)[whole]])
     mlp0 = hold(mlp0, attn)
     attn = to_all(attn)
     mlp0 = jnp.stack(mlp0)

time: 258 us -> 253 us (0.981)
  waiting for transfers between devices: 59.2 us -> 62.6 us
  Pallas kernels: 112 us -> 109 us
    ppermute x9 -> x3, starting transfers between devices: 12.5 us -> 3.55 us  [to_seq(): lax.ppermute(total[spot], 'seq', turn(step))]
    ppermute x3 -> x7, starting transfers between devices: 1.85 us -> 8.51 us  [the longest x6 7.18 us: part_of(): return (total[:count], lax.ppermute(total[count:], 'seq', turn(step)))]
    ppermute x9, starting transfers between devices: 10.3 us -> 13.9 us  [to_rows(): lax.ppermute(blocks[step], 'seq', turn(step))]
    pallas_call x15, Pallas kernels: 112 us -> 109 us  [call(): pl.pallas_call(strip, out_shape=tuple(piles) + tuple((pltpu.HBM(a.shape,...]
    ppermute x3 -> x7, waiting for transfers between devices: 14.7 us -> 16.6 us  [the longest x6 16.6 us: part_of(): return (total[:count], lax.ppermute(total[count:], 'seq', turn(step)))]
  transfers between devices with their start and end apart: 62 -> 60, of which waited for: 20 -> 21; matrix products, arithmetic and copies ran while one was open for 3% -> 3% of each run, Pallas kernels for 36% -> 31%
where the time goes in v1:
time: 253 us; the launch traced here: 249 us
  Pallas kernels  109 us (43%)
  starting transfers between devices  64.5 us (25%)
  waiting for transfers between devices  62.6 us (25%)
  other arithmetic  7.49 us (3%)
  local copies, waits for them, and re-layouts  3.56 us (1%)
    pallas_call x15, Pallas kernels, call(): pl.pallas_call(strip, out_shape=tuple(piles) + tuple((pltpu.HBM(a.shape,...  109 us
    ppermute x6, waiting for transfers between devices, part_of(): return (total[:count], lax.ppermute(total[count:], 'seq', turn(step)))  16.6 us
    ppermute x9, starting transfers between devices, to_rows(): lax.ppermute(blocks[step], 'seq', turn(step))  13.9 us
    ppermute x3, waiting for transfers between devices, on_device(): lax.ppermute(packets[step], 'seq', turn(step))  11.8 us
    ppermute x9, waiting for transfers between devices, to_rows(): lax.ppermute(blocks[step], 'seq', turn(step))  11.5 us
    ppermute x9, starting transfers between devices, to_all(): lax.ppermute(piece, 'row', [(r, r ^ step) for r in range(4)])  10.1 us
    ppermute x6, starting transfers between devices, part_of(): return (total[:count], lax.ppermute(total[count:], 'seq', turn(step)))  7.18 us
    ppermute x4, waiting for transfers between devices, to_first(): return lax.ppermute(out, ('section', 'row'), first_pairs)  6.05 us
  transfers between devices with their start and end apart: 60, of which 21 were waited for; matrix products, arithmetic and copies ran while one was open for 3% of the time, Pallas kernels for 31%

profile of v1, /device:TPU:0, one launch (start us, length us, event | category | flops | bytes accessed | tf_op | source)
XLA Modules:
  0.0 248.6 jit_solution(16034522761102417055)
XLA Ops:
  0.7 4.2 %shard_map.203 = (bf16[592,128]{1,0:T(8,128)(2,1)}, bf16[592,128]{1,0:T(8,128)(2,1)}, bf16[592,128]{1,0:T(8,128)(2,1)}, bf16[592,128]{1,0:T(8,128)(2,1)}, bf16[5...) custom-call(bf16[4,576,256]{2,1,0:T(8,128)(2,1)} %bitcast.157, ...), custom_call_target="tpu_custom_call" | custom-call | bytes 5882368 | tf_op jit(solution)/shard_map/pallas_call | solution.py:87
  5.5 2.6 %collective-permute-start = (bf16[592,128]{1,0:T(8,128)(2,1)}, bf16[592,128]{1,0:T(8,128)(2,1)S(1)}, u32[]{:S(2)}, u32[]{:S(2)}) collective-permute-start(bf16[592,128]{1,0:T(8,128)(2,1)} %get-tuple-element.178), channel_id=1, source_target_pairs={{0,1},{1,0},{2,3},{3,2},{4,5},{5,4},{6,7},{7,6},{8,9},{9,8},{10,11... | collective-permute-start | bytes 454664 | tf_op jit(solution)/shard_map/ppermute | solution.py:916
  8.1 2.6 %collective-permute-start.1 = (bf16[592,128]{1,0:T(8,128)(2,1)}, bf16[592,128]{1,0:T(8,128)(2,1)S(1)}, u32[]{:S(2)}, u32[]{:S(2)}) collective-permute-start(bf16[592,128]{1,0:T(8,128)(2,1)} %get-tuple-element.179), channel_id=1, source_target_pairs={{0,2},{1,3},{2,0},{3,1},{4,6},{5,7},{6,4},{7,5},{8,10},{9,11},{10,... | collective-permute-start | bytes 454664 | tf_op jit(solution)/shard_map/ppermute | solution.py:916
  10.7 5.0 %collective-permute-done.refs_2_ = bf16[592,128]{1,0:T(8,128)(2,1)S(1)} collective-permute-done((bf16[592,128]{1,0:T(8,128)(2,1)}, bf16[592,128]{1,0:T(8,128)(2,1)S(1)}, u32[]{:S(2)}, u32[]{:S(2)}) %collective-permute-start) | collective-permute-done | bytes 151584 | tf_op jit(solution)/shard_map/ppermute | solution.py:916
  15.6 6.9 %collective-permute-done.1.refs_3_ = bf16[592,128]{1,0:T(8,128)(2,1)S(1)} collective-permute-done((bf16[592,128]{1,0:T(8,128)(2,1)}, bf16[592,128]{1,0:T(8,128)(2,1)S(1)}, u32[]{:S(2)}, u32[]{:S(2)}) %collective-permute-start.1) | collective-permute-done | bytes 151584 | tf_op jit(solution)/shard_map/ppermute | solution.py:916
  25.0 1.8 fusion.21
  26.9 2.2 pad_maximum_fusion.4
  29.2 3.1 %shard_map.204 = (bf16[4,128,576]{2,1,0:T(8,128)(2,1)S(1)}, bf16[9,512,128]{2,1,0:T(8,128)(2,1)S(1)}, bf16[512,384]{1,0:T(8,128)(2,1)S(1)}) custom-call(s32[5]{0:T(128)S(1)} %stack.89.refs_0_.refs_4_, bf16[592,128]{1,0:T(8,128)(2,1)S(1)} %copy-done.3, bf16[592,128]{1,0:T(8,128)(2,1)S(1)} %collective-permute-done.refs_2_, bf16[592,128]{1,0:T(8,128)(2,1)S(1)} %copy-done.5, ...), custom_call_target="tpu_custom_call" | custom-call | flops 603979776 | bytes 5718036 | tf_op jit(solution)/shard_map/pallas_call | solution.py:87
  32.5 1.8 collective-permute-done.4.refs_5_
  34.3 14.7 %shard_map.205 = (bf16[9,512,128]{2,1,0:T(8,128)(2,1)}, bf16[512,576]{1,0:T(8,128)(2,1)S(1)}, f32[512,576]{1,0:T(8,128)}, bf16[512,1536]{1,0:T(8,128)(2,1)}, bf1...) custom-call(s32[5]{0:T(128)S(1)} %stack.89.refs_0_.refs_4_, ...), custom_call_target="tpu_custom_call" | custom-call | flops 5473566720 | bytes 26296348 | tf_op jit(solution)/shard_map/pallas_call | solution.py:87
  49.1 2.4 collective-permute-start.10
  52.7 1.4 collective-permute-start.12
  54.1 12.1 %shard_map.206 = (bf16[9,512,128]{2,1,0:T(8,128)(2,1)S(1)}, bf16[512,576]{1,0:T(8,128)(2,1)S(1)}, f32[512,576]{1,0:T(8,128)S(1)}, bf16[512,1536]{1,0:T(8,128)(2,...) custom-call(s32[5]{0:T(128)S(1)} %stack.89.refs_0_.refs_4_, ...), custom_call_target="tpu_custom_call" | custom-call | flops 5473566720 | bytes 25903132 | tf_op jit(solution)/shard_map/pallas_call | solution.py:87
  66.3 9.2 %shard_map.207 = (bf16[4,128,576]{2,1,0:T(8,128)(2,1)S(1)}, bf16[512,1536]{1,0:T(8,128)(2,1)S(1)}, bf16[512,1536]{1,0:T(8,128)(2,1)S(1)}, bf16[2,2,4,216,384]{4,...) custom-call(s32[5]{0:T(128)S(1)} %stack.89.refs_0_.refs_4_, bf16[576,128]{1,0:T(8,128)(2,1)S(1)} %copy-done.8, ...), custom_call_target="tpu_custom_call" | custom-call | flops 3623878656 | bytes 19922964 | tf_op jit(solution)/shard_map/pallas_call | solution.py:87
  75.8 2.1 collective-permute-start.13
  78.9 8.5 %shard_map.208 = (f32[512,576]{1,0:T(8,128)S(1)}, f32[1,576]{1,0:T(1,128)S(1)}, bf16[9,512,128]{2,1,0:T(8,128)(2,1)S(1)}) custom-call(s32[5]{0:T(128)S(1)} %stack.89.refs_0_.refs_4_, bf16[512,576]{1,0:T(8,128)(2,1)S(1)} %bitcast.144, f32[512,576]{1,0:T(8,128)S(1)} %get-tuple-element.210.refs_5_.refs_2_, bf16[512,1536]{1,0:T(8,128)(2,1)S(1)} %get-tuple-element.216.refs_3_, ...), custom_call_target="tpu_custom_call" | custom-call | tf_op jit(solution)/shard_map/pallas_call | solution.py:87
  87.4 4.2 %collective-permute-done.13.refs_1_.refs_2_ = bf16[2,576,128]{2,1,0:T(8,128)(2,1)S(1)} collective-permute-done((bf16[2,576,128]{2,1,0:T(8,128)(2,1)S(1)}, bf16[2,576,128]{2,1,0:T(8,128)(2,1)S(1)}, u32[]{:S(2)}, u32[]{:S(2)}) %collective-permute-start.13) | collective-permute-done | bytes 294944 | tf_op jit(solution)/shard_map/ppermute | solution.py:1119
  91.6 2.6 %collective-permute-done.14.refs_2_.refs_3_ = bf16[2,576,128]{2,1,0:T(8,128)(2,1)S(1)} collective-permute-done((bf16[2,576,128]{2,1,0:T(8,128)(2,1)S(1)}, bf16[2,576,128]{2,1,0:T(8,128)(2,1)S(1)}, u32[]{:S(2)}, u32[]{:S(2)}) %collective-permute-start.14) | collective-permute-done | bytes 294944 | tf_op jit(solution)/shard_map/ppermute | solution.py:1119
  94.5 1.6 collective-permute-start.17
  96.1 2.4 collective-permute-start.15
  98.6 10.6 %shard_map.209 = (bf16[512,640]{1,0:T(8,128)(2,1)S(1)}, f32[4,128,384]{2,1,0:T(8,128)S(1)}, bf16[4,128,384]{2,1,0:T(8,128)(2,1)S(1)}) custom-call(s32[5]{0:T(128)S(1)} %stack.89.refs_0_.refs_4_, s32[2]{0:T(128)S(1)} %fusion.37.refs_1_, bf16[9,512,128]{2,1,0:T(8,128)(2,1)S(1)} %get-tuple-element.214.refs_2_, ...), custom_call_target="tpu_custom_call" | custom-call | flops 7247757312 | bytes 5505052 | tf_op jit(solution)/shard_map/pallas_call | solution.py:87
  109.2 3.8 %collective-permute-done.17 = bf16[2,4,216,384]{3,2,1,0:T(8,128)(2,1)S(1)} collective-permute-done((bf16[2,4,216,384]{3,2,1,0:T(8,128)(2,1)S(1)}, bf16[2,4,216,384]{3,2,1,0:T(8,128)(2,1)S(1)}, u32[]{:S(2)}, u32[]{:S(2)}) %collective-permute-start.17) | collective-permute-done | bytes 1327136 | tf_op jit(solution)/shard_map/ppermute | solution.py:1087
  113.2 1.6 collective-permute-start.19
  114.8 1.7 collective-permute-done.18
  116.5 5.0 %shard_map.210 = (bf16[4,2,576,128]{3,2,1,0:T(8,128)(2,1)S(1)}, bf16[512,576]{1,0:T(8,128)(2,1)S(1)}, bf16[576,128]{1,0:T(8,128)(2,1)S(1)}, bf16[576,128]{1,0:T(...) custom-call(bf16[2,576,128]{2,1,0:T(8,128)(2,1)S(1)} %get-tuple-elem, ...), custom_call_target="tpu_custom_call" | custom-call | flops 1547698176 | bytes 10291476 | tf_op jit(solution)/shard_map/pallas_call | solution.py:87
  121.6 2.4 collective-permute-done.19
  126.8 9.2 %shard_map.212 = (bf16[512,1536]{1,0:T(8,128)(2,1)S(1)}, bf16[512,1536]{1,0:T(8,128)(2,1)S(1)}, bf16[2,2,4,216,384]{4,3,2,1,0:T(8,128)(2,1)S(1)}, bf16[2,2,4,216,384]{4,3,2,1,0:T(8,128)(2,1)S(1)}) custom-call(s32[5]{0:T(128)S(1)} %stack.89.refs_0_.refs_4_, bf16[512,576]{1,0:T(8,128)(2,1)S(1)} %get-tuple-element.247.refs_1_, f32[512,576]{1,0:T(8,128)S(1)} %copy-done.2, ...), custom_call_target="tpu_custom_call" | custom-call | flops 3623878656 | bytes 19333140 | tf_op jit(solution)/shard_map/pallas_call | solution.py:87
  136.3 1.6 collective-permute-start.23
  138.7 1.8 shard_map.211
  140.5 8.3 %shard_map.213 = (f32[512,576]{1,0:T(8,128)S(1)}, f32[1,576]{1,0:T(1,128)S(1)}, bf16[9,512,128]{2,1,0:T(8,128)(2,1)S(1)}) custom-call(s32[5]{0:T(128)S(1)} %stack.89.refs_0_.refs_4_, bf16[512,576]{1,0:T(8,128)(2,1)S(1)} %get-tuple-element.247.refs_1_, f32[512,576]{1,0:T(8,128)S(1)} %copy-done.2, bf16[512,1536]{1,0:T(8,128)(2,1)S(1)} %get-tuple-element.257.refs_3_, ...), custom_call_target="tpu_custom_call" | custom-call | flops 2151677952 | bytes 18696468 | tf_op jit(solution)/shard_map/pallas_call | solution.py:87
  150.3 1.3 collective-permute-start.26
  151.6 1.8 collective-permute-start.28
  154.1 1.9 collective-permute-start.30
  156.0 10.5 %shard_map.214 = (bf16[512,640]{1,0:T(8,128)(2,1)S(1)}, f32[4,128,384]{2,1,0:T(8,128)S(1)}, bf16[4,128,384]{2,1,0:T(8,128)(2,1)S(1)}) custom-call(s32[5]{0:T(128)S(1)} %stack.89.refs_0_.refs_4_, s32[2]{0:T(128)S(1)} %fusion.37.refs_1_, bf16[9,512,128]{2,1,0:T(8,128)(2,1)S(1)} %copy-done.11, bf16[9,512,128]{2,1,0:T(8,128)(2,1)S(1)} %get-tuple-element.272.refs_3_, ...), custom_call_target="tpu_custom_call" | custom-call | flops 7247757312 | bytes 5505052 | tf_op jit(solution)/shard_map/pallas_call | solution.py:87
  167.0 2.3 collective-permute-done.27
  169.6 1.6 collective-permute-start.32
  171.2 1.3 collective-permute-start.36
  172.5 1.2 collective-permute-start.35
  174.9 1.5 collective-permute-done.31
  176.5 1.8 collective-permute-start.33
  178.3 6.6 %shard_map.215 = (bf16[4,576,128]{2,1,0:T(8,128)(2,1)S(1)}, bf16[512,576]{1,0:T(8,128)(2,1)}, bf16[576,128]{1,0:T(8,128)(2,1)S(1)}, bf16[576,128]{1,0:T(8,128)(2...) custom-call(bf16[576,128]{1,0:T(8,128)(2,1)S(1)} %get-tuple-element., ...), custom_call_target="tpu_custom_call" | custom-call | flops 1547698176 | bytes 10291476 | tf_op jit(solution)/shard_map/pallas_call | solution.py:87
  184.9 2.5 %collective-permute-done.35 = bf16[216,384]{1,0:T(8,128)(2,1)S(1)} collective-permute-done((bf16[216,384]{1,0:T(8,128)(2,1)S(1)}, bf16[216,384]{1,0:T(8,128)(2,1)S(1)}, u32[]{:S(2)}, u32[]{:S(2)}) %collective-permute-start.35) | collective-permute-done | bytes 165920 | tf_op jit(solution)/shard_map/ppermute | solution.py:1147
  187.8 2.2 collective-permute-done.38
  190.1 1.4 collective-permute-start.39
  191.6 1.6 collective-permute-start.37
  193.2 8.4 %collective-permute-done.37 = bf16[2,216,384]{2,1,0:T(8,128)(2,1)S(1)} collective-permute-done((bf16[2,216,384]{2,1,0:T(8,128)(2,1)S(1)}, bf16[2,216,384]{2,1,0:T(8,128)(2,1)S(1)}, u32[]{:S(2)}, u32[]{:S(2)}) %collective-permute-start.37) | collective-permute-done | bytes 331808 | tf_op jit(solution)/shard_map/ppermute | solution.py:1109
  201.6 2.3 collective-permute-start.40
  205.4 8.2 %collective-permute-done.40 = bf16[1,216,384]{2,1,0:T(8,128)(2,1)S(1)} collective-permute-done((bf16[1,216,384]{2,1,0:T(8,128)(2,1)S(1)}, bf16[1,216,384]{2,1,0:T(8,128)(2,1)S(1)}, u32[]{:S(2)}, u32[]{:S(2)}) %collective-permute-start.40) | collective-permute-done | bytes 165920 | tf_op jit(solution)/shard_map/ppermute | solution.py:1109
  214.4 2.2 collective-permute-start.55
  216.7 2.0 collective-permute-start.47
  218.7 1.5 collective-permute-start.46
  222.0 1.4 collective-permute-done.47
  224.2 1.9 collective-permute-start.43
  226.2 2.0 collective-permute-start.44
  228.6 2.0 collective-permute-start.50
  232.2 3.2 %collective-permute-done.43.refs_3_ = bf16[576,128]{1,0:T(8,128)(2,1)S(1)} collective-permute-done((bf16[576,128]{1,0:T(8,128)(2,1)S(1)}, bf16[576,128]{1,0:T(8,128)(2,1)S(1)}, u32[]{:S(2)}, u32[]{:S(2)}) %collective-permute-start.43) | collective-permute-done | bytes 147488 | tf_op jit(solution)/shard_map/ppermute | solution.py:1119
  235.4 1.3 collective-permute-start.53
  236.8 1.3 collective-permute-start.58
  238.1 1.3 collective-permute-start.57
  239.6 1.3 collective-permute-start.52
  240.9 1.3 collective-permute-start.59
  242.2 1.4 collective-permute-done.52.refs_5_
  243.5 1.9 shard_map.216
  245.4 3.0 %shard_map.217 = (f32[1,144,576]{2,1,0:T(8,128)}, f32[1,144,192]{2,1,0:T(8,128)}, f32[1,144,192]{2,1,0:T(8,128)}, f32[1,144,576]{2,1,0:T(8,128)}, f32[1,144,1536...) custom-call(s32[5]{0:T(128)S(1)} %stack.89.refs_0_.refs_4_, ...), custom_call_target="tpu_custom_call" | custom-call | bytes 7177364 | tf_op jit(solution)/shard_map/pallas_call | solution.py:87
  (138 shorter events, 22.1 us)
Async XLA Ops:
  0.6 23.8 %copy-start.1 = (bf16[1,576,576]{2,1,0:T(8,128)(2,1)S(1)}, bf16[1,576,576]{2,1,0:T(8,128)(2,1)}, u32[]{:S(2)}) copy-start(bf16[1,576,576]{2,1,0:T(8,128)(2,1)} %param.18) | copy-start | bytes 1990660
  4.9 24.3 %copy-start = (bf16[592,1024]{1,0:T(8,128)(2,1)S(1)}, bf16[592,1024]{1,0:T(8,128)(2,1)}, u32[]{:S(2)}) copy-start(bf16[592,1024]{1,0:T(8,128)(2,1)} %get-tuple-element.181.refs_5_.refs_16_.refs_10_.refs_12_.refs_7_) | copy-start | bytes 3637252
  4.9 24.3 %copy-start.3 = (bf16[592,128]{1,0:T(8,128)(2,1)S(1)}, bf16[592,128]{1,0:T(8,128)(2,1)}, u32[]{:S(2)}) copy-start(bf16[592,128]{1,0:T(8,128)(2,1)} %get-tuple-element.177.refs_1_) | copy-start | bytes 454660
  4.9 19.5 %collective-permute-start.3 = (bf16[592,1024]{1,0:T(8,128)(2,1)}, bf16[592,1024]{1,0:T(8,128)(2,1)S(1)}, u32[]{:S(2)}, u32[]{:S(2)}) collective-permute-start(bf16[592,1024]{1,0:T(8,128)(2,1)} %get-tuple-element.181.refs_5_.refs_16_.refs_10_.refs_12_.refs_7_), channel_id=1, source_target_pairs={{0,16},{16,0},{1,17},{17,1},{2,18},{18,2},{3,19},{19,3},{4,20},{20... | collective-permute-start | bytes 3637256 | tf_op jit(solution)/shard_map/ppermute | solution.py:918
  5.5 10.2 %collective-permute-start = (bf16[592,128]{1,0:T(8,128)(2,1)}, bf16[592,128]{1,0:T(8,128)(2,1)S(1)}, u32[]{:S(2)}, u32[]{:S(2)}) collective-permute-start(bf16[592,128]{1,0:T(8,128)(2,1)} %get-tuple-element.178), channel_id=1, source_target_pairs={{0,1},{1,0},{2,3},{3,2},{4,5},{5,4},{6,7},{7,6},{8,9},{9,8},{10,11... | collective-permute-start | bytes 454664 | tf_op jit(solution)/shard_map/ppermute | solution.py:916
  8.1 14.4 %collective-permute-start.1 = (bf16[592,128]{1,0:T(8,128)(2,1)}, bf16[592,128]{1,0:T(8,128)(2,1)S(1)}, u32[]{:S(2)}, u32[]{:S(2)}) collective-permute-start(bf16[592,128]{1,0:T(8,128)(2,1)} %get-tuple-element.179), channel_id=1, source_target_pairs={{0,2},{1,3},{2,0},{3,1},{4,6},{5,7},{6,4},{7,5},{8,10},{9,11},{10,... | collective-permute-start | bytes 454664 | tf_op jit(solution)/shard_map/ppermute | solution.py:916
  10.7 12.5 %collective-permute-start.2 = (bf16[592,128]{1,0:T(8,128)(2,1)}, bf16[592,128]{1,0:T(8,128)(2,1)S(1)}, u32[]{:S(2)}, u32[]{:S(2)}) collective-permute-start(bf16[592,128]{1,0:T(8,128)(2,1)} %get-tuple-element.180), channel_id=1, source_target_pairs={{0,3},{1,2},{2,1},{3,0},{4,7},{5,6},{6,5},{7,4},{8,11},{9,10},{10,... | collective-permute-start | bytes 454664 | tf_op jit(solution)/shard_map/ppermute | solution.py:916
  23.9 10.4 %collective-permute-start.7 = (bf16[576,1536]{1,0:T(8,128)(2,1)}, bf16[576,1536]{1,0:T(8,128)(2,1)}, u32[]{:S(2)}, u32[]{:S(2)}) collective-permute-start(bf16[576,1536]{1,0:T(8,128)(2,1)} %bitcast.18.refs_12_.refs_8_.refs_5_), channel_id=1, source_target_pairs={{0,16},{16,0},{1,17},{17,1},{2,18},{18,2},{3,19},{19,3},{4,20},{20... | collective-permute-start | bytes 5308424 | tf_op jit(solution)/shard_map/ppermute | solution.py:922
  23.9 10.4 %collective-permute-start.6 = (bf16[576,1536]{1,0:T(8,128)(2,1)}, bf16[576,1536]{1,0:T(8,128)(2,1)}, u32[]{:S(2)}, u32[]{:S(2)}) collective-permute-start(bf16[576,1536]{1,0:T(8,128)(2,1)} %bitcast.16.refs_10_.refs_8_), channel_id=1, source_target_pairs={{0,16},{16,0},{1,17},{17,1},{2,18},{18,2},{3,19},{19,3},{4,20},{20... | collective-permute-start | bytes 5308424 | tf_op jit(solution)/shard_map/ppermute | solution.py:922
  24.4 9.9 %collective-permute-start.5 = (bf16[576,1536]{1,0:T(8,128)(2,1)}, bf16[576,1536]{1,0:T(8,128)(2,1)}, u32[]{:S(2)}, u32[]{:S(2)}) collective-permute-start(bf16[576,1536]{1,0:T(8,128)(2,1)} %bitcast.15.refs_8_.refs_6_), channel_id=1, source_target_pairs={{0,16},{16,0},{1,17},{17,1},{2,18},{18,2},{3,19},{19,3},{4,20},{20... | collective-permute-start | bytes 5308424 | tf_op jit(solution)/shard_map/ppermute | solution.py:922
  24.4 9.8 %collective-permute-start.8 = (bf16[576,576]{1,0:T(8,128)(2,1)S(1)}, bf16[576,576]{1,0:T(8,128)(2,1)}, u32[]{:S(2)}, u32[]{:S(2)}) collective-permute-start(bf16[576,576]{1,0:T(8,128)(2,1)S(1)} %bitcast.135), channel_id=1, source_target_pairs={{0,16},{16,0},{1,17},{17,1},{2,18},{18,2},{3,19},{19,3},{4,20},{20... | collective-permute-start | bytes 1990664 | tf_op jit(solution)/shard_map/ppermute | solution.py:922
  32.4 1.9 collective-permute-start.4
  34.3 18.4 %copy-start.12 = (bf16[576,128]{1,0:T(8,128)(2,1)S(1)}, bf16[576,128]{1,0:T(8,128)(2,1)}, u32[]{:S(2)}) copy-start(bf16[576,128]{1,0:T(8,128)(2,1)} %get-tuple-element.205) | copy-start | bytes 442372
  49.0 5.1 %collective-permute-start.9 = (bf16[4,128,384]{2,1,0:T(8,128)(2,1)S(1)}, bf16[4,128,384]{2,1,0:T(8,128)(2,1)S(1)}, u32[]{:S(2)}, u32[]{:S(2)}) collective-permute-start(bf16[4,128,384]{2,1,0:T(8,128)(2,1)S(1)} %bitcast.154), channel_id=1, source_target_pairs={{0,16},{16,0},{1,17},{17,1},{2,18},{18,2},{3,19},{19,3},{4,20},{20... | collective-permute-start | bytes 1179656 | tf_op jit(solution)/shard_map/ppermute | solution.py:954
  49.1 17.1 %collective-permute-start.10 = (bf16[576,128]{1,0:T(8,128)(2,1)S(1)}, bf16[576,128]{1,0:T(8,128)(2,1)S(1)}, u32[]{:S(2)}, u32[]{:S(2)}) collective-permute-start(bf16[576,128]{1,0:T(8,128)(2,1)S(1)} %copy-done.14), channel_id=1, source_target_pairs={{0,1},{1,0},{2,3},{3,2},{4,5},{5,4},{6,7},{7,6},{8,9},{9,8},{10,11... | collective-permute-start | bytes 442376 | tf_op jit(solution)/shard_map/ppermute | solution.py:995
  51.6 14.7 %collective-permute-start.11 = (bf16[576,128]{1,0:T(8,128)(2,1)S(1)}, bf16[576,128]{1,0:T(8,128)(2,1)S(1)}, u32[]{:S(2)}, u32[]{:S(2)}) collective-permute-start(bf16[576,128]{1,0:T(8,128)(2,1)S(1)} %copy-done.13), channel_id=1, source_target_pairs={{0,2},{1,3},{2,0},{3,1},{4,6},{5,7},{6,4},{7,5},{8,10},{9,11},{10,... | collective-permute-start | bytes 442376 | tf_op jit(solution)/shard_map/ppermute | solution.py:995
  52.7 13.6 %collective-permute-start.12 = (bf16[576,128]{1,0:T(8,128)(2,1)S(1)}, bf16[576,128]{1,0:T(8,128)(2,1)S(1)}, u32[]{:S(2)}, u32[]{:S(2)}) collective-permute-start(bf16[576,128]{1,0:T(8,128)(2,1)S(1)} %copy-done.12), channel_id=1, source_target_pairs={{0,3},{1,2},{2,1},{3,0},{4,7},{5,6},{6,5},{7,4},{8,11},{9,10},{10,... | collective-permute-start | bytes 442376 | tf_op jit(solution)/shard_map/ppermute | solution.py:995
  75.5 18.7 %collective-permute-start.16 = (bf16[2,2,4,216,384]{4,3,2,1,0:T(8,128)(2,1)S(1)}, bf16[2,2,4,216,384]{4,3,2,1,0:T(8,128)(2,1)S(1)}, u32[]{:S(2)}, u32[]{:S(2)}) collective-permute-start(bf16[2,2,4,216,384]{4,3,2,1,0:T(8,128)(2,1)S(1)} %get-tuple-element.222), channel_id=1, source_target_pairs={{0,16},{16,0},{1,17},{17,1},{2,18},{18,2},{3,19},{19,3},{4,20},{20... | collective-permute-start | bytes 7962632 | tf_op jit(solution)/shard_map/ppermute | solution.py:1081
  75.8 15.9 %collective-permute-start.13 = (bf16[2,576,128]{2,1,0:T(8,128)(2,1)S(1)}, bf16[2,576,128]{2,1,0:T(8,128)(2,1)S(1)}, u32[]{:S(2)}, u32[]{:S(2)}) collective-permute-start(bf16[2,576,128]{2,1,0:T(8,128)(2,1)S(1)} %get-tuple-element.207), channel_id=1, source_target_pairs={{0,1},{1,0},{2,3},{3,2},{4,5},{5,4},{6,7},{7,6},{8,9},{9,8},{10,11... | collective-permute-start | bytes 884744 | tf_op jit(solution)/shard_map/ppermute | solution.py:1119
  77.8 16.3 %collective-permute-start.14 = (bf16[2,576,128]{2,1,0:T(8,128)(2,1)S(1)}, bf16[2,576,128]{2,1,0:T(8,128)(2,1)S(1)}, u32[]{:S(2)}, u32[]{:S(2)}) collective-permute-start(bf16[2,576,128]{2,1,0:T(8,128)(2,1)S(1)} %get-tuple-element.208), channel_id=1, source_target_pairs={{0,2},{1,3},{2,0},{3,1},{4,6},{5,7},{6,4},{7,5},{8,10},{9,11},{10,... | collective-permute-start | bytes 884744 | tf_op jit(solution)/shard_map/ppermute | solution.py:1119
  94.5 18.4 %collective-permute-start.17 = (bf16[2,4,216,384]{3,2,1,0:T(8,128)(2,1)S(1)}, bf16[2,4,216,384]{3,2,1,0:T(8,128)(2,1)S(1)}, u32[]{:S(2)}, u32[]{:S(2)}) collective-permute-start(bf16[2,4,216,384]{3,2,1,0:T(8,128)(2,1)S(1)} %fusion), channel_id=1, source_target_pairs={{0,4},{4,0},{8,12},{12,8},{16,24},{20,28},{24,16},{28,20},{1,5},{5... | collective-permute-start | bytes 3981320 | tf_op jit(solution)/shard_map/ppermute | solution.py:1087
  96.1 13.1 %collective-permute-start.15 = (bf16[2,576,128]{2,1,0:T(8,128)(2,1)S(1)}, bf16[2,576,128]{2,1,0:T(8,128)(2,1)S(1)}, u32[]{:S(2)}, u32[]{:S(2)}) collective-permute-start(bf16[2,576,128]{2,1,0:T(8,128)(2,1)S(1)} %get-tuple-element.209), channel_id=1, source_target_pairs={{0,3},{1,2},{2,1},{3,0},{4,7},{5,6},{6,5},{7,4},{8,11},{9,10},{10,... | collective-permute-start | bytes 884744 | tf_op jit(solution)/shard_map/ppermute | solution.py:1119
  113.2 10.7 %collective-permute-start.19 = (bf16[4,216,384]{2,1,0:T(8,128)(2,1)S(1)}, bf16[4,216,384]{2,1,0:T(8,128)(2,1)S(1)}, u32[]{:S(2)}, u32[]{:S(2)}) collective-permute-start(bf16[4,216,384]{2,1,0:T(8,128)(2,1)S(1)} %fusion.7), channel_id=1, source_target_pairs={{0,8},{4,12},{8,0},{12,4},{16,20},{20,16},{24,28},{28,24},{1,9},{5... | collective-permute-start | bytes 1990664 | tf_op jit(solution)/shard_map/ppermute | solution.py:1093
  114.8 1.7 collective-permute-start.18
  124.0 12.1 %collective-permute-start.20 = (bf16[4,2,576,128]{3,2,1,0:T(8,128)(2,1)S(1)}, bf16[4,2,576,128]{3,2,1,0:T(8,128)(2,1)S(1)}, u32[]{:S(2)}, u32[]{:S(2)}) collective-permute-start(bf16[4,2,576,128]{3,2,1,0:T(8,128)(2,1)S(1)} %get-tuple-element.243), channel_id=1, source_target_pairs={{0,16},{16,0},{1,17},{17,1},{2,18},{18,2},{3,19},{19,3},{4,20},{20... | collective-permute-start | bytes 3538952 | tf_op jit(solution)/shard_map/ppermute | solution.py:1081
  124.0 12.1 %collective-permute-start.21 = (bf16[2,2,4,80,384]{4,3,2,1,0:T(8,128)(2,1)S(1)}, bf16[2,2,4,80,384]{4,3,2,1,0:T(8,128)(2,1)S(1)}, u32[]{:S(2)}, u32[]{:S(2)}) collective-permute-start(bf16[2,2,4,80,384]{4,3,2,1,0:T(8,128)(2,1)S(1)} %get-tuple-element.255), channel_id=1, source_target_pairs={{0,16},{16,0},{1,17},{17,1},{2,18},{18,2},{3,19},{19,3},{4,20},{20... | collective-permute-start | bytes 2949128 | tf_op jit(solution)/shard_map/ppermute | solution.py:1081
  124.9 11.1 %collective-permute-start.22 = (bf16[2,216,384]{2,1,0:T(8,128)(2,1)S(1)}, bf16[2,216,384]{2,1,0:T(8,128)(2,1)S(1)}, u32[]{:S(2)}, u32[]{:S(2)}) collective-permute-start(bf16[2,216,384]{2,1,0:T(8,128)(2,1)S(1)} %get-tuple-element.346), channel_id=1, source_target_pairs={{0,1},{1,0},{2,3},{3,2},{4,5},{5,4},{6,7},{7,6},{8,9},{9,8},{10,11... | collective-permute-start | bytes 995336 | tf_op jit(solution)/shard_map/ppermute | solution.py:1109
  136.1 12.8 %collective-permute-start.24 = (bf16[2,2,4,216,384]{4,3,2,1,0:T(8,128)(2,1)S(1)}, bf16[2,2,4,216,384]{4,3,2,1,0:T(8,128)(2,1)S(1)}, u32[]{:S(2)}, u32[]{:S(2)}) collective-permute-start(bf16[2,2,4,216,384]{4,3,2,1,0:T(8,128)(2,1)S(1)} %get-tuple-element.266), channel_id=1, source_target_pairs={{0,16},{16,0},{1,17},{17,1},{2,18},{18,2},{3,19},{19,3},{4,20},{20... | collective-permute-start | bytes 7962632 | tf_op jit(solution)/shard_map/ppermute | solution.py:1081
  136.3 12.6 %collective-permute-start.23 = (bf16[2,4,80,384]{3,2,1,0:T(8,128)(2,1)S(1)}, bf16[2,4,80,384]{3,2,1,0:T(8,128)(2,1)S(1)}, u32[]{:S(2)}, u32[]{:S(2)}) collective-permute-start(bf16[2,4,80,384]{3,2,1,0:T(8,128)(2,1)S(1)} %fusion.8), channel_id=1, source_target_pairs={{0,4},{4,0},{8,12},{12,8},{16,24},{20,28},{24,16},{28,20},{1,5},{5... | collective-permute-start | bytes 1474568 | tf_op jit(solution)/shard_map/ppermute | solution.py:1087
  138.0 10.9 %collective-permute-start.25 = (bf16[1,216,384]{2,1,0:T(8,128)(2,1)S(1)}, bf16[1,216,384]{2,1,0:T(8,128)(2,1)S(1)}, u32[]{:S(2)}, u32[]{:S(2)}) collective-permute-start(bf16[1,216,384]{2,1,0:T(8,128)(2,1)S(1)} %get-tuple-element.349), channel_id=1, source_target_pairs={{0,2},{1,3},{2,0},{3,1},{4,6},{5,7},{6,4},{7,5},{8,10},{9,11},{10,... | collective-permute-start | bytes 497672 | tf_op jit(solution)/shard_map/ppermute | solution.py:1109
  149.3 20.0 %collective-permute-start.27 = (bf16[2,4,216,384]{3,2,1,0:T(8,128)(2,1)S(1)}, bf16[2,4,216,384]{3,2,1,0:T(8,128)(2,1)S(1)}, u32[]{:S(2)}, u32[]{:S(2)}) collective-permute-start(bf16[2,4,216,384]{3,2,1,0:T(8,128)(2,1)S(1)} %fusion.1), channel_id=1, source_target_pairs={{0,4},{4,0},{8,12},{12,8},{16,24},{20,28},{24,16},{28,20},{1,5},{5... | collective-permute-start | bytes 3981320 | tf_op jit(solution)/shard_map/ppermute | solution.py:1087
  150.3 16.7 %collective-permute-start.26 = (bf16[4,80,384]{2,1,0:T(8,128)(2,1)S(1)}, bf16[4,80,384]{2,1,0:T(8,128)(2,1)S(1)}, u32[]{:S(2)}, u32[]{:S(2)}) collective-permute-start(bf16[4,80,384]{2,1,0:T(8,128)(2,1)S(1)} %fusion.15), channel_id=1, source_target_pairs={{0,8},{4,12},{8,0},{12,4},{16,20},{20,16},{24,28},{28,24},{1,9},{5... | collective-permute-start | bytes 737288 | tf_op jit(solution)/shard_map/ppermute | solution.py:1093
  151.6 14.9 %collective-permute-start.28 = (bf16[576,128]{1,0:T(8,128)(2,1)S(1)}, bf16[576,128]{1,0:T(8,128)(2,1)S(1)}, u32[]{:S(2)}, u32[]{:S(2)}) collective-permute-start(bf16[576,128]{1,0:T(8,128)(2,1)S(1)} %get-tuple-element.281), channel_id=1, source_target_pairs={{0,1},{1,0},{2,3},{3,2},{4,5},{5,4},{6,7},{7,6},{8,9},{9,8},{10,11... | collective-permute-start | bytes 442376 | tf_op jit(solution)/shard_map/ppermute | solution.py:1119
  153.4 13.6 %collective-permute-start.29 = (bf16[576,128]{1,0:T(8,128)(2,1)S(1)}, bf16[576,128]{1,0:T(8,128)(2,1)S(1)}, u32[]{:S(2)}, u32[]{:S(2)}) collective-permute-start(bf16[576,128]{1,0:T(8,128)(2,1)S(1)} %get-tuple-element.282), channel_id=1, source_target_pairs={{0,2},{1,3},{2,0},{3,1},{4,6},{5,7},{6,4},{7,5},{8,10},{9,11},{10,... | collective-permute-start | bytes 442376 | tf_op jit(solution)/shard_map/ppermute | solution.py:1119
  154.1 13.0 %collective-permute-start.30 = (bf16[576,128]{1,0:T(8,128)(2,1)S(1)}, bf16[576,128]{1,0:T(8,128)(2,1)S(1)}, u32[]{:S(2)}, u32[]{:S(2)}) collective-permute-start(bf16[576,128]{1,0:T(8,128)(2,1)S(1)} %get-tuple-element.283), channel_id=1, source_target_pairs={{0,3},{1,2},{2,1},{3,0},{4,7},{5,6},{6,5},{7,4},{8,11},{9,10},{10,... | collective-permute-start | bytes 442376 | tf_op jit(solution)/shard_map/ppermute | solution.py:1119
  169.6 17.9 %collective-permute-start.32 = (bf16[4,216,384]{2,1,0:T(8,128)(2,1)S(1)}, bf16[4,216,384]{2,1,0:T(8,128)(2,1)S(1)}, u32[]{:S(2)}, u32[]{:S(2)}) collective-permute-start(bf16[4,216,384]{2,1,0:T(8,128)(2,1)S(1)} %fusion.4), channel_id=1, source_target_pairs={{0,8},{4,12},{8,0},{12,4},{16,20},{20,16},{24,28},{28,24},{1,9},{5... | collective-permute-start | bytes 1990664 | tf_op jit(solution)/shard_map/ppermute | solution.py:1093
  171.2 13.7 %collective-permute-start.36 = (bf16[216,384]{1,0:T(8,128)(2,1)S(1)}, bf16[216,384]{1,0:T(8,128)(2,1)S(1)}, u32[]{:S(2)}, u32[]{:S(2)}) collective-permute-start(bf16[216,384]{1,0:T(8,128)(2,1)S(1)} %fusion.16), channel_id=1, source_target_pairs={{0,12},{4,8},{8,4},{12,0},{1,13},{5,9},{9,5},{13,1},{2,14},{6,10},... | collective-permute-start | bytes 497672 | tf_op jit(solution)/shard_map/ppermute | solution.py:1147
  172.5 14.9 %collective-permute-start.35 = (bf16[216,384]{1,0:T(8,128)(2,1)S(1)}, bf16[216,384]{1,0:T(8,128)(2,1)S(1)}, u32[]{:S(2)}, u32[]{:S(2)}) collective-permute-start(bf16[216,384]{1,0:T(8,128)(2,1)S(1)} %fusion.16), channel_id=1, source_target_pairs={{0,8},{4,12},{8,0},{12,4},{1,9},{5,13},{9,1},{13,5},{2,10},{6,14},... | collective-permute-start | bytes 497672 | tf_op jit(solution)/shard_map/ppermute | solution.py:1147
  173.7 13.7 %collective-permute-start.34 = (bf16[216,384]{1,0:T(8,128)(2,1)S(1)}, bf16[216,384]{1,0:T(8,128)(2,1)S(1)}, u32[]{:S(2)}, u32[]{:S(2)}) collective-permute-start(bf16[216,384]{1,0:T(8,128)(2,1)S(1)} %fusion.16), channel_id=1, source_target_pairs={{0,4},{4,0},{8,12},{12,8},{1,5},{5,1},{9,13},{13,9},{2,6},{6,2},{1... | collective-permute-start | bytes 497672 | tf_op jit(solution)/shard_map/ppermute | solution.py:1147
  174.8 1.7 collective-permute-start.31
  176.5 8.4 %collective-permute-start.33 = (bf16[2,80,384]{2,1,0:T(8,128)(2,1)S(1)}, bf16[2,80,384]{2,1,0:T(8,128)(2,1)S(1)}, u32[]{:S(2)}, u32[]{:S(2)}) collective-permute-start(bf16[2,80,384]{2,1,0:T(8,128)(2,1)S(1)} %get-tuple-element.354), channel_id=1, source_target_pairs={{0,1},{1,0},{2,3},{3,2},{4,5},{5,4},{6,7},{7,6},{8,9},{9,8},{10,11... | collective-permute-start | bytes 368648 | tf_op jit(solution)/shard_map/ppermute | solution.py:1109
  187.4 2.6 %collective-permute-start.38 = (bf16[2,2,4,80,384]{4,3,2,1,0:T(8,128)(2,1)S(1)}, bf16[2,2,4,80,384]{4,3,2,1,0:T(8,128)(2,1)S(1)}, u32[]{:S(2)}, u32[]{:S(2)}) collective-permute-start(bf16[2,2,4,80,384]{4,3,2,1,0:T(8,128)(2,1)S(1)} %get-tuple-element.303), channel_id=1, source_target_pairs={{0,16},{16,0},{1,17},{17,1},{2,18},{18,2},{3,19},{19,3},{4,20},{20... | collective-permute-start | bytes 2949128 | tf_op jit(solution)/shard_map/ppermute | solution.py:1081
  190.1 11.4 %collective-permute-start.39 = (bf16[2,4,80,384]{3,2,1,0:T(8,128)(2,1)S(1)}, bf16[2,4,80,384]{3,2,1,0:T(8,128)(2,1)S(1)}, u32[]{:S(2)}, u32[]{:S(2)}) collective-permute-start(bf16[2,4,80,384]{3,2,1,0:T(8,128)(2,1)S(1)} %fusion.9), channel_id=1, source_target_pairs={{0,4},{4,0},{8,12},{12,8},{16,24},{20,28},{24,16},{28,20},{1,5},{5... | collective-permute-start | bytes 1474568 | tf_op jit(solution)/shard_map/ppermute | solution.py:1087
  191.6 9.9 %collective-permute-start.37 = (bf16[2,216,384]{2,1,0:T(8,128)(2,1)S(1)}, bf16[2,216,384]{2,1,0:T(8,128)(2,1)S(1)}, u32[]{:S(2)}, u32[]{:S(2)}) collective-permute-start(bf16[2,216,384]{2,1,0:T(8,128)(2,1)S(1)} %get-tuple-element.344), channel_id=1, source_target_pairs={{0,1},{1,0},{2,3},{3,2},{4,5},{5,4},{6,7},{7,6},{8,9},{9,8},{10,11... | collective-permute-start | bytes 995336 | tf_op jit(solution)/shard_map/ppermute | solution.py:1109
  201.6 12.0 %collective-permute-start.40 = (bf16[1,216,384]{2,1,0:T(8,128)(2,1)S(1)}, bf16[1,216,384]{2,1,0:T(8,128)(2,1)S(1)}, u32[]{:S(2)}, u32[]{:S(2)}) collective-permute-start(bf16[1,216,384]{2,1,0:T(8,128)(2,1)S(1)} %get-tuple-element.347), channel_id=1, source_target_pairs={{0,2},{1,3},{2,0},{3,1},{4,6},{5,7},{6,4},{7,5},{8,10},{9,11},{10,... | collective-permute-start | bytes 497672 | tf_op jit(solution)/shard_map/ppermute | solution.py:1109
  204.0 9.6 %collective-permute-start.41 = (bf16[4,80,384]{2,1,0:T(8,128)(2,1)S(1)}, bf16[4,80,384]{2,1,0:T(8,128)(2,1)S(1)}, u32[]{:S(2)}, u32[]{:S(2)}) collective-permute-start(bf16[4,80,384]{2,1,0:T(8,128)(2,1)S(1)} %fusion.10), channel_id=1, source_target_pairs={{0,8},{4,12},{8,0},{12,4},{16,20},{20,16},{24,28},{28,24},{1,9},{5... | collective-permute-start | bytes 737288 | tf_op jit(solution)/shard_map/ppermute | solution.py:1093
  204.7 14.1 %collective-permute-start.48 = (bf16[1,80,384]{2,1,0:T(8,128)(2,1)S(1)}, bf16[1,80,384]{2,1,0:T(8,128)(2,1)S(1)}, u32[]{:S(2)}, u32[]{:S(2)}) collective-permute-start(bf16[1,80,384]{2,1,0:T(8,128)(2,1)S(1)} %get-tuple-element.358), channel_id=1, source_target_pairs={{0,2},{1,3},{2,0},{3,1},{4,6},{5,7},{6,4},{7,5},{8,10},{9,11},{10,... | collective-permute-start | bytes 184328 | tf_op jit(solution)/shard_map/ppermute | solution.py:1109
  213.8 12.4 %collective-permute-start.56 = (bf16[216,384]{1,0:T(8,128)(2,1)S(1)}, bf16[216,384]{1,0:T(8,128)(2,1)S(1)}, u32[]{:S(2)}, u32[]{:S(2)}) collective-permute-start(bf16[216,384]{1,0:T(8,128)(2,1)S(1)} %fusion.17), channel_id=1, source_target_pairs={{0,12},{4,8},{8,4},{12,0},{1,13},{5,9},{9,5},{13,1},{2,14},{6,10},... | collective-permute-start | bytes 497672 | tf_op jit(solution)/shard_map/ppermute | solution.py:1147
  214.4 13.8 %collective-permute-start.55 = (bf16[216,384]{1,0:T(8,128)(2,1)S(1)}, bf16[216,384]{1,0:T(8,128)(2,1)S(1)}, u32[]{:S(2)}, u32[]{:S(2)}) collective-permute-start(bf16[216,384]{1,0:T(8,128)(2,1)S(1)} %fusion.17), channel_id=1, source_target_pairs={{0,8},{4,12},{8,0},{12,4},{1,9},{5,13},{9,1},{13,5},{2,10},{6,14},... | collective-permute-start | bytes 497672 | tf_op jit(solution)/shard_map/ppermute | solution.py:1147
  216.6 4.6 %collective-permute-start.45 = (bf16[80,384]{1,0:T(8,128)(2,1)S(1)}, bf16[80,384]{1,0:T(8,128)(2,1)S(1)}, u32[]{:S(2)}, u32[]{:S(2)}) collective-permute-start(bf16[80,384]{1,0:T(8,128)(2,1)S(1)} %get-tuple-element.351), channel_id=1, source_target_pairs={{0,1},{1,0},{2,3},{3,2},{4,5},{5,4},{6,7},{7,6},{8,9},{9,8},{10,11... | collective-permute-start | bytes 184328 | tf_op jit(solution)/shard_map/ppermute | solution.py:1102
  216.7 6.8 %collective-permute-start.47 = (bf16[80,384]{1,0:T(8,128)(2,1)S(1)}, bf16[80,384]{1,0:T(8,128)(2,1)S(1)}, u32[]{:S(2)}, u32[]{:S(2)}) collective-permute-start(bf16[80,384]{1,0:T(8,128)(2,1)S(1)} %get-tuple-element.352), channel_id=1, source_target_pairs={{0,3},{1,2},{2,1},{3,0},{4,7},{5,6},{6,5},{7,4},{8,11},{9,10},{10,... | collective-permute-start | bytes 184328 | tf_op jit(solution)/shard_map/ppermute | solution.py:1102
  218.7 5.5 %collective-permute-start.46 = (bf16[80,384]{1,0:T(8,128)(2,1)S(1)}, bf16[80,384]{1,0:T(8,128)(2,1)S(1)}, u32[]{:S(2)}, u32[]{:S(2)}) collective-permute-start(bf16[80,384]{1,0:T(8,128)(2,1)S(1)} %get-tuple-element.353), channel_id=1, source_target_pairs={{0,2},{1,3},{2,0},{3,1},{4,6},{5,7},{6,4},{7,5},{8,10},{9,11},{10,... | collective-permute-start | bytes 184328 | tf_op jit(solution)/shard_map/ppermute | solution.py:1102
  221.3 7.3 %collective-permute-start.54 = (bf16[216,384]{1,0:T(8,128)(2,1)S(1)}, bf16[216,384]{1,0:T(8,128)(2,1)S(1)}, u32[]{:S(2)}, u32[]{:S(2)}) collective-permute-start(bf16[216,384]{1,0:T(8,128)(2,1)S(1)} %fusion.17), channel_id=1, source_target_pairs={{0,4},{4,0},{8,12},{12,8},{1,5},{5,1},{9,13},{13,9},{2,6},{6,2},{1... | collective-permute-start | bytes 497672 | tf_op jit(solution)/shard_map/ppermute | solution.py:1147
  223.5 7.9 %collective-permute-start.42 = (bf16[576,128]{1,0:T(8,128)(2,1)S(1)}, bf16[576,128]{1,0:T(8,128)(2,1)S(1)}, u32[]{:S(2)}, u32[]{:S(2)}) collective-permute-start(bf16[576,128]{1,0:T(8,128)(2,1)S(1)} %get-tuple-element.315), channel_id=1, source_target_pairs={{0,1},{1,0},{2,3},{3,2},{4,5},{5,4},{6,7},{7,6},{8,9},{9,8},{10,11... | collective-permute-start | bytes 442376 | tf_op jit(solution)/shard_map/ppermute | solution.py:1119
  224.2 11.2 %collective-permute-start.43 = (bf16[576,128]{1,0:T(8,128)(2,1)S(1)}, bf16[576,128]{1,0:T(8,128)(2,1)S(1)}, u32[]{:S(2)}, u32[]{:S(2)}) collective-permute-start(bf16[576,128]{1,0:T(8,128)(2,1)S(1)} %get-tuple-element.316), channel_id=1, source_target_pairs={{0,2},{1,3},{2,0},{3,1},{4,6},{5,7},{6,4},{7,5},{8,10},{9,11},{10,... | collective-permute-start | bytes 442376 | tf_op jit(solution)/shard_map/ppermute | solution.py:1119
  226.2 10.6 %collective-permute-start.44 = (bf16[576,128]{1,0:T(8,128)(2,1)S(1)}, bf16[576,128]{1,0:T(8,128)(2,1)S(1)}, u32[]{:S(2)}, u32[]{:S(2)}) collective-permute-start(bf16[576,128]{1,0:T(8,128)(2,1)S(1)} %get-tuple-element.317), channel_id=1, source_target_pairs={{0,3},{1,2},{2,1},{3,0},{4,7},{5,6},{6,5},{7,4},{8,11},{9,10},{10,... | collective-permute-start | bytes 442376 | tf_op jit(solution)/shard_map/ppermute | solution.py:1119
  228.2 9.9 %collective-permute-start.51 = (bf16[2,80,384]{2,1,0:T(8,128)(2,1)S(1)}, bf16[2,80,384]{2,1,0:T(8,128)(2,1)S(1)}, u32[]{:S(2)}, u32[]{:S(2)}) collective-permute-start(bf16[2,80,384]{2,1,0:T(8,128)(2,1)S(1)} %get-tuple-element.357), channel_id=1, source_target_pairs={{0,12},{4,8},{8,4},{12,0},{1,13},{5,9},{9,5},{13,1},{2,14},{6,10},... | collective-permute-start | bytes 368648 | tf_op jit(solution)/shard_map/ppermute | solution.py:1147
  228.6 10.9 %collective-permute-start.50 = (bf16[2,80,384]{2,1,0:T(8,128)(2,1)S(1)}, bf16[2,80,384]{2,1,0:T(8,128)(2,1)S(1)}, u32[]{:S(2)}, u32[]{:S(2)}) collective-permute-start(bf16[2,80,384]{2,1,0:T(8,128)(2,1)S(1)} %get-tuple-element.357), channel_id=1, source_target_pairs={{0,8},{4,12},{8,0},{12,4},{1,9},{5,13},{9,1},{13,5},{2,10},{6,14},... | collective-permute-start | bytes 368648 | tf_op jit(solution)/shard_map/ppermute | solution.py:1147
  231.4 8.0 %collective-permute-start.49 = (bf16[2,80,384]{2,1,0:T(8,128)(2,1)S(1)}, bf16[2,80,384]{2,1,0:T(8,128)(2,1)S(1)}, u32[]{:S(2)}, u32[]{:S(2)}) collective-permute-start(bf16[2,80,384]{2,1,0:T(8,128)(2,1)S(1)} %get-tuple-element.357), channel_id=1, source_target_pairs={{0,4},{4,0},{8,12},{12,8},{1,5},{5,1},{9,13},{13,9},{2,6},{6,2},{1... | collective-permute-start | bytes 368648 | tf_op jit(solution)/shard_map/ppermute | solution.py:1147
  235.4 6.7 %collective-permute-start.53 = (bf16[4,576,128]{2,1,0:T(8,128)(2,1)S(1)}, bf16[4,576,128]{2,1,0:T(8,128)(2,1)S(1)}, u32[]{:S(2)}, u32[]{:S(2)}) collective-permute-start(bf16[4,576,128]{2,1,0:T(8,128)(2,1)S(1)} %get-tuple-element.324), channel_id=1, source_target_pairs={{0,16},{1,17},{2,18},{3,19},{4,20},{5,21},{6,22},{7,23},{8,24},{9,... | collective-permute-start | bytes 1769480 | tf_op jit(solution)/shard_map/ppermute | solution.py:1226
  236.8 8.6 %collective-permute-start.58 = (bf16[4,216,384]{2,1,0:T(8,128)(2,1)S(1)}, bf16[4,216,384]{2,1,0:T(8,128)(2,1)S(1)}, u32[]{:S(2)}, u32[]{:S(2)}) collective-permute-start(bf16[4,216,384]{2,1,0:T(8,128)(2,1)S(1)} %pad_maximum_fusion.1.refs_4_), channel_id=1, source_target_pairs={{0,16},{1,17},{2,18},{3,19},{4,20},{5,21},{6,22},{7,23},{8,24},{9,... | collective-permute-start | bytes 1990664 | tf_op jit(solution)/shard_map/ppermute | solution.py:1225
  238.1 7.3 %collective-permute-start.57 = (bf16[4,216,384]{2,1,0:T(8,128)(2,1)S(1)}, bf16[4,216,384]{2,1,0:T(8,128)(2,1)S(1)}, u32[]{:S(2)}, u32[]{:S(2)}) collective-permute-start(bf16[4,216,384]{2,1,0:T(8,128)(2,1)S(1)} %pad_maximum_fusion.refs_1_), channel_id=1, source_target_pairs={{16,0},{17,1},{18,2},{19,3},{20,4},{21,5},{22,6},{23,7},{24,8},{25... | collective-permute-start | bytes 1990664 | tf_op jit(solution)/shard_map/ppermute | solution.py:1232
  239.6 3.9 %collective-permute-start.52 = (bf16[4,576,128]{2,1,0:T(8,128)(2,1)S(1)}, bf16[4,576,128]{2,1,0:T(8,128)(2,1)S(1)}, u32[]{:S(2)}, u32[]{:S(2)}) collective-permute-start(bf16[4,576,128]{2,1,0:T(8,128)(2,1)S(1)} %pad_maximum_fusion.2), channel_id=1, source_target_pairs={{16,0},{17,1},{18,2},{19,3},{20,4},{21,5},{22,6},{23,7},{24,8},{25... | collective-permute-start | bytes 1769480 | tf_op jit(solution)/shard_map/ppermute | solution.py:1236
  240.9 4.5 %collective-permute-start.59 = (bf16[4,2,80,384]{3,2,1,0:T(8,128)(2,1)S(1)}, bf16[4,2,80,384]{3,2,1,0:T(8,128)(2,1)S(1)}, u32[]{:S(2)}, u32[]{:S(2)}) collective-permute-start(bf16[4,2,80,384]{3,2,1,0:T(8,128)(2,1)S(1)} %pad_maximum_fusion.3.refs_5_), channel_id=1, source_target_pairs={{0,16},{16,0},{1,17},{17,1},{2,18},{18,2},{3,19},{19,3},{4,20},{20... | collective-permute-start | bytes 1474568 | tf_op jit(solution)/shard_map/ppermute | solution.py:1081
  (11 other events, 62.5 us)

commit v2 on v1

--- a/solution.py
+++ b/solution.py
@@ -1204,7 +1204,7 @@
     )
     mlp1 = to_all(hold(piece_m1, out))
     kept_m0, low_a1, pile, dx0, *blocks0, kept_a0, sent = hold(
-        (kept_m0, low_a1, *outs), far_m0, got, mlp1
+        (kept_m0, low_a1, *outs), far_m0, got, mlp1[1]
     )
 
     got_a0 = to_core(sent)
@@ -1217,15 +1217,19 @@
     low_a1, got_a1 = part_of(sum_two(hold(low_a1, kept_a0), got), 2)
     out = sum_first(kept_a0, got_a0, near_a0)
     far_a0 = to_second(out)
-    total = sum_second(hold(kept_a0, got_low), got_a0, near_a0, far_a0)
+    nearest = lax.ppermute(hold(blocks0[1], kept_a0), "seq", turn(1))
+    total = sum_second(hold(kept_a0, got_low, nearest), got_a0, near_a0, far_a0)
     parts_a0 = to_seq(total)
     low_m0, low_a1, blocks0, pile, mlp1 = hold((low_m0, low_a1, blocks0, pile, mlp1), total)
     mlp0 = to_all(sum_two(low_m0, got_low)[whole])
     mlp1 = jnp.stack(mlp1)
     mlp1 = lax.ppermute(mlp1, "section", [(0, 1)]), mlp1
     dxs1.append(lax.ppermute(pile, "section", [(0, 1)]))
-    dxs0 = to_rows(blocks0)
+    dxs0 = [blocks0[0], nearest] + [
+        lax.ppermute(blocks0[step], "seq", turn(step)) for step in range(2, rows)
+    ]
     attn = jnp.stack([sum_seq(parts_a0[0], parts_a0[1:]), sum_two(low_a1, got_a1)[whole]])
+    attn = hold(attn, mlp1[0], dxs1[rows])
     mlp0 = hold(mlp0, attn)
     attn = to_all(attn)
     mlp0 = jnp.stack(mlp0)

time: 253 us -> 250 us (0.988)
  waiting for transfers between devices: 62.6 us -> 52.6 us
  starting transfers between devices: 64.5 us -> 71.3 us
    ppermute x6, waiting for transfers between devices: 16.6 us -> 10.8 us  [part_of(): return (total[:count], lax.ppermute(total[count:], 'seq', turn(step)))]
    ppermute x0 -> x3, waiting for transfers between devices: none -> 5.06 us  [the longest x2 4.06 us: on_device(): lax.ppermute(blocks0[step], 'seq', turn(step))]
    ppermute x0 -> x3, starting transfers between devices: none -> 4.54 us  [the longest x2 2.64 us: on_device(): lax.ppermute(blocks0[step], 'seq', turn(step))]
    ppermute x9 -> x6, waiting for transfers between devices: 11.5 us -> 7.34 us  [to_rows(): lax.ppermute(blocks[step], 'seq', turn(step))]
    ppermute x9 -> x6, starting transfers between devices: 13.9 us -> 10 us  [to_rows(): lax.ppermute(blocks[step], 'seq', turn(step))]
  transfers between devices with their start and end apart: 60 -> 60, of which waited for: 21 -> 18; matrix products, arithmetic and copies ran while one was open for 3% -> 3% of each run, Pallas kernels for 31% -> 32%
where the time goes in v2:
time: 250 us; the launch traced here: 245 us
  Pallas kernels  109 us (44%)
  starting transfers between devices  71.3 us (29%)
  waiting for transfers between devices  52.6 us (21%)
  other arithmetic  7.48 us (3%)
  local copies, waits for them, and re-layouts  3.56 us (1%)
    pallas_call x15, Pallas kernels, call(): pl.pallas_call(strip, out_shape=tuple(piles) + tuple((pltpu.HBM(a.shape,...  109 us
    ppermute x3, waiting for transfers between devices, on_device(): lax.ppermute(packets[step], 'seq', turn(step))  11.8 us
    ppermute x9, starting transfers between devices, to_all(): lax.ppermute(piece, 'row', [(r, r ^ step) for r in range(4)])  11.3 us
    ppermute x6, waiting for transfers between devices, part_of(): return (total[:count], lax.ppermute(total[count:], 'seq', turn(step)))  10.8 us
    ppermute x6, starting transfers between devices, to_rows(): lax.ppermute(blocks[step], 'seq', turn(step))  10 us
    ppermute x6, starting transfers between devices, part_of(): return (total[:count], lax.ppermute(total[count:], 'seq', turn(step)))  7.36 us
    ppermute x6, waiting for transfers between devices, to_rows(): lax.ppermute(blocks[step], 'seq', turn(step))  7.34 us
    ppermute x4, waiting for transfers between devices, to_first(): return lax.ppermute(out, ('section', 'row'), first_pairs)  6.1 us
  transfers between devices with their start and end apart: 60, of which 18 were waited for; matrix products, arithmetic and copies ran while one was open for 3% of the time, Pallas kernels for 32%

profile of v2, /device:TPU:0, one launch (start us, length us, event | category | flops | bytes accessed | tf_op | source)
XLA Modules:
  0.0 245.4 jit_solution(16576820869047204928)
XLA Ops:
  0.7 4.3 %shard_map.203 = (bf16[592,128]{1,0:T(8,128)(2,1)}, bf16[592,128]{1,0:T(8,128)(2,1)}, bf16[592,128]{1,0:T(8,128)(2,1)}, bf16[592,128]{1,0:T(8,128)(2,1)}, bf16[5...) custom-call(bf16[4,576,256]{2,1,0:T(8,128)(2,1)} %bitcast.156, ...), custom_call_target="tpu_custom_call" | custom-call | bytes 5882368 | tf_op jit(solution)/shard_map/pallas_call | solution.py:87
  5.5 2.6 %collective-permute-start = (bf16[592,128]{1,0:T(8,128)(2,1)}, bf16[592,128]{1,0:T(8,128)(2,1)S(1)}, u32[]{:S(2)}, u32[]{:S(2)}) collective-permute-start(bf16[592,128]{1,0:T(8,128)(2,1)} %get-tuple-element.179), channel_id=1, source_target_pairs={{0,1},{1,0},{2,3},{3,2},{4,5},{5,4},{6,7},{7,6},{8,9},{9,8},{10,11... | collective-permute-start | bytes 454664 | tf_op jit(solution)/shard_map/ppermute | solution.py:916
  8.1 2.6 %collective-permute-start.1 = (bf16[592,128]{1,0:T(8,128)(2,1)}, bf16[592,128]{1,0:T(8,128)(2,1)S(1)}, u32[]{:S(2)}, u32[]{:S(2)}) collective-permute-start(bf16[592,128]{1,0:T(8,128)(2,1)} %get-tuple-element.180), channel_id=1, source_target_pairs={{0,2},{1,3},{2,0},{3,1},{4,6},{5,7},{6,4},{7,5},{8,10},{9,11},{10,... | collective-permute-start | bytes 454664 | tf_op jit(solution)/shard_map/ppermute | solution.py:916
  10.7 5.0 %collective-permute-done.refs_2_ = bf16[592,128]{1,0:T(8,128)(2,1)S(1)} collective-permute-done((bf16[592,128]{1,0:T(8,128)(2,1)}, bf16[592,128]{1,0:T(8,128)(2,1)S(1)}, u32[]{:S(2)}, u32[]{:S(2)}) %collective-permute-start) | collective-permute-done | bytes 151584 | tf_op jit(solution)/shard_map/ppermute | solution.py:916
  15.7 6.9 %collective-permute-done.1.refs_3_ = bf16[592,128]{1,0:T(8,128)(2,1)S(1)} collective-permute-done((bf16[592,128]{1,0:T(8,128)(2,1)}, bf16[592,128]{1,0:T(8,128)(2,1)S(1)}, u32[]{:S(2)}, u32[]{:S(2)}) %collective-permute-start.1) | collective-permute-done | bytes 151584 | tf_op jit(solution)/shard_map/ppermute | solution.py:916
  25.0 1.8 fusion.21
  26.9 2.2 pad_maximum_fusion.4
  29.2 3.1 %shard_map.204 = (bf16[4,128,576]{2,1,0:T(8,128)(2,1)S(1)}, bf16[9,512,128]{2,1,0:T(8,128)(2,1)S(1)}, bf16[512,384]{1,0:T(8,128)(2,1)S(1)}) custom-call(s32[5]{0:T(128)S(1)} %stack.89.refs_0_.refs_4_, bf16[592,128]{1,0:T(8,128)(2,1)S(1)} %copy-done.3, bf16[592,128]{1,0:T(8,128)(2,1)S(1)} %collective-permute-done.refs_2_, bf16[592,128]{1,0:T(8,128)(2,1)S(1)} %copy-done.5, ...), custom_call_target="tpu_custom_call" | custom-call | flops 603979776 | bytes 5718036 | tf_op jit(solution)/shard_map/pallas_call | solution.py:87
  32.5 1.8 collective-permute-done.4.refs_5_
  34.3 14.7 %shard_map.205 = (bf16[9,512,128]{2,1,0:T(8,128)(2,1)}, bf16[512,576]{1,0:T(8,128)(2,1)S(1)}, f32[512,576]{1,0:T(8,128)}, bf16[512,1536]{1,0:T(8,128)(2,1)}, bf1...) custom-call(s32[5]{0:T(128)S(1)} %stack.89.refs_0_.refs_4_, ...), custom_call_target="tpu_custom_call" | custom-call | flops 5473566720 | bytes 26296348 | tf_op jit(solution)/shard_map/pallas_call | solution.py:87
  49.1 2.4 collective-permute-start.10
  52.7 1.4 collective-permute-start.12
  54.1 12.1 %shard_map.206 = (bf16[9,512,128]{2,1,0:T(8,128)(2,1)S(1)}, bf16[512,576]{1,0:T(8,128)(2,1)S(1)}, f32[512,576]{1,0:T(8,128)S(1)}, bf16[512,1536]{1,0:T(8,128)(2,...) custom-call(s32[5]{0:T(128)S(1)} %stack.89.refs_0_.refs_4_, ...), custom_call_target="tpu_custom_call" | custom-call | flops 5473566720 | bytes 25903132 | tf_op jit(solution)/shard_map/pallas_call | solution.py:87
  66.3 9.2 %shard_map.207 = (bf16[4,128,576]{2,1,0:T(8,128)(2,1)S(1)}, bf16[512,1536]{1,0:T(8,128)(2,1)S(1)}, bf16[512,1536]{1,0:T(8,128)(2,1)S(1)}, bf16[2,2,4,216,384]{4,...) custom-call(s32[5]{0:T(128)S(1)} %stack.89.refs_0_.refs_4_, bf16[576,128]{1,0:T(8,128)(2,1)S(1)} %copy-done.8, ...), custom_call_target="tpu_custom_call" | custom-call | flops 3623878656 | bytes 19922964 | tf_op jit(solution)/shard_map/pallas_call | solution.py:87
  75.8 2.1 collective-permute-start.13
  78.9 8.5 %shard_map.208 = (f32[512,576]{1,0:T(8,128)S(1)}, f32[1,576]{1,0:T(1,128)S(1)}, bf16[9,512,128]{2,1,0:T(8,128)(2,1)S(1)}) custom-call(s32[5]{0:T(128)S(1)} %stack.89.refs_0_.refs_4_, bf16[512,576]{1,0:T(8,128)(2,1)S(1)} %bitcast.143, f32[512,576]{1,0:T(8,128)S(1)} %get-tuple-element.211.refs_5_.refs_2_, bf16[512,1536]{1,0:T(8,128)(2,1)S(1)} %get-tuple-element.217.refs_3_, ...), custom_call_target="tpu_custom_call" | custom-call | tf_op jit(solution)/shard_map/pallas_call | solution.py:87
  87.4 4.2 %collective-permute-done.13.refs_1_.refs_2_ = bf16[2,576,128]{2,1,0:T(8,128)(2,1)S(1)} collective-permute-done((bf16[2,576,128]{2,1,0:T(8,128)(2,1)S(1)}, bf16[2,576,128]{2,1,0:T(8,128)(2,1)S(1)}, u32[]{:S(2)}, u32[]{:S(2)}) %collective-permute-start.13) | collective-permute-done | bytes 294944 | tf_op jit(solution)/shard_map/ppermute | solution.py:1119
  91.6 2.5 %collective-permute-done.14.refs_2_.refs_3_ = bf16[2,576,128]{2,1,0:T(8,128)(2,1)S(1)} collective-permute-done((bf16[2,576,128]{2,1,0:T(8,128)(2,1)S(1)}, bf16[2,576,128]{2,1,0:T(8,128)(2,1)S(1)}, u32[]{:S(2)}, u32[]{:S(2)}) %collective-permute-start.14) | collective-permute-done | bytes 294944 | tf_op jit(solution)/shard_map/ppermute | solution.py:1119
  94.6 1.6 collective-permute-start.17
  96.1 2.5 %collective-permute-start.15 = (bf16[2,576,128]{2,1,0:T(8,128)(2,1)S(1)}, bf16[2,576,128]{2,1,0:T(8,128)(2,1)S(1)}, u32[]{:S(2)}, u32[]{:S(2)}) collective-permute-start(bf16[2,576,128]{2,1,0:T(8,128)(2,1)S(1)} %get-tuple-element.210), channel_id=1, source_target_pairs={{0,3},{1,2},{2,1},{3,0},{4,7},{5,6},{6,5},{7,4},{8,11},{9,10},{10,... | collective-permute-start | bytes 884744 | tf_op jit(solution)/shard_map/ppermute | solution.py:1119
  98.6 10.6 %shard_map.209 = (bf16[512,640]{1,0:T(8,128)(2,1)S(1)}, f32[4,128,384]{2,1,0:T(8,128)S(1)}, bf16[4,128,384]{2,1,0:T(8,128)(2,1)S(1)}) custom-call(s32[5]{0:T(128)S(1)} %stack.89.refs_0_.refs_4_, s32[2]{0:T(128)S(1)} %fusion.37.refs_1_, bf16[9,512,128]{2,1,0:T(8,128)(2,1)S(1)} %get-tuple-element.215.refs_2_, ...), custom_call_target="tpu_custom_call" | custom-call | flops 7247757312 | bytes 5505052 | tf_op jit(solution)/shard_map/pallas_call | solution.py:87
  109.3 3.7 %collective-permute-done.17 = bf16[2,4,216,384]{3,2,1,0:T(8,128)(2,1)S(1)} collective-permute-done((bf16[2,4,216,384]{3,2,1,0:T(8,128)(2,1)S(1)}, bf16[2,4,216,384]{3,2,1,0:T(8,128)(2,1)S(1)}, u32[]{:S(2)}, u32[]{:S(2)}) %collective-permute-start.17) | collective-permute-done | bytes 1327136 | tf_op jit(solution)/shard_map/ppermute | solution.py:1087
  113.2 1.6 collective-permute-start.19
  114.8 1.7 collective-permute-done.18
  116.5 5.0 %shard_map.210 = (bf16[4,2,576,128]{3,2,1,0:T(8,128)(2,1)S(1)}, bf16[512,576]{1,0:T(8,128)(2,1)S(1)}, bf16[576,128]{1,0:T(8,128)(2,1)S(1)}, bf16[576,128]{1,0:T(...) custom-call(bf16[2,576,128]{2,1,0:T(8,128)(2,1)S(1)} %get-tuple-elem, ...), custom_call_target="tpu_custom_call" | custom-call | flops 1547698176 | bytes 10291476 | tf_op jit(solution)/shard_map/pallas_call | solution.py:87
  121.6 2.4 collective-permute-done.19
  126.8 9.2 %shard_map.212 = (bf16[512,1536]{1,0:T(8,128)(2,1)S(1)}, bf16[512,1536]{1,0:T(8,128)(2,1)S(1)}, bf16[2,2,4,216,384]{4,3,2,1,0:T(8,128)(2,1)S(1)}, bf16[2,2,4,216,384]{4,3,2,1,0:T(8,128)(2,1)S(1)}) custom-call(s32[5]{0:T(128)S(1)} %stack.89.refs_0_.refs_4_, bf16[512,576]{1,0:T(8,128)(2,1)S(1)} %get-tuple-element.248.refs_1_, f32[512,576]{1,0:T(8,128)S(1)} %copy-done.2, ...), custom_call_target="tpu_custom_call" | custom-call | flops 3623878656 | bytes 19333140 | tf_op jit(solution)/shard_map/pallas_call | solution.py:87
  136.3 1.6 collective-permute-start.23
  138.7 1.8 shard_map.211
  140.6 8.3 %shard_map.213 = (f32[512,576]{1,0:T(8,128)S(1)}, f32[1,576]{1,0:T(1,128)S(1)}, bf16[9,512,128]{2,1,0:T(8,128)(2,1)S(1)}) custom-call(s32[5]{0:T(128)S(1)} %stack.89.refs_0_.refs_4_, bf16[512,576]{1,0:T(8,128)(2,1)S(1)} %get-tuple-element.248.refs_1_, f32[512,576]{1,0:T(8,128)S(1)} %copy-done.2, bf16[512,1536]{1,0:T(8,128)(2,1)S(1)} %get-tuple-element.258.refs_3_, ...), custom_call_target="tpu_custom_call" | custom-call | flops 2151677952 | bytes 18696468 | tf_op jit(solution)/shard_map/pallas_call | solution.py:87
  150.3 1.3 collective-permute-start.26
  151.6 1.8 collective-permute-start.28
  154.1 1.9 collective-permute-start.30
  156.0 10.5 %shard_map.214 = (bf16[512,640]{1,0:T(8,128)(2,1)S(1)}, f32[4,128,384]{2,1,0:T(8,128)S(1)}, bf16[4,128,384]{2,1,0:T(8,128)(2,1)S(1)}) custom-call(s32[5]{0:T(128)S(1)} %stack.89.refs_0_.refs_4_, s32[2]{0:T(128)S(1)} %fusion.37.refs_1_, bf16[9,512,128]{2,1,0:T(8,128)(2,1)S(1)} %copy-done.11, bf16[9,512,128]{2,1,0:T(8,128)(2,1)S(1)} %get-tuple-element.273.refs_3_, ...), custom_call_target="tpu_custom_call" | custom-call | flops 7247757312 | bytes 5505052 | tf_op jit(solution)/shard_map/pallas_call | solution.py:87
  167.1 2.3 collective-permute-done.27
  169.6 1.6 collective-permute-start.32
  172.5 1.9 collective-permute-start.33
  174.4 6.6 %shard_map.215 = (bf16[4,576,128]{2,1,0:T(8,128)(2,1)S(1)}, bf16[512,576]{1,0:T(8,128)(2,1)}, bf16[576,128]{1,0:T(8,128)(2,1)S(1)}, bf16[576,128]{1,0:T(8,128)(2...) custom-call(bf16[576,128]{1,0:T(8,128)(2,1)S(1)} %get-tuple-element., ...), custom_call_target="tpu_custom_call" | custom-call | flops 1547698176 | bytes 10291476 | tf_op jit(solution)/shard_map/pallas_call | solution.py:87
  181.0 1.4 collective-permute-start.36
  182.8 1.9 collective-permute-done.36
  184.8 1.6 collective-permute-start.37
  186.4 1.8 collective-permute-start.35
  188.8 1.5 collective-permute-start.38
  190.3 5.1 %collective-permute-done.35 = bf16[2,216,384]{2,1,0:T(8,128)(2,1)S(1)} collective-permute-done((bf16[2,216,384]{2,1,0:T(8,128)(2,1)S(1)}, bf16[2,216,384]{2,1,0:T(8,128)(2,1)S(1)}, u32[]{:S(2)}, u32[]{:S(2)}) %collective-permute-start.35) | collective-permute-done | bytes 331808 | tf_op jit(solution)/shard_map/ppermute | solution.py:1109
  195.6 1.9 collective-permute-start.41
  198.2 1.5 collective-permute-start.42
  200.8 2.3 collective-permute-start.48
  203.1 5.7 %collective-permute-done.40 = bf16[1,216,384]{2,1,0:T(8,128)(2,1)S(1)} collective-permute-done((bf16[1,216,384]{2,1,0:T(8,128)(2,1)S(1)}, bf16[1,216,384]{2,1,0:T(8,128)(2,1)S(1)}, u32[]{:S(2)}, u32[]{:S(2)}) %collective-permute-start.40) | collective-permute-done | bytes 165920 | tf_op jit(solution)/shard_map/ppermute | solution.py:1109
  209.0 2.0 collective-permute-start.47
  211.0 3.8 %collective-permute-start.50 = (bf16[4,576,128]{2,1,0:T(8,128)(2,1)S(1)}, bf16[4,576,128]{2,1,0:T(8,128)(2,1)S(1)}, u32[]{:S(2)}, u32[]{:S(2)}) collective-permute-start(bf16[4,576,128]{2,1,0:T(8,128)(2,1)S(1)} %get-tuple-element.324), channel_id=1, source_target_pairs={{0,16},{1,17},{2,18},{3,19},{4,20},{5,21},{6,22},{7,23},{8,24},{9,... | collective-permute-start | bytes 1769480 | tf_op jit(solution)/shard_map/ppermute | solution.py:1227
  214.9 1.3 collective-permute-start.49
  216.3 1.3 collective-permute-start.46
  217.6 2.5 collective-permute-start.57
  220.5 1.6 collective-permute-done.46
  222.1 1.4 collective-permute-start.55
  224.3 1.9 collective-permute-start.44
  226.2 1.7 collective-permute-start.53
  230.2 4.1 %collective-permute-done.43.refs_3_ = bf16[576,128]{1,0:T(8,128)(2,1)S(1)} collective-permute-done((bf16[576,128]{1,0:T(8,128)(2,1)S(1)}, bf16[576,128]{1,0:T(8,128)(2,1)S(1)}, u32[]{:S(2)}, u32[]{:S(2)}) %collective-permute-start.43) | collective-permute-done | bytes 147488 | tf_op jit(solution)/shard_map/ppermute | solution.py:1229
  234.2 1.3 collective-permute-start.58
  235.7 1.3 collective-permute-start.54
  237.0 1.3 collective-permute-start.59
  238.3 2.1 collective-permute-done.59.refs_6_
  240.4 3.0 %shard_map.217 = (f32[1,144,576]{2,1,0:T(8,128)}, f32[1,144,192]{2,1,0:T(8,128)}, f32[1,144,192]{2,1,0:T(8,128)}, f32[1,144,576]{2,1,0:T(8,128)}, f32[1,144,1536...) custom-call(s32[5]{0:T(128)S(1)} %stack.89.refs_0_.refs_4_, ...), custom_call_target="tpu_custom_call" | custom-call | bytes 7177364 | tf_op jit(solution)/shard_map/pallas_call | solution.py:87
  243.3 1.9 shard_map.216
  (138 shorter events, 21.5 us)
Async XLA Ops:
  0.6 23.8 %copy-start.1 = (bf16[1,576,576]{2,1,0:T(8,128)(2,1)S(1)}, bf16[1,576,576]{2,1,0:T(8,128)(2,1)}, u32[]{:S(2)}) copy-start(bf16[1,576,576]{2,1,0:T(8,128)(2,1)} %param.18) | copy-start | bytes 1990660
  4.9 24.3 %copy-start = (bf16[592,1024]{1,0:T(8,128)(2,1)S(1)}, bf16[592,1024]{1,0:T(8,128)(2,1)}, u32[]{:S(2)}) copy-start(bf16[592,1024]{1,0:T(8,128)(2,1)} %get-tuple-element.182.refs_5_.refs_16_.refs_10_.refs_12_.refs_7_) | copy-start | bytes 3637252
  4.9 24.3 %copy-start.3 = (bf16[592,128]{1,0:T(8,128)(2,1)S(1)}, bf16[592,128]{1,0:T(8,128)(2,1)}, u32[]{:S(2)}) copy-start(bf16[592,128]{1,0:T(8,128)(2,1)} %get-tuple-element.178.refs_1_) | copy-start | bytes 454660
  4.9 19.5 %collective-permute-start.3 = (bf16[592,1024]{1,0:T(8,128)(2,1)}, bf16[592,1024]{1,0:T(8,128)(2,1)S(1)}, u32[]{:S(2)}, u32[]{:S(2)}) collective-permute-start(bf16[592,1024]{1,0:T(8,128)(2,1)} %get-tuple-element.182.refs_5_.refs_16_.refs_10_.refs_12_.refs_7_), channel_id=1, source_target_pairs={{0,16},{16,0},{1,17},{17,1},{2,18},{18,2},{3,19},{19,3},{4,20},{20... | collective-permute-start | bytes 3637256 | tf_op jit(solution)/shard_map/ppermute | solution.py:918
  5.5 10.2 %collective-permute-start = (bf16[592,128]{1,0:T(8,128)(2,1)}, bf16[592,128]{1,0:T(8,128)(2,1)S(1)}, u32[]{:S(2)}, u32[]{:S(2)}) collective-permute-start(bf16[592,128]{1,0:T(8,128)(2,1)} %get-tuple-element.179), channel_id=1, source_target_pairs={{0,1},{1,0},{2,3},{3,2},{4,5},{5,4},{6,7},{7,6},{8,9},{9,8},{10,11... | collective-permute-start | bytes 454664 | tf_op jit(solution)/shard_map/ppermute | solution.py:916
  8.1 14.4 %collective-permute-start.1 = (bf16[592,128]{1,0:T(8,128)(2,1)}, bf16[592,128]{1,0:T(8,128)(2,1)S(1)}, u32[]{:S(2)}, u32[]{:S(2)}) collective-permute-start(bf16[592,128]{1,0:T(8,128)(2,1)} %get-tuple-element.180), channel_id=1, source_target_pairs={{0,2},{1,3},{2,0},{3,1},{4,6},{5,7},{6,4},{7,5},{8,10},{9,11},{10,... | collective-permute-start | bytes 454664 | tf_op jit(solution)/shard_map/ppermute | solution.py:916
  10.7 12.5 %collective-permute-start.2 = (bf16[592,128]{1,0:T(8,128)(2,1)}, bf16[592,128]{1,0:T(8,128)(2,1)S(1)}, u32[]{:S(2)}, u32[]{:S(2)}) collective-permute-start(bf16[592,128]{1,0:T(8,128)(2,1)} %get-tuple-element.181), channel_id=1, source_target_pairs={{0,3},{1,2},{2,1},{3,0},{4,7},{5,6},{6,5},{7,4},{8,11},{9,10},{10,... | collective-permute-start | bytes 454664 | tf_op jit(solution)/shard_map/ppermute | solution.py:916
  23.9 10.4 %collective-permute-start.7 = (bf16[576,1536]{1,0:T(8,128)(2,1)}, bf16[576,1536]{1,0:T(8,128)(2,1)}, u32[]{:S(2)}, u32[]{:S(2)}) collective-permute-start(bf16[576,1536]{1,0:T(8,128)(2,1)} %bitcast.18.refs_12_.refs_8_.refs_5_), channel_id=1, source_target_pairs={{0,16},{16,0},{1,17},{17,1},{2,18},{18,2},{3,19},{19,3},{4,20},{20... | collective-permute-start | bytes 5308424 | tf_op jit(solution)/shard_map/ppermute | solution.py:922
  23.9 10.4 %collective-permute-start.6 = (bf16[576,1536]{1,0:T(8,128)(2,1)}, bf16[576,1536]{1,0:T(8,128)(2,1)}, u32[]{:S(2)}, u32[]{:S(2)}) collective-permute-start(bf16[576,1536]{1,0:T(8,128)(2,1)} %bitcast.16.refs_10_.refs_8_), channel_id=1, source_target_pairs={{0,16},{16,0},{1,17},{17,1},{2,18},{18,2},{3,19},{19,3},{4,20},{20... | collective-permute-start | bytes 5308424 | tf_op jit(solution)/shard_map/ppermute | solution.py:922
  24.4 9.9 %collective-permute-start.5 = (bf16[576,1536]{1,0:T(8,128)(2,1)}, bf16[576,1536]{1,0:T(8,128)(2,1)}, u32[]{:S(2)}, u32[]{:S(2)}) collective-permute-start(bf16[576,1536]{1,0:T(8,128)(2,1)} %bitcast.15.refs_8_.refs_6_), channel_id=1, source_target_pairs={{0,16},{16,0},{1,17},{17,1},{2,18},{18,2},{3,19},{19,3},{4,20},{20... | collective-permute-start | bytes 5308424 | tf_op jit(solution)/shard_map/ppermute | solution.py:922
  24.4 9.8 %collective-permute-start.8 = (bf16[576,576]{1,0:T(8,128)(2,1)S(1)}, bf16[576,576]{1,0:T(8,128)(2,1)}, u32[]{:S(2)}, u32[]{:S(2)}) collective-permute-start(bf16[576,576]{1,0:T(8,128)(2,1)S(1)} %bitcast.134), channel_id=1, source_target_pairs={{0,16},{16,0},{1,17},{17,1},{2,18},{18,2},{3,19},{19,3},{4,20},{20... | collective-permute-start | bytes 1990664 | tf_op jit(solution)/shard_map/ppermute | solution.py:922
  32.4 1.9 collective-permute-start.4
  34.3 18.4 %copy-start.12 = (bf16[576,128]{1,0:T(8,128)(2,1)S(1)}, bf16[576,128]{1,0:T(8,128)(2,1)}, u32[]{:S(2)}) copy-start(bf16[576,128]{1,0:T(8,128)(2,1)} %get-tuple-element.206) | copy-start | bytes 442372
  49.1 5.1 %collective-permute-start.9 = (bf16[4,128,384]{2,1,0:T(8,128)(2,1)S(1)}, bf16[4,128,384]{2,1,0:T(8,128)(2,1)S(1)}, u32[]{:S(2)}, u32[]{:S(2)}) collective-permute-start(bf16[4,128,384]{2,1,0:T(8,128)(2,1)S(1)} %bitcast.153), channel_id=1, source_target_pairs={{0,16},{16,0},{1,17},{17,1},{2,18},{18,2},{3,19},{19,3},{4,20},{20... | collective-permute-start | bytes 1179656 | tf_op jit(solution)/shard_map/ppermute | solution.py:954
  49.1 17.1 %collective-permute-start.10 = (bf16[576,128]{1,0:T(8,128)(2,1)S(1)}, bf16[576,128]{1,0:T(8,128)(2,1)S(1)}, u32[]{:S(2)}, u32[]{:S(2)}) collective-permute-start(bf16[576,128]{1,0:T(8,128)(2,1)S(1)} %copy-done.14), channel_id=1, source_target_pairs={{0,1},{1,0},{2,3},{3,2},{4,5},{5,4},{6,7},{7,6},{8,9},{9,8},{10,11... | collective-permute-start | bytes 442376 | tf_op jit(solution)/shard_map/ppermute | solution.py:995
  51.6 14.7 %collective-permute-start.11 = (bf16[576,128]{1,0:T(8,128)(2,1)S(1)}, bf16[576,128]{1,0:T(8,128)(2,1)S(1)}, u32[]{:S(2)}, u32[]{:S(2)}) collective-permute-start(bf16[576,128]{1,0:T(8,128)(2,1)S(1)} %copy-done.13), channel_id=1, source_target_pairs={{0,2},{1,3},{2,0},{3,1},{4,6},{5,7},{6,4},{7,5},{8,10},{9,11},{10,... | collective-permute-start | bytes 442376 | tf_op jit(solution)/shard_map/ppermute | solution.py:995
  52.7 13.6 %collective-permute-start.12 = (bf16[576,128]{1,0:T(8,128)(2,1)S(1)}, bf16[576,128]{1,0:T(8,128)(2,1)S(1)}, u32[]{:S(2)}, u32[]{:S(2)}) collective-permute-start(bf16[576,128]{1,0:T(8,128)(2,1)S(1)} %copy-done.12), channel_id=1, source_target_pairs={{0,3},{1,2},{2,1},{3,0},{4,7},{5,6},{6,5},{7,4},{8,11},{9,10},{10,... | collective-permute-start | bytes 442376 | tf_op jit(solution)/shard_map/ppermute | solution.py:995
  75.5 18.7 %collective-permute-start.16 = (bf16[2,2,4,216,384]{4,3,2,1,0:T(8,128)(2,1)S(1)}, bf16[2,2,4,216,384]{4,3,2,1,0:T(8,128)(2,1)S(1)}, u32[]{:S(2)}, u32[]{:S(2)}) collective-permute-start(bf16[2,2,4,216,384]{4,3,2,1,0:T(8,128)(2,1)S(1)} %get-tuple-element.223), channel_id=1, source_target_pairs={{0,16},{16,0},{1,17},{17,1},{2,18},{18,2},{3,19},{19,3},{4,20},{20... | collective-permute-start | bytes 7962632 | tf_op jit(solution)/shard_map/ppermute | solution.py:1081
  75.8 15.9 %collective-permute-start.13 = (bf16[2,576,128]{2,1,0:T(8,128)(2,1)S(1)}, bf16[2,576,128]{2,1,0:T(8,128)(2,1)S(1)}, u32[]{:S(2)}, u32[]{:S(2)}) collective-permute-start(bf16[2,576,128]{2,1,0:T(8,128)(2,1)S(1)} %get-tuple-element.208), channel_id=1, source_target_pairs={{0,1},{1,0},{2,3},{3,2},{4,5},{5,4},{6,7},{7,6},{8,9},{9,8},{10,11... | collective-permute-start | bytes 884744 | tf_op jit(solution)/shard_map/ppermute | solution.py:1119
  77.8 16.3 %collective-permute-start.14 = (bf16[2,576,128]{2,1,0:T(8,128)(2,1)S(1)}, bf16[2,576,128]{2,1,0:T(8,128)(2,1)S(1)}, u32[]{:S(2)}, u32[]{:S(2)}) collective-permute-start(bf16[2,576,128]{2,1,0:T(8,128)(2,1)S(1)} %get-tuple-element.209), channel_id=1, source_target_pairs={{0,2},{1,3},{2,0},{3,1},{4,6},{5,7},{6,4},{7,5},{8,10},{9,11},{10,... | collective-permute-start | bytes 884744 | tf_op jit(solution)/shard_map/ppermute | solution.py:1119
  94.6 18.4 %collective-permute-start.17 = (bf16[2,4,216,384]{3,2,1,0:T(8,128)(2,1)S(1)}, bf16[2,4,216,384]{3,2,1,0:T(8,128)(2,1)S(1)}, u32[]{:S(2)}, u32[]{:S(2)}) collective-permute-start(bf16[2,4,216,384]{3,2,1,0:T(8,128)(2,1)S(1)} %fusion), channel_id=1, source_target_pairs={{0,4},{4,0},{8,12},{12,8},{16,24},{20,28},{24,16},{28,20},{1,5},{5... | collective-permute-start | bytes 3981320 | tf_op jit(solution)/shard_map/ppermute | solution.py:1087
  96.1 13.1 %collective-permute-start.15 = (bf16[2,576,128]{2,1,0:T(8,128)(2,1)S(1)}, bf16[2,576,128]{2,1,0:T(8,128)(2,1)S(1)}, u32[]{:S(2)}, u32[]{:S(2)}) collective-permute-start(bf16[2,576,128]{2,1,0:T(8,128)(2,1)S(1)} %get-tuple-element.210), channel_id=1, source_target_pairs={{0,3},{1,2},{2,1},{3,0},{4,7},{5,6},{6,5},{7,4},{8,11},{9,10},{10,... | collective-permute-start | bytes 884744 | tf_op jit(solution)/shard_map/ppermute | solution.py:1119
  113.2 10.7 %collective-permute-start.19 = (bf16[4,216,384]{2,1,0:T(8,128)(2,1)S(1)}, bf16[4,216,384]{2,1,0:T(8,128)(2,1)S(1)}, u32[]{:S(2)}, u32[]{:S(2)}) collective-permute-start(bf16[4,216,384]{2,1,0:T(8,128)(2,1)S(1)} %fusion.7), channel_id=1, source_target_pairs={{0,8},{4,12},{8,0},{12,4},{16,20},{20,16},{24,28},{28,24},{1,9},{5... | collective-permute-start | bytes 1990664 | tf_op jit(solution)/shard_map/ppermute | solution.py:1093
  114.8 1.7 collective-permute-start.18
  124.0 12.1 %collective-permute-start.20 = (bf16[4,2,576,128]{3,2,1,0:T(8,128)(2,1)S(1)}, bf16[4,2,576,128]{3,2,1,0:T(8,128)(2,1)S(1)}, u32[]{:S(2)}, u32[]{:S(2)}) collective-permute-start(bf16[4,2,576,128]{3,2,1,0:T(8,128)(2,1)S(1)} %get-tuple-element.244), channel_id=1, source_target_pairs={{0,16},{16,0},{1,17},{17,1},{2,18},{18,2},{3,19},{19,3},{4,20},{20... | collective-permute-start | bytes 3538952 | tf_op jit(solution)/shard_map/ppermute | solution.py:1081
  124.0 12.1 %collective-permute-start.21 = (bf16[2,2,4,80,384]{4,3,2,1,0:T(8,128)(2,1)S(1)}, bf16[2,2,4,80,384]{4,3,2,1,0:T(8,128)(2,1)S(1)}, u32[]{:S(2)}, u32[]{:S(2)}) collective-permute-start(bf16[2,2,4,80,384]{4,3,2,1,0:T(8,128)(2,1)S(1)} %get-tuple-element.256), channel_id=1, source_target_pairs={{0,16},{16,0},{1,17},{17,1},{2,18},{18,2},{3,19},{19,3},{4,20},{20... | collective-permute-start | bytes 2949128 | tf_op jit(solution)/shard_map/ppermute | solution.py:1081
  124.9 11.1 %collective-permute-start.22 = (bf16[2,216,384]{2,1,0:T(8,128)(2,1)S(1)}, bf16[2,216,384]{2,1,0:T(8,128)(2,1)S(1)}, u32[]{:S(2)}, u32[]{:S(2)}) collective-permute-start(bf16[2,216,384]{2,1,0:T(8,128)(2,1)S(1)} %get-tuple-element.348), channel_id=1, source_target_pairs={{0,1},{1,0},{2,3},{3,2},{4,5},{5,4},{6,7},{7,6},{8,9},{9,8},{10,11... | collective-permute-start | bytes 995336 | tf_op jit(solution)/shard_map/ppermute | solution.py:1109
  136.1 12.9 %collective-permute-start.24 = (bf16[2,2,4,216,384]{4,3,2,1,0:T(8,128)(2,1)S(1)}, bf16[2,2,4,216,384]{4,3,2,1,0:T(8,128)(2,1)S(1)}, u32[]{:S(2)}, u32[]{:S(2)}) collective-permute-start(bf16[2,2,4,216,384]{4,3,2,1,0:T(8,128)(2,1)S(1)} %get-tuple-element.267), channel_id=1, source_target_pairs={{0,16},{16,0},{1,17},{17,1},{2,18},{18,2},{3,19},{19,3},{4,20},{20... | collective-permute-start | bytes 7962632 | tf_op jit(solution)/shard_map/ppermute | solution.py:1081
  136.3 12.6 %collective-permute-start.23 = (bf16[2,4,80,384]{3,2,1,0:T(8,128)(2,1)S(1)}, bf16[2,4,80,384]{3,2,1,0:T(8,128)(2,1)S(1)}, u32[]{:S(2)}, u32[]{:S(2)}) collective-permute-start(bf16[2,4,80,384]{3,2,1,0:T(8,128)(2,1)S(1)} %fusion.8), channel_id=1, source_target_pairs={{0,4},{4,0},{8,12},{12,8},{16,24},{20,28},{24,16},{28,20},{1,5},{5... | collective-permute-start | bytes 1474568 | tf_op jit(solution)/shard_map/ppermute | solution.py:1087
  138.0 10.9 %collective-permute-start.25 = (bf16[1,216,384]{2,1,0:T(8,128)(2,1)S(1)}, bf16[1,216,384]{2,1,0:T(8,128)(2,1)S(1)}, u32[]{:S(2)}, u32[]{:S(2)}) collective-permute-start(bf16[1,216,384]{2,1,0:T(8,128)(2,1)S(1)} %get-tuple-element.351), channel_id=1, source_target_pairs={{0,2},{1,3},{2,0},{3,1},{4,6},{5,7},{6,4},{7,5},{8,10},{9,11},{10,... | collective-permute-start | bytes 497672 | tf_op jit(solution)/shard_map/ppermute | solution.py:1109
  149.3 20.0 %collective-permute-start.27 = (bf16[2,4,216,384]{3,2,1,0:T(8,128)(2,1)S(1)}, bf16[2,4,216,384]{3,2,1,0:T(8,128)(2,1)S(1)}, u32[]{:S(2)}, u32[]{:S(2)}) collective-permute-start(bf16[2,4,216,384]{3,2,1,0:T(8,128)(2,1)S(1)} %fusion.1), channel_id=1, source_target_pairs={{0,4},{4,0},{8,12},{12,8},{16,24},{20,28},{24,16},{28,20},{1,5},{5... | collective-permute-start | bytes 3981320 | tf_op jit(solution)/shard_map/ppermute | solution.py:1087
  150.3 16.7 %collective-permute-start.26 = (bf16[4,80,384]{2,1,0:T(8,128)(2,1)S(1)}, bf16[4,80,384]{2,1,0:T(8,128)(2,1)S(1)}, u32[]{:S(2)}, u32[]{:S(2)}) collective-permute-start(bf16[4,80,384]{2,1,0:T(8,128)(2,1)S(1)} %fusion.15), channel_id=1, source_target_pairs={{0,8},{4,12},{8,0},{12,4},{16,20},{20,16},{24,28},{28,24},{1,9},{5... | collective-permute-start | bytes 737288 | tf_op jit(solution)/shard_map/ppermute | solution.py:1093
  151.6 14.9 %collective-permute-start.28 = (bf16[576,128]{1,0:T(8,128)(2,1)S(1)}, bf16[576,128]{1,0:T(8,128)(2,1)S(1)}, u32[]{:S(2)}, u32[]{:S(2)}) collective-permute-start(bf16[576,128]{1,0:T(8,128)(2,1)S(1)} %get-tuple-element.282), channel_id=1, source_target_pairs={{0,1},{1,0},{2,3},{3,2},{4,5},{5,4},{6,7},{7,6},{8,9},{9,8},{10,11... | collective-permute-start | bytes 442376 | tf_op jit(solution)/shard_map/ppermute | solution.py:1119
  153.4 13.6 %collective-permute-start.29 = (bf16[576,128]{1,0:T(8,128)(2,1)S(1)}, bf16[576,128]{1,0:T(8,128)(2,1)S(1)}, u32[]{:S(2)}, u32[]{:S(2)}) collective-permute-start(bf16[576,128]{1,0:T(8,128)(2,1)S(1)} %get-tuple-element.283), channel_id=1, source_target_pairs={{0,2},{1,3},{2,0},{3,1},{4,6},{5,7},{6,4},{7,5},{8,10},{9,11},{10,... | collective-permute-start | bytes 442376 | tf_op jit(solution)/shard_map/ppermute | solution.py:1119
  154.1 13.0 %collective-permute-start.30 = (bf16[576,128]{1,0:T(8,128)(2,1)S(1)}, bf16[576,128]{1,0:T(8,128)(2,1)S(1)}, u32[]{:S(2)}, u32[]{:S(2)}) collective-permute-start(bf16[576,128]{1,0:T(8,128)(2,1)S(1)} %get-tuple-element.284), channel_id=1, source_target_pairs={{0,3},{1,2},{2,1},{3,0},{4,7},{5,6},{6,5},{7,4},{8,11},{9,10},{10,... | collective-permute-start | bytes 442376 | tf_op jit(solution)/shard_map/ppermute | solution.py:1119
  169.6 11.4 %collective-permute-start.32 = (bf16[4,216,384]{2,1,0:T(8,128)(2,1)S(1)}, bf16[4,216,384]{2,1,0:T(8,128)(2,1)S(1)}, u32[]{:S(2)}, u32[]{:S(2)}) collective-permute-start(bf16[4,216,384]{2,1,0:T(8,128)(2,1)S(1)} %fusion.4), channel_id=1, source_target_pairs={{0,8},{4,12},{8,0},{12,4},{16,20},{20,16},{24,28},{28,24},{1,9},{5... | collective-permute-start | bytes 1990664 | tf_op jit(solution)/shard_map/ppermute | solution.py:1093
  171.2 3.2 %collective-permute-start.31 = (bf16[4,128,384]{2,1,0:T(8,128)(2,1)S(1)}, bf16[4,128,384]{2,1,0:T(8,128)(2,1)S(1)}, u32[]{:S(2)}, u32[]{:S(2)}) collective-permute-start(bf16[4,128,384]{2,1,0:T(8,128)(2,1)S(1)} %get-tuple-element.290), channel_id=1, source_target_pairs={{0,16},{16,0},{1,17},{17,1},{2,18},{18,2},{3,19},{19,3},{4,20},{20... | collective-permute-start | bytes 1179656 | tf_op jit(solution)/shard_map/ppermute | solution.py:1046
  171.3 9.7 %collective-permute-start.34 = (bf16[216,384]{1,0:T(8,128)(2,1)S(1)}, bf16[216,384]{1,0:T(8,128)(2,1)S(1)}, u32[]{:S(2)}, u32[]{:S(2)}) collective-permute-start(bf16[216,384]{1,0:T(8,128)(2,1)S(1)} %fusion.16), channel_id=1, source_target_pairs={{0,4},{4,0},{8,12},{12,8},{1,5},{5,1},{9,13},{13,9},{2,6},{6,2},{1... | collective-permute-start | bytes 497672 | tf_op jit(solution)/shard_map/ppermute | solution.py:1147
  172.5 8.5 %collective-permute-start.33 = (bf16[2,80,384]{2,1,0:T(8,128)(2,1)S(1)}, bf16[2,80,384]{2,1,0:T(8,128)(2,1)S(1)}, u32[]{:S(2)}, u32[]{:S(2)}) collective-permute-start(bf16[2,80,384]{2,1,0:T(8,128)(2,1)S(1)} %get-tuple-element.356), channel_id=1, source_target_pairs={{0,1},{1,0},{2,3},{3,2},{4,5},{5,4},{6,7},{7,6},{8,9},{9,8},{10,11... | collective-permute-start | bytes 368648 | tf_op jit(solution)/shard_map/ppermute | solution.py:1109
  181.0 3.6 %collective-permute-start.36 = (bf16[2,2,4,80,384]{4,3,2,1,0:T(8,128)(2,1)S(1)}, bf16[2,2,4,80,384]{4,3,2,1,0:T(8,128)(2,1)S(1)}, u32[]{:S(2)}, u32[]{:S(2)}) collective-permute-start(bf16[2,2,4,80,384]{4,3,2,1,0:T(8,128)(2,1)S(1)} %get-tuple-element.304), channel_id=1, source_target_pairs={{0,16},{16,0},{1,17},{17,1},{2,18},{18,2},{3,19},{19,3},{4,20},{20... | collective-permute-start | bytes 2949128 | tf_op jit(solution)/shard_map/ppermute | solution.py:1081
  184.8 10.7 %collective-permute-start.37 = (bf16[2,4,80,384]{3,2,1,0:T(8,128)(2,1)S(1)}, bf16[2,4,80,384]{3,2,1,0:T(8,128)(2,1)S(1)}, u32[]{:S(2)}, u32[]{:S(2)}) collective-permute-start(bf16[2,4,80,384]{3,2,1,0:T(8,128)(2,1)S(1)} %fusion.9), channel_id=1, source_target_pairs={{0,4},{4,0},{8,12},{12,8},{16,24},{20,28},{24,16},{28,20},{1,5},{5... | collective-permute-start | bytes 1474568 | tf_op jit(solution)/shard_map/ppermute | solution.py:1087
  186.4 9.0 %collective-permute-start.35 = (bf16[2,216,384]{2,1,0:T(8,128)(2,1)S(1)}, bf16[2,216,384]{2,1,0:T(8,128)(2,1)S(1)}, u32[]{:S(2)}, u32[]{:S(2)}) collective-permute-start(bf16[2,216,384]{2,1,0:T(8,128)(2,1)S(1)} %get-tuple-element.346), channel_id=1, source_target_pairs={{0,1},{1,0},{2,3},{3,2},{4,5},{5,4},{6,7},{7,6},{8,9},{9,8},{10,11... | collective-permute-start | bytes 995336 | tf_op jit(solution)/shard_map/ppermute | solution.py:1109
  188.2 20.7 %collective-permute-start.39 = (bf16[216,384]{1,0:T(8,128)(2,1)S(1)}, bf16[216,384]{1,0:T(8,128)(2,1)S(1)}, u32[]{:S(2)}, u32[]{:S(2)}) collective-permute-start(bf16[216,384]{1,0:T(8,128)(2,1)S(1)} %fusion.16), channel_id=1, source_target_pairs={{0,12},{4,8},{8,4},{12,0},{1,13},{5,9},{9,5},{13,1},{2,14},{6,10},... | collective-permute-start | bytes 497672 | tf_op jit(solution)/shard_map/ppermute | solution.py:1147
  188.8 20.1 %collective-permute-start.38 = (bf16[216,384]{1,0:T(8,128)(2,1)S(1)}, bf16[216,384]{1,0:T(8,128)(2,1)S(1)}, u32[]{:S(2)}, u32[]{:S(2)}) collective-permute-start(bf16[216,384]{1,0:T(8,128)(2,1)S(1)} %fusion.16), channel_id=1, source_target_pairs={{0,8},{4,12},{8,0},{12,4},{1,9},{5,13},{9,1},{13,5},{2,10},{6,14},... | collective-permute-start | bytes 497672 | tf_op jit(solution)/shard_map/ppermute | solution.py:1147
  195.6 5.2 %collective-permute-start.41 = (bf16[576,128]{1,0:T(8,128)(2,1)S(1)}, bf16[576,128]{1,0:T(8,128)(2,1)S(1)}, u32[]{:S(2)}, u32[]{:S(2)}) collective-permute-start(bf16[576,128]{1,0:T(8,128)(2,1)S(1)} %get-tuple-element.314), channel_id=1, source_target_pairs={{0,1},{1,0},{2,3},{3,2},{4,5},{5,4},{6,7},{7,6},{8,9},{9,8},{10,11... | collective-permute-start | bytes 442376 | tf_op jit(solution)/shard_map/ppermute | solution.py:1220
  197.5 11.3 %collective-permute-start.40 = (bf16[1,216,384]{2,1,0:T(8,128)(2,1)S(1)}, bf16[1,216,384]{2,1,0:T(8,128)(2,1)S(1)}, u32[]{:S(2)}, u32[]{:S(2)}) collective-permute-start(bf16[1,216,384]{2,1,0:T(8,128)(2,1)S(1)} %get-tuple-element.349), channel_id=1, source_target_pairs={{0,2},{1,3},{2,0},{3,1},{4,6},{5,7},{6,4},{7,5},{8,10},{9,11},{10,... | collective-permute-start | bytes 497672 | tf_op jit(solution)/shard_map/ppermute | solution.py:1109
  198.2 10.5 %collective-permute-start.42 = (bf16[4,80,384]{2,1,0:T(8,128)(2,1)S(1)}, bf16[4,80,384]{2,1,0:T(8,128)(2,1)S(1)}, u32[]{:S(2)}, u32[]{:S(2)}) collective-permute-start(bf16[4,80,384]{2,1,0:T(8,128)(2,1)S(1)} %fusion.10), channel_id=1, source_target_pairs={{0,8},{4,12},{8,0},{12,4},{16,20},{20,16},{24,28},{28,24},{1,9},{5... | collective-permute-start | bytes 737288 | tf_op jit(solution)/shard_map/ppermute | solution.py:1093
  200.8 15.5 %collective-permute-start.48 = (bf16[1,80,384]{2,1,0:T(8,128)(2,1)S(1)}, bf16[1,80,384]{2,1,0:T(8,128)(2,1)S(1)}, u32[]{:S(2)}, u32[]{:S(2)}) collective-permute-start(bf16[1,80,384]{2,1,0:T(8,128)(2,1)S(1)} %get-tuple-element.358), channel_id=1, source_target_pairs={{0,2},{1,3},{2,0},{3,1},{4,6},{5,7},{6,4},{7,5},{8,10},{9,11},{10,... | collective-permute-start | bytes 184328 | tf_op jit(solution)/shard_map/ppermute | solution.py:1109
  209.0 8.6 %collective-permute-start.45 = (bf16[80,384]{1,0:T(8,128)(2,1)S(1)}, bf16[80,384]{1,0:T(8,128)(2,1)S(1)}, u32[]{:S(2)}, u32[]{:S(2)}) collective-permute-start(bf16[80,384]{1,0:T(8,128)(2,1)S(1)} %get-tuple-element.353), channel_id=1, source_target_pairs={{0,1},{1,0},{2,3},{3,2},{4,5},{5,4},{6,7},{7,6},{8,9},{9,8},{10,11... | collective-permute-start | bytes 184328 | tf_op jit(solution)/shard_map/ppermute | solution.py:1102
  209.0 11.0 %collective-permute-start.47 = (bf16[80,384]{1,0:T(8,128)(2,1)S(1)}, bf16[80,384]{1,0:T(8,128)(2,1)S(1)}, u32[]{:S(2)}, u32[]{:S(2)}) collective-permute-start(bf16[80,384]{1,0:T(8,128)(2,1)S(1)} %get-tuple-element.354), channel_id=1, source_target_pairs={{0,3},{1,2},{2,1},{3,0},{4,7},{5,6},{6,5},{7,4},{8,11},{9,10},{10,... | collective-permute-start | bytes 184328 | tf_op jit(solution)/shard_map/ppermute | solution.py:1102
  211.0 12.6 %collective-permute-start.50 = (bf16[4,576,128]{2,1,0:T(8,128)(2,1)S(1)}, bf16[4,576,128]{2,1,0:T(8,128)(2,1)S(1)}, u32[]{:S(2)}, u32[]{:S(2)}) collective-permute-start(bf16[4,576,128]{2,1,0:T(8,128)(2,1)S(1)} %get-tuple-element.324), channel_id=1, source_target_pairs={{0,16},{1,17},{2,18},{3,19},{4,20},{5,21},{6,22},{7,23},{8,24},{9,... | collective-permute-start | bytes 1769480 | tf_op jit(solution)/shard_map/ppermute | solution.py:1227
  214.9 9.4 %collective-permute-start.49 = (bf16[4,216,384]{2,1,0:T(8,128)(2,1)S(1)}, bf16[4,216,384]{2,1,0:T(8,128)(2,1)S(1)}, u32[]{:S(2)}, u32[]{:S(2)}) collective-permute-start(bf16[4,216,384]{2,1,0:T(8,128)(2,1)S(1)} %pad_maximum_fusion.refs_4_), channel_id=1, source_target_pairs={{0,16},{1,17},{2,18},{3,19},{4,20},{5,21},{6,22},{7,23},{8,24},{9,... | collective-permute-start | bytes 1990664 | tf_op jit(solution)/shard_map/ppermute | solution.py:1226
  216.3 5.8 %collective-permute-start.46 = (bf16[80,384]{1,0:T(8,128)(2,1)S(1)}, bf16[80,384]{1,0:T(8,128)(2,1)S(1)}, u32[]{:S(2)}, u32[]{:S(2)}) collective-permute-start(bf16[80,384]{1,0:T(8,128)(2,1)S(1)} %get-tuple-element.355), channel_id=1, source_target_pairs={{0,2},{1,3},{2,0},{3,1},{4,6},{5,7},{6,4},{7,5},{8,10},{9,11},{10,... | collective-permute-start | bytes 184328 | tf_op jit(solution)/shard_map/ppermute | solution.py:1102
  217.6 8.6 %collective-permute-start.57 = (bf16[216,384]{1,0:T(8,128)(2,1)S(1)}, bf16[216,384]{1,0:T(8,128)(2,1)S(1)}, u32[]{:S(2)}, u32[]{:S(2)}) collective-permute-start(bf16[216,384]{1,0:T(8,128)(2,1)S(1)} %fusion.17), channel_id=1, source_target_pairs={{0,12},{4,8},{8,4},{12,0},{1,13},{5,9},{9,5},{13,1},{2,14},{6,10},... | collective-permute-start | bytes 497672 | tf_op jit(solution)/shard_map/ppermute | solution.py:1147
  220.1 7.9 %collective-permute-start.56 = (bf16[216,384]{1,0:T(8,128)(2,1)S(1)}, bf16[216,384]{1,0:T(8,128)(2,1)S(1)}, u32[]{:S(2)}, u32[]{:S(2)}) collective-permute-start(bf16[216,384]{1,0:T(8,128)(2,1)S(1)} %fusion.17), channel_id=1, source_target_pairs={{0,8},{4,12},{8,0},{12,4},{1,9},{5,13},{9,1},{13,5},{2,10},{6,14},... | collective-permute-start | bytes 497672 | tf_op jit(solution)/shard_map/ppermute | solution.py:1147
  222.1 6.9 %collective-permute-start.55 = (bf16[216,384]{1,0:T(8,128)(2,1)S(1)}, bf16[216,384]{1,0:T(8,128)(2,1)S(1)}, u32[]{:S(2)}, u32[]{:S(2)}) collective-permute-start(bf16[216,384]{1,0:T(8,128)(2,1)S(1)} %fusion.17), channel_id=1, source_target_pairs={{0,4},{4,0},{8,12},{12,8},{1,5},{5,1},{9,13},{13,9},{2,6},{6,2},{1... | collective-permute-start | bytes 497672 | tf_op jit(solution)/shard_map/ppermute | solution.py:1147
  223.6 10.7 %collective-permute-start.43 = (bf16[576,128]{1,0:T(8,128)(2,1)S(1)}, bf16[576,128]{1,0:T(8,128)(2,1)S(1)}, u32[]{:S(2)}, u32[]{:S(2)}) collective-permute-start(bf16[576,128]{1,0:T(8,128)(2,1)S(1)} %get-tuple-element.317), channel_id=1, source_target_pairs={{0,2},{1,3},{2,0},{3,1},{4,6},{5,7},{6,4},{7,5},{8,10},{9,11},{10,... | collective-permute-start | bytes 442376 | tf_op jit(solution)/shard_map/ppermute | solution.py:1229
  224.3 11.2 %collective-permute-start.44 = (bf16[576,128]{1,0:T(8,128)(2,1)S(1)}, bf16[576,128]{1,0:T(8,128)(2,1)S(1)}, u32[]{:S(2)}, u32[]{:S(2)}) collective-permute-start(bf16[576,128]{1,0:T(8,128)(2,1)S(1)} %get-tuple-element.318), channel_id=1, source_target_pairs={{0,3},{1,2},{2,1},{3,0},{4,7},{5,6},{6,5},{7,4},{8,11},{9,10},{10,... | collective-permute-start | bytes 442376 | tf_op jit(solution)/shard_map/ppermute | solution.py:1229
  226.2 9.3 %collective-permute-start.53 = (bf16[2,80,384]{2,1,0:T(8,128)(2,1)S(1)}, bf16[2,80,384]{2,1,0:T(8,128)(2,1)S(1)}, u32[]{:S(2)}, u32[]{:S(2)}) collective-permute-start(bf16[2,80,384]{2,1,0:T(8,128)(2,1)S(1)} %pad_maximum_fusion.6), channel_id=1, source_target_pairs={{0,12},{4,8},{8,4},{12,0},{1,13},{5,9},{9,5},{13,1},{2,14},{6,10},... | collective-permute-start | bytes 368648 | tf_op jit(solution)/shard_map/ppermute | solution.py:1147
  228.0 7.6 %collective-permute-start.52 = (bf16[2,80,384]{2,1,0:T(8,128)(2,1)S(1)}, bf16[2,80,384]{2,1,0:T(8,128)(2,1)S(1)}, u32[]{:S(2)}, u32[]{:S(2)}) collective-permute-start(bf16[2,80,384]{2,1,0:T(8,128)(2,1)S(1)} %pad_maximum_fusion.6), channel_id=1, source_target_pairs={{0,8},{4,12},{8,0},{12,4},{1,9},{5,13},{9,1},{13,5},{2,10},{6,14},... | collective-permute-start | bytes 368648 | tf_op jit(solution)/shard_map/ppermute | solution.py:1147
  229.1 6.5 %collective-permute-start.51 = (bf16[2,80,384]{2,1,0:T(8,128)(2,1)S(1)}, bf16[2,80,384]{2,1,0:T(8,128)(2,1)S(1)}, u32[]{:S(2)}, u32[]{:S(2)}) collective-permute-start(bf16[2,80,384]{2,1,0:T(8,128)(2,1)S(1)} %pad_maximum_fusion.6), channel_id=1, source_target_pairs={{0,4},{4,0},{8,12},{12,8},{1,5},{5,1},{9,13},{13,9},{2,6},{6,2},{1... | collective-permute-start | bytes 368648 | tf_op jit(solution)/shard_map/ppermute | solution.py:1147
  234.2 6.1 %collective-permute-start.58 = (bf16[4,216,384]{2,1,0:T(8,128)(2,1)S(1)}, bf16[4,216,384]{2,1,0:T(8,128)(2,1)S(1)}, u32[]{:S(2)}, u32[]{:S(2)}) collective-permute-start(bf16[4,216,384]{2,1,0:T(8,128)(2,1)S(1)} %pad_maximum_fusion.1.refs_1_), channel_id=1, source_target_pairs={{16,0},{17,1},{18,2},{19,3},{20,4},{21,5},{22,6},{23,7},{24,8},{25... | collective-permute-start | bytes 1990664 | tf_op jit(solution)/shard_map/ppermute | solution.py:1236
  235.7 7.6 %collective-permute-start.54 = (bf16[4,576,128]{2,1,0:T(8,128)(2,1)S(1)}, bf16[4,576,128]{2,1,0:T(8,128)(2,1)S(1)}, u32[]{:S(2)}, u32[]{:S(2)}) collective-permute-start(bf16[4,576,128]{2,1,0:T(8,128)(2,1)S(1)} %pad_maximum_fusion.2), channel_id=1, source_target_pairs={{16,0},{17,1},{18,2},{19,3},{20,4},{21,5},{22,6},{23,7},{24,8},{25... | collective-permute-start | bytes 1769480 | tf_op jit(solution)/shard_map/ppermute | solution.py:1240
  237.0 3.3 %collective-permute-start.59 = (bf16[4,2,80,384]{3,2,1,0:T(8,128)(2,1)S(1)}, bf16[4,2,80,384]{3,2,1,0:T(8,128)(2,1)S(1)}, u32[]{:S(2)}, u32[]{:S(2)}) collective-permute-start(bf16[4,2,80,384]{3,2,1,0:T(8,128)(2,1)S(1)} %pad_maximum_fusion.3.refs_5_), channel_id=1, source_target_pairs={{0,16},{16,0},{1,17},{17,1},{2,18},{18,2},{3,19},{19,3},{4,20},{20... | collective-permute-start | bytes 1474568 | tf_op jit(solution)/shard_map/ppermute | solution.py:1081
  (11 other events, 62.5 us)
